TPU v7x, 256 devices: a whole 4x4x8 slice. The times are simulated.
256 devices in a mesh: sector: 64 (over y_lo, z, x), level: 4 (over y_hi, core).
Axes of the slice: x: 4, y: 4 (y_hi: 2, y_lo: 2; y = y_hi * 2 + y_lo), z: 8, core: 2. Of those that a mesh axis runs over, the one named last changes fastest.
Arguments:
- nodes: bfloat16 [4, 1536, 48, 768], P(None, 'sector', 'level'), may hold values from -6 to 6
- level_mask: int32 [48], replicated, may hold values from 0 to 1, as said below
- source_weight: bfloat16 [768, 768], replicated, may hold values from -0.21875 to 0.21875
- target_weight: bfloat16 [768, 768], replicated, may hold values from -0.21875 to 0.21875
- direction_bias: float32 [4, 768], replicated, may hold values from -6 to 6
- node_weight: bfloat16 [768, 768], replicated, may hold values from -0.21875 to 0.21875
- query_key: bfloat16 [2, 768, 768], replicated, may hold values from -1 to 1
- value_weight: bfloat16 [768, 768], replicated, may hold values from -0.21875 to 0.21875
- output_weight: bfloat16 [768, 768], replicated, may hold values from -0.21875 to 0.21875
Outputs:
- mixed: bfloat16 [4, 1536, 48, 768], P(None, 'sector', 'level')
Inputs may be any that keep to these rules, and one draw needn't show every extreme that they name: `level_mask`: exactly 37 entries are 1, the rest 0.
All inputs are finite; a program needn't handle non-finite values.
Results may differ from a plain program's by a relative error of at most 0.0065.
Values may be sent and summed in bfloat16 or wider, within the bound.
No kernel may reach another device: no remote copies, remote signals or barrier semaphores. Data moves between devices by JAX's collectives and lax.ppermute only.
A program may use at most 128 MiB of HBM per device.

v0:
```python
import jax
import jax.numpy as jnp
from jax import lax
from jax.sharding import PartitionSpec as P

HEAD = 64


epsilon = 1e-06
masked_score = -1e30


def padded_2(x, sides, width):
    for axis, dim in sides:
        devices, length = (lax.axis_size(axis), x.shape[dim])
        up = [(i, (i + 1) % devices) for i in range(devices)]
        down = [(j, i) for i, j in up]
        last = lax.slice_in_dim(x, length - width, length, axis=dim)
        initial = lax.slice_in_dim(x, 0, width, axis=dim)
        before = lax.ppermute(last, axis, up)
        after = lax.ppermute(initial, axis, down)
        x = jnp.concatenate([before, x, after], axis=dim)
    return x


def normalize(inputs):
    widened = inputs.astype(jnp.float32)
    return widened * lax.rsqrt(jnp.mean(widened * widened, axis=-1, keepdims=True) + epsilon)


def project(inputs, weight):
    flattened = inputs.reshape(-1, inputs.shape[-1])
    product = jnp.dot(flattened, weight, preferred_element_type=jnp.float32)
    return product.reshape(inputs.shape[:-1] + (weight.shape[1],))


def head_split(inputs):
    return inputs.reshape(inputs.shape[:-1] + (inputs.shape[-1] // HEAD, HEAD))


def per_device(
    nodes,
    level_mask,
    source_weight,
    target_weight,
    direction_bias,
    node_weight,
    query_key,
    value_weight,
    output_weight,
):
    lat_rows = nodes.shape[0]
    level_valid = level_mask > 0
    normed = normalize(nodes).astype(jnp.bfloat16)
    target = project(normed, target_weight)
    source = project(normed, source_weight).astype(jnp.bfloat16)
    padded = padded_2(source, (("sector", 1),), 1)
    east_side = padded[:, 2:]
    west_side = padded[:, :-2]
    zero_row = jnp.zeros((1,) + source.shape[1:], jnp.bfloat16)
    north_side = jnp.concatenate([zero_row, source[:-1]], axis=0)
    south_side = jnp.concatenate([source[1:], zero_row], axis=0)
    row_number = lax.broadcasted_iota(jnp.int32, (lat_rows, 1, 1, 1), 0)
    message_sum = jax.nn.silu(target + east_side + direction_bias[0]) + jax.nn.silu(
        target + west_side + direction_bias[1]
    )
    message_sum = message_sum + jnp.where(
        row_number >= 1, jax.nn.silu(target + north_side + direction_bias[2]), 0.0
    )
    message_sum = message_sum + jnp.where(
        row_number <= lat_rows - 2, jax.nn.silu(target + south_side + direction_bias[3]), 0.0
    )
    summed = message_sum.astype(jnp.bfloat16)
    updated = (nodes.astype(jnp.float32) + project(summed, node_weight)).astype(jnp.bfloat16)
    score_scale = HEAD ** (-0.5)
    normed_updated = normalize(updated).astype(jnp.bfloat16)
    queries = head_split(project(normed_updated, query_key[0]).astype(jnp.bfloat16))
    keys_local = project(normed_updated, query_key[1]).astype(jnp.bfloat16)
    values_local = project(normed_updated, value_weight).astype(jnp.bfloat16)
    start_max = jnp.full(queries.shape[:-1], masked_score, jnp.float32)
    key_piece = head_split(lax.all_gather(keys_local, "level", axis=2, tiled=True))
    value_piece = head_split(lax.all_gather(values_local, "level", axis=2, tiled=True))
    scores = (
        jnp.einsum("ncqhd,nckhd->ncqhk", queries, key_piece, preferred_element_type=jnp.float32)
        * score_scale
    )
    scores = jnp.where(level_valid, scores, masked_score)
    new_max = jnp.maximum(start_max, jnp.max(scores, axis=-1))
    weights = jnp.where(level_valid, jnp.exp(scores - new_max[..., None]), 0.0)
    denominator = jnp.sum(weights, axis=-1)
    addition = jnp.einsum(
        "ncqhk,nckhd->ncqhd",
        weights.astype(jnp.bfloat16),
        value_piece,
        preferred_element_type=jnp.float32,
    )
    numerator = addition
    final_max, denominator, numerator = (new_max, denominator, numerator)
    attended = (numerator / denominator[..., None]).astype(jnp.bfloat16).reshape(updated.shape)
    return (updated.astype(jnp.float32) + project(attended, output_weight)).astype(jnp.bfloat16)


def solution(mesh):
    placed = (P(None, "sector", "level", None), P(), P(), P(), P(), P(), P(), P(), P())
    return jax.shard_map(
        per_device,
        mesh=mesh,
        in_specs=placed,
        out_specs=P(None, "sector", "level", None),
        check_vma=False,
    )
```

profile of v0, /device:TPU:1, one launch (start us, length us, event | category | flops | bytes accessed | tf_op | source)
XLA Modules:
  0.0 217.4 jit_solution(1092270242042196358)
XLA Ops:
  6.5 0.0 copy-start
  6.5 0.0 all-gather.5.cloned.1.call-start
  6.5 2.0 fusion.21
  8.5 3.5 %convolution_convert_fusion.3 = bf16[4,24,12,768]{3,1,2,0:T(8,128)(2,1)S(1)} fusion(bf16[4,24,12,768]{3,1,2,0:T(8,128)(2,1)} %param.9, f32[4,24,12]{1,2,0:T(8,128)S(1)} %add_rsqrt_fusion.1, bf16[768,768]{1,0:T(8,128)(2,1)} %param.11), kind=kOutput, calls=%fused_computation.38 | convolution fusion | flops 1362493440 | bytes 4723200 | tf_op jit(solution)/shard_map/dot_general | solution.py:33
  12.1 0.0 copy-start.2
  12.1 0.2 fusion.55
  12.3 2.1 collective-permute-start.1
  14.4 7.7 %collective-permute-start = (bf16[4,1,12,768]{3,1,2,0:T(2,128)(2,1)S(1)}, bf16[4,1,12,768]{3,1,2,0:T(2,128)(2,1)S(1)}, u32[]{:S(2)}, u32[]{:S(2)}) collective-permute-start(bf16[4,1,12,768]{3,1,2,0:T(2,128)(2,1)S(1)} %get-tuple-element.11), channel_id=1, source_target_pairs={{4,0},{8,4},{12,8},{16,12},{20,16},{24,20},{28,24},{32,28},{36,32}... | collective-permute-start | bytes 221192 | tf_op jit(solution)/shard_map/ppermute | solution.py:21
  22.1 1.7 fusion.54
  23.8 1.7 collective-permute-done.1
  25.6 0.0 collective-permute-done
  25.6 11.7 %fusion.24 = (f32[4,24,12]{1,2,0:T(8,128)S(1)}, bf16[4,24,12,768]{3,1,2,0:T(8,128)(2,1)}) fusion(bf16[768,768]{1,0:T(8,128)(2,1)S(1)} %copy-done, bf16[4,24,12,768]{3,1,2,0:T(8,128)(2,1)S(1)} %convolution_convert_fusion.3, bf16[4,1,12,768]{3,1,2,0:T(2,128)(2,1)S(1)} %collective-permute-done.1, bf16[4,1,12,768]{3,1,2,0:T(2,128)(2,1)S(1)} %collective-permute-done, ...), kind=kOutput, calls=%fused_computation.29 | convolution fusion | flops 2761260032 | bytes 10490888 | tf_op jit(solution)/shard_map/dot_general | solution.py:33
  37.3 0.0 copy-start.3
  37.3 4.8 %convolution_convert_fusion.1 = bf16[4,24,12,768]{3,1,2,0:T(8,128)(2,1)} fusion(bf16[4,24,12,768]{3,1,2,0:T(8,128)(2,1)} %get-tuple-element.14, f32[4,24,12]{1,2,0:T(8,128)S(1)} %add_rsqrt_fusion, bf16[2,768,768]{2,1,0:T(8,128)(2,1)} %param.15), kind=kOutput, calls=%fused_computation.36 | convolution fusion | flops 1362493440 | bytes 4723200 | tf_op jit(solution)/shard_map/dot_general | solution.py:33
  42.1 0.0 all-gather.5.cloned.1.call-update
  42.1 0.0 copy-start.4
  42.1 0.2 all-gather.3.cloned.1.call-start
  42.4 4.4 %convolution_convert_fusion.2 = bf16[4,24,12,768]{3,1,2,0:T(8,128)(2,1)} fusion(bf16[4,24,12,768]{3,1,2,0:T(8,128)(2,1)} %get-tuple-element.14, f32[4,24,12]{1,2,0:T(8,128)S(1)} %add_rsqrt_fusion, bf16[768,768]{1,0:T(8,128)(2,1)S(1)} %copy-done.3), kind=kOutput, calls=%fused_computation.37 | convolution fusion | flops 1362493440 | bytes 4723200 | tf_op jit(solution)/shard_map/dot_general | solution.py:33
  46.8 0.0 all-gather.3.cloned.1.call-update
  46.8 3.5 %convolution_convert_fusion = bf16[4,24,12,768]{3,1,2,0:T(8,128)(2,1)S(1)} fusion(bf16[4,24,12,768]{3,1,2,0:T(8,128)(2,1)} %get-tuple-element.14, f32[4,24,12]{1,2,0:T(8,128)S(1)} %add_rsqrt_fusion, bf16[2,768,768]{2,1,0:T(8,128)(2,1)} %param.15), kind=kOutput, calls=%fused_computation.35 | convolution fusion | flops 1362493440 | bytes 4723200 | tf_op jit(solution)/shard_map/dot_general | solution.py:33
  50.3 4.6 %reshape.72 = bf16[4,24,12,12,64]{4,3,1,2,0:T(8,128)(2,1)} reshape(bf16[4,24,12,768]{3,1,2,0:T(8,128)(2,1)S(1)} %convolution_convert_fusion) | data formatting | bytes 3538944 | tf_op jit(solution)/shard_map/reshape | solution.py:38
  54.9 44.7 %all-gather.5.cloned.1.call-done = bf16[4,24,48,768]{3,1,2,0:T(8,128)(2,1)} async-done(((bf16[4,24,12,768]{3,1,2,0:T(8,128)(2,1)}), bf16[4,24,48,768]{3,1,2,0:T(8,128)(2,1)}) %all-gather.5.cloned.1.call-update) | async-done | bytes 7077904 | tf_op jit(solution)/shard_map/all_gather | solution.py:81
  99.6 21.9 %reshape.81 = bf16[4,24,48,12,64]{4,3,1,2,0:T(8,128)(2,1)} reshape(bf16[4,24,48,768]{3,1,2,0:T(8,128)(2,1)} %all-gather.5.cloned.1.call-done) | data formatting | bytes 14155776 | tf_op jit(solution)/shard_map/reshape | solution.py:38
  121.5 23.2 %bitcast_reduce_fusion = (f32[4,24,12,12]{2,3,1,0:T(8,128)S(1)}, f32[4,24,12,48,12]{3,4,2,1,0:T(8,128)}) fusion(pred[48]{0:T(512)(128)(4,1)S(1)} %broadcast_compare_fusion, bf16[4,24,12,12,64]{4,3,1,2,0:T(8,128)(2,1)} %reshape.72, bf16[4,24,48,12,64]{4,3,1,2,0:T(8,128)(2,1)} %reshape.81), kind=kOutput, calls=%fused_computation.7 | convolution fusion | flops 86911488 | bytes 11556912 | tf_op jit(solution)/shard_map/ncqhd,nckhd->ncqhk/dot_general | solution.py:84
  144.7 0.1 broadcast_maximum_fusion
  144.8 8.2 %fusion.7 = f32[4,24,12,12]{2,3,1,0:T(8,128)S(1)} fusion(f32[4,24,12,48,12]{3,4,2,1,0:T(8,128)} %get-tuple-element.16, f32[4,24,12,12]{2,3,1,0:T(8,128)S(1)} %broadcast_maximum_fusion, pred[48]{0:T(512)(128)(4,1)S(1)} %broadcast_compare_fusion), kind=kLoop, calls=%fused_computation.11 | loop fusion | flops 3303936 | bytes 2764848 | tf_op jit(solution)/shard_map/reduce_sum | solution.py:90
  153.0 5.3 %all-gather.3.cloned.1.call-done = bf16[4,24,48,768]{3,1,2,0:T(8,128)(2,1)} async-done(((bf16[4,24,12,768]{3,1,2,0:T(8,128)(2,1)}), bf16[4,24,48,768]{3,1,2,0:T(8,128)(2,1)}) %all-gather.3.cloned.1.call-update) | async-done | bytes 7077904 | tf_op jit(solution)/shard_map/all_gather | solution.py:82
  158.4 21.9 %reshape.80 = bf16[4,24,48,12,64]{4,3,1,2,0:T(8,128)(2,1)} reshape(bf16[4,24,48,768]{3,1,2,0:T(8,128)(2,1)} %all-gather.3.cloned.1.call-done) | data formatting | bytes 14155776 | tf_op jit(solution)/shard_map/reshape | solution.py:38
  180.3 16.7 %fusion.4 = bf16[4,24,12,12,64]{4,2,3,1,0:T(8,128)(2,1)S(1)} fusion(f32[4,24,12,48,12]{3,4,2,1,0:T(8,128)} %get-tuple-element.16, bf16[4,24,48,12,64]{4,3,1,2,0:T(8,128)(2,1)} %reshape.80, f32[4,24,12,12]{2,3,1,0:T(8,128)S(1)} %fusion.7, f32[4,24,12,12]{2,3,1,0:T(8,128)S(1)} %broadcast_maximum_fusion, pred[48]{0:T(512)(128)(4,1)S(1)} %broadcast_compare_fusion), kind=kOutput, calls=%fused_computation.5 | convolution fusion | flops 90021888 | bytes 11612208 | tf_op jit(solution)/shard_map/ncqhk,nckhd->ncqhd/dot_general | solution.py:91
  196.9 3.4 %copy.18 = bf16[4,24,12,12,64]{4,3,1,2,0:T(8,128)(2,1)} copy(bf16[4,24,12,12,64]{4,2,3,1,0:T(8,128)(2,1)S(1)} %fusion.4) | data formatting | bytes 3538944 | tf_op jit(solution)/shard_map/convert_element_type | solution.py:99
  200.3 5.6 %dot_general.37 = bf16[4,24,12,768]{3,1,2,0:T(8,128)(2,1)S(1)} reshape(bf16[4,24,12,12,64]{4,3,1,2,0:T(8,128)(2,1)} %copy.18) | data formatting | bytes 3538944 | tf_op jit(solution)/shard_map/dot_general | solution.py:33
  205.9 4.6 %fusion.26 = bf16[4,24,12,768]{3,1,2,0:T(8,128)(2,1)} fusion(bf16[4,24,12,768]{3,1,2,0:T(8,128)(2,1)} %get-tuple-element.14, bf16[4,24,12,768]{3,1,2,0:T(8,128)(2,1)S(1)} %dot_general.37, bf16[768,768]{1,0:T(8,128)(2,1)} %param.17), kind=kOutput, calls=%fused_computation.31 | convolution fusion | flops 1361608704 | bytes 6488064 | tf_op jit(solution)/shard_map/dot_general | solution.py:33
  (11 shorter events, 0.1 us)
Async XLA Ops:
  6.5 19.0 %copy-start = (bf16[768,768]{1,0:T(8,128)(2,1)S(1)}, bf16[768,768]{1,0:T(8,128)(2,1)}, u32[]{:S(2)}) copy-start(bf16[768,768]{1,0:T(8,128)(2,1)} %param.14) | copy-start | bytes 3538948
  6.5 93.1 %all-gather.5.cloned.1.call-start = ((), (), s32[]{:S(2)}) async-start(), calls=%async_computation.1 | async-start | bytes 8847360 | tf_op jit(solution)/shard_map/all_gather | solution.py:81
  12.1 11.7 %copy-start.2 = (f32[4,768]{1,0:T(4,128)S(1)}, f32[4,768]{1,0:T(4,128)}, u32[]{:S(2)}) copy-start(f32[4,768]{1,0:T(4,128)} %param.13) | copy-start | bytes 36868
  12.3 13.3 %collective-permute-start.1 = (bf16[4,1,12,768]{3,1,2,0:T(2,128)(2,1)S(1)}, bf16[4,1,12,768]{3,1,2,0:T(2,128)(2,1)S(1)}, u32[]{:S(2)}, u32[]{:S(2)}) collective-permute-start(bf16[4,1,12,768]{3,1,2,0:T(2,128)(2,1)S(1)} %get-tuple-element.12), channel_id=1, source_target_pairs={{0,4},{4,8},{8,12},{12,16},{16,20},{20,24},{24,28},{28,32},{32,36}... | collective-permute-start | bytes 221192 | tf_op jit(solution)/shard_map/ppermute | solution.py:20
  14.4 11.1 %collective-permute-start = (bf16[4,1,12,768]{3,1,2,0:T(2,128)(2,1)S(1)}, bf16[4,1,12,768]{3,1,2,0:T(2,128)(2,1)S(1)}, u32[]{:S(2)}, u32[]{:S(2)}) collective-permute-start(bf16[4,1,12,768]{3,1,2,0:T(2,128)(2,1)S(1)} %get-tuple-element.11), channel_id=1, source_target_pairs={{4,0},{8,4},{12,8},{16,12},{20,16},{24,20},{28,24},{32,28},{36,32}... | collective-permute-start | bytes 221192 | tf_op jit(solution)/shard_map/ppermute | solution.py:21
  37.3 5.1 %copy-start.3 = (bf16[768,768]{1,0:T(8,128)(2,1)S(1)}, bf16[768,768]{1,0:T(8,128)(2,1)}, u32[]{:S(2)}) copy-start(bf16[768,768]{1,0:T(8,128)(2,1)} %param.16) | copy-start | bytes 3538948
  42.1 4.6 %copy-start.4 = (s32[48]{0:T(128)S(1)}, s32[48]{0:T(128)}, u32[]{:S(2)}) copy-start(s32[48]{0:T(128)} %param.10) | copy-start | bytes 580
  42.1 116.2 %all-gather.3.cloned.1.call-start = ((), (), s32[]{:S(2)}) async-start(), calls=%async_computation | async-start | bytes 8847360 | tf_op jit(solution)/shard_map/all_gather | solution.py:82
  200.3 10.3 %copy-start.1 = (bf16[768,768]{1,0:T(8,128)(2,1)S(1)}, bf16[768,768]{1,0:T(8,128)(2,1)}, u32[]{:S(2)}) copy-start(bf16[768,768]{1,0:T(8,128)(2,1)} %param.14) | copy-start | bytes 3538948
Sparse Core Ops, SparseCore 0:
  42.3 57.3 all-gather.4
  101.4 56.8 all-gather.2
where the time goes:
time: 219 us; the launch traced here: 217 us
  matrix products  72.3 us (33%)
  local copies, waits for them, and re-layouts  59.4 us (27%)
  waiting for transfers between devices  51.8 us (24%)
  between operations  13.5 us (6%)
  other arithmetic  10.3 us (5%)
  starting transfers between devices  10 us (5%)
    reshape x3, local copies, waits for them, and re-layouts, head_split(): return inputs.reshape(inputs.shape[:-1] + (inputs.shape[-1] // HEAD, HEAD))  48.4 us
    all_gather x1, waiting for transfers between devices, per_device(): lax.all_gather(keys_local, 'level', axis=2, tiled=True)  44.7 us
    dot_general x6, matrix products, project(): product = jnp.dot(flattened, weight, preferred_element_type=jnp.float32)  32.5 us
    dot_general x1, matrix products, per_device(): jnp.einsum('ncqhd,nckhd->ncqhk', queries, key_piece, preferred_element_ty...  23.2 us
    dot_general x1, matrix products, per_device(): jnp.einsum('ncqhk,nckhd->ncqhd', weights.astype(jnp.bfloat16), value_piec...  16.7 us
    reduce_sum x1, other arithmetic, per_device(): denominator = jnp.sum(weights, axis=-1)  8.23 us
    ppermute x1, starting transfers between devices, padded_2(): after = lax.ppermute(initial, axis, down)  7.66 us
    dot_general x1, local copies, waits for them, and re-layouts, project(): product = jnp.dot(flattened, weight, preferred_element_type=jnp.float32)  5.63 us
  transfers between devices with their start and end apart: 4, of which 3 were waited for; matrix products, arithmetic and copies ran while one was open for 31% of the time, Pallas kernels for 0%

commit v1 on v0

v1 whole, which is shorter than its diff:
```python
import functools

import jax
import jax.numpy as jnp
import numpy as np
from jax import lax
from jax.experimental import pallas as pl
from jax.experimental.pallas import tpu as pltpu
from jax.sharding import PartitionSpec as P

HEAD = 64
EPSILON = 1e-06
MASKED = -1e30
GROUP = 8
F32, BF16 = jnp.float32, jnp.bfloat16
WHOLE = pl.BlockSpec(memory_space=pltpu.VMEM)
SCALARS = pl.BlockSpec(memory_space=pltpu.SMEM)


def params(mib=24):
    return pltpu.CompilerParams(vmem_limit_bytes=mib << 20)


def normalize(x):
    return x * lax.rsqrt(jnp.mean(x * x, axis=-1, keepdims=True) + EPSILON)


def matmul(x, weight):
    return jnp.dot(x, weight, preferred_element_type=F32)


def block_of(ref, row, block, levels):
    lon = ref.shape[-2] // levels
    x = ref[row].astype(F32).reshape(levels, lon, ref.shape[-1])
    x = x[:, GROUP * block : GROUP * (block + 1)]
    return x.reshape(levels * GROUP, ref.shape[-1])


def source_kernel(nodes_ref, weight_ref, normed_ref, source_ref):
    normed = normalize(nodes_ref[0].astype(F32)).astype(BF16)
    normed_ref[0] = normed
    source_ref[0] = (matmul(normed, weight_ref[...]) * 0.5).astype(BF16)


def sources(nodes, weight):
    rows, width = nodes.shape[1:]
    block = pl.BlockSpec((1, rows, width), lambda i: (i, 0, 0))
    like = jax.ShapeDtypeStruct(nodes.shape, BF16)
    return pl.pallas_call(
        source_kernel,
        grid=(nodes.shape[0],),
        in_specs=[block, WHOLE],
        out_specs=[block, block],
        out_shape=[like, like],
        compiler_params=params(),
        cost_estimate=pl.CostEstimate(
            flops=2 * nodes.size * width, bytes_accessed=8 * nodes.size, transcendentals=0
        ),
    )(nodes, weight)


def message_kernel(blocks, levels, order, normed_ref, source_ref, nodes_ref, target_w, node_w, bias_ref, *rest):
    lon = normed_ref.shape[1] // levels
    edges = 0 in blocks or lon // GROUP - 1 in blocks
    if edges:
        west_ref, east_ref = rest[:2]
        rest = rest[2:]
    out_ref, target_ref, sum_ref = rest
    last = normed_ref.shape[0] - 1
    width = normed_ref.shape[-1]
    size = levels * GROUP
    pieces = [(i, b) for b in blocks for i in range(2)]
    x = [block_of(normed_ref, order[i], b, levels).astype(BF16) for i, b in pieces]
    target_ref[...] = matmul(jnp.concatenate(x, axis=0), target_w[...]) * 0.5
    step = 128
    for n, (i, b) in enumerate(pieces):
        row = order[i]
        north, south = jnp.maximum(row - 1, 0), jnp.minimum(row + 1, last)
        has_north = jnp.where(row >= 1, 1.0, 0.0)
        has_south = jnp.where(row <= last - 1, 1.0, 0.0)
        if edges:
            west_edge = west_ref[row].astype(F32)
            east_edge = east_ref[row].astype(F32)
        for pair in range(levels // 2):
            for lane in range(0, width, step):
                cols = slice(lane, lane + step)
                rows = slice(2 * lon * pair, 2 * lon * (pair + 1))

                def take(x):
                    x = x.reshape(2, lon, step)[:, GROUP * b : GROUP * (b + 1)]
                    return x.reshape(2 * GROUP, step)

                middle = source_ref[row, rows, cols].astype(F32)
                east = take(pltpu.roll(middle, 2 * lon - 1, 0))
                west = take(pltpu.roll(middle, 1, 0))
                if edges and b == 0:
                    at = lax.broadcasted_iota(jnp.int32, (GROUP, step), 0) == 0
                    west = jnp.concatenate(
                        [
                            jnp.where(at, west_edge[2 * pair + k : 2 * pair + k + 1, cols], west[GROUP * k : GROUP * (k + 1)])
                            for k in range(2)
                        ],
                        axis=0,
                    )
                if edges and GROUP * (b + 1) == lon:
                    at = lax.broadcasted_iota(jnp.int32, (GROUP, step), 0) == GROUP - 1
                    east = jnp.concatenate(
                        [
                            jnp.where(at, east_edge[2 * pair + k : 2 * pair + k + 1, cols], east[GROUP * k : GROUP * (k + 1)])
                            for k in range(2)
                        ],
                        axis=0,
                    )
                target = target_ref[slice(n * size + 16 * pair, n * size + 16 * (pair + 1)), cols]

                def halved_silu(other, k):
                    half = target + other + bias_ref[k : k + 1, cols] * 0.5
                    return half + half * jnp.tanh(half)

                total = halved_silu(east, 0) + halved_silu(west, 1)
                other = take(source_ref[north, rows, cols].astype(F32))
                total = total + halved_silu(other, 2) * has_north
                other = take(source_ref[south, rows, cols].astype(F32))
                total = total + halved_silu(other, 3) * has_south
                sum_ref[n * size + 16 * pair : n * size + 16 * (pair + 1), cols] = total.astype(BF16)
    update = matmul(sum_ref[...], node_w[...])
    for n, (i, b) in enumerate(pieces):
        own = block_of(nodes_ref, order[i], b, levels)
        out_ref[n // 2, n % 2] = (own + update[n * size : (n + 1) * size]).astype(BF16)


def messages(blocks, levels, order, normed, source, nodes, target_w, node_w, bias, edges=()):
    size = levels * GROUP
    width = nodes.shape[-1]
    rows = 2 * len(blocks) * size
    args = (order, normed, source, nodes, target_w, node_w, bias, *edges)
    return pl.pallas_call(
        functools.partial(message_kernel, blocks, levels),
        in_specs=[SCALARS] + [WHOLE] * (len(args) - 1),
        out_specs=WHOLE,
        out_shape=jax.ShapeDtypeStruct((len(blocks), 2, size, width), BF16),
        scratch_shapes=[pltpu.VMEM((rows, width), F32), pltpu.VMEM((rows, width), BF16)],
        compiler_params=params(),
        cost_estimate=pl.CostEstimate(
            flops=4 * rows * width * width, bytes_accessed=16 * rows * width, transcendentals=4 * rows * width
        ),
    )(*args)


def attention_kernel(
    block, own_ref, opposite_ref, sibling_ref, across_ref, bias_ref, gather_ref, scatter_ref,
    query_key, value_w, output_w, out_own, out_opposite, out_sibling, q_ref, k_ref, v_ref, att_ref,
):
    size, width = across_ref.shape
    x = jnp.concatenate([own_ref[block, 0], opposite_ref[0, 0], sibling_ref[block], across_ref[...]], axis=0)
    normed = normalize(x.astype(F32)).astype(BF16)
    normed = matmul(gather_ref[...], normed).astype(BF16)
    q_ref[...] = (matmul(normed, query_key[0]) * HEAD**-0.5).astype(BF16)
    k_ref[...] = matmul(normed, query_key[1]).astype(BF16)
    v_ref[...] = matmul(normed, value_w[...]).astype(BF16)
    levels = 4 * size // GROUP
    pair = 2 * HEAD
    low = lax.broadcasted_iota(jnp.int32, (levels, pair), 1) < HEAD
    pad = jnp.zeros((pair - 2 * levels, pair), BF16)
    bias = bias_ref[...]
    for column in range(GROUP):
        rows = slice(levels * column, levels * (column + 1))
        for lane in range(0, width, pair):
            cols = slice(lane, lane + pair)
            query, key, value = q_ref[rows, cols], k_ref[rows, cols], v_ref[rows, cols]
            zero = jnp.zeros_like(query)
            both = jnp.concatenate([jnp.where(low, query, zero), jnp.where(low, zero, query), pad], axis=0)
            scores = lax.dot_general(key, both, (((1,), (1,)), ((), ())), preferred_element_type=F32)
            scores = scores + bias
            weights = jnp.exp(scores - jnp.max(scores, axis=0, keepdims=True))
            weights = weights * (1.0 / jnp.sum(weights, axis=0, keepdims=True))
            mixed = lax.dot_general(
                weights.astype(BF16), value, (((0,), (0,)), ((), ())), preferred_element_type=F32
            )
            att_ref[rows, cols] = jnp.where(low, mixed[:levels], mixed[levels : 2 * levels]).astype(BF16)
    attended = matmul(scatter_ref[...], att_ref[...]).astype(BF16)
    out = (x.astype(F32) + matmul(attended, output_w[...])).astype(BF16)
    out_own[...] = out[:size]
    out_opposite[...] = out[size : 2 * size]
    out_sibling[0] = out[2 * size : 3 * size]
    out_sibling[1] = out[3 * size :]


def attention(block, *args):
    size, width = args[3].shape
    rows = 4 * size
    piece = jax.ShapeDtypeStruct((size, width), BF16)
    return pl.pallas_call(
        functools.partial(attention_kernel, block),
        in_specs=[WHOLE] * len(args),
        out_specs=[WHOLE] * 3,
        out_shape=[piece, piece, jax.ShapeDtypeStruct((2, size, width), BF16)],
        scratch_shapes=[pltpu.VMEM((rows, width), BF16)] * 4,
        compiler_params=params(),
        cost_estimate=pl.CostEstimate(
            flops=14 * rows * width * width, bytes_accessed=16 * rows * width, transcendentals=rows * rows
        ),
    )(*args)


def finish_kernel(blocks, levels, place, *refs):
    out_ref = refs[-1]
    own, siblings, opposites = (refs[blocks * k : blocks * (k + 1)] for k in range(3))
    width = out_ref.shape[-1]
    lon = GROUP * blocks

    def write(pieces):
        for pair in range(levels // 2):
            rows = slice(2 * GROUP * pair, 2 * GROUP * (pair + 1))
            parts = [p[rows].astype(F32).reshape(2, GROUP, width) for p in pieces]
            whole = jnp.concatenate(parts, axis=1).reshape(2 * lon, width)
            out_ref[0, 2 * lon * pair : 2 * lon * (pair + 1)] = whole.astype(BF16)

    @pl.when(pl.program_id(0) == 0)
    def _():
        write(own)

    @pl.when(pl.program_id(0) == 1)
    def _():
        write([s.at[0] for s in siblings])

    @pl.when(pl.program_id(0) == 2)
    def _():
        write([s.at[0] for s in opposites])

    @pl.when(pl.program_id(0) == 3)
    def _():
        write([s.at[1] for s in opposites])


def finish(levels, place, own, siblings, opposites):
    blocks = len(own)
    width = own[0].shape[-1]
    rows = levels * GROUP * blocks
    args = (*own, *siblings, *opposites)
    return pl.pallas_call(
        functools.partial(finish_kernel, blocks, levels),
        grid_spec=pltpu.PrefetchScalarGridSpec(
            num_scalar_prefetch=1,
            grid=(4,),
            in_specs=[WHOLE] * len(args),
            out_specs=pl.BlockSpec((1, rows, width), lambda i, place: (i ^ place[0], 0, 0)),
        ),
        out_shape=jax.ShapeDtypeStruct((4, rows, width), BF16),
        compiler_params=params(),
        cost_estimate=pl.CostEstimate(flops=0, bytes_accessed=16 * rows * width, transcendentals=0),
    )(place, *args)


def per_device(
    nodes, level_mask, source_weight, target_weight, direction_bias, node_weight, query_key, value_weight, output_weight
):
    lat, lon, levels, width = nodes.shape
    blocks = lon // GROUP
    rows = levels * lon
    here = lax.axis_index("level")
    opposite = [(i, i ^ 2) for i in range(4)]
    sibling = [(i, i ^ 1) for i in range(4)]
    ring = lax.axis_size("sector")
    up = [(i, (i + 1) % ring) for i in range(ring)]
    down = [(j, i) for i, j in up]

    nodes = jnp.transpose(nodes, (0, 2, 1, 3)).reshape(lat, rows, width)
    own_rows = jnp.stack([here, here ^ 1]).astype(jnp.int32)
    far_rows = own_rows ^ 2
    kept = jnp.where(level_mask > 0, 0.0, MASKED).astype(F32).reshape(4, levels)
    kept = jnp.concatenate([lax.dynamic_slice(kept, (here ^ k, 0), (1, levels)) for k in (0, 2, 1, 3)], axis=0)
    bias = jnp.broadcast_to(kept.reshape(4 * levels, 1), (4 * levels, 2 * HEAD))
    total = 4 * levels * GROUP
    gather = np.zeros((total, total), np.float32)
    at = np.arange(total)
    gather[at, GROUP * (at % (4 * levels)) + at // (4 * levels)] = 1
    gather, scatter = jnp.asarray(gather, BF16), jnp.asarray(gather.T, BF16)

    normed, source = sources(nodes, source_weight)
    edge = source.reshape(lat, levels, lon, width)
    west = lax.ppermute(edge[:, :, lon - 1], "sector", up)
    east = lax.ppermute(edge[:, :, 0], "sector", down)
    message = functools.partial(
        messages,
        levels=levels,
        normed=normed,
        source=source,
        nodes=nodes,
        target_w=target_weight,
        node_w=node_weight,
        bias=direction_bias,
    )
    far = {1: message((1,), order=far_rows)}
    far[0] = message((0,), order=far_rows, edges=(west, east))
    far[2] = message((2,), order=far_rows, edges=(west, east))
    own = message(tuple(range(blocks)), order=own_rows, edges=(west, east))

    near = lax.ppermute(own[:, 1], "level", sibling)
    done_own, done_sibling, done_opposite = {}, {}, {}
    for b in (1, 0, 2):
        arrived = lax.ppermute(far[b], "level", opposite)
        across = lax.ppermute(arrived[0, 1], "level", sibling)
        done_own[b], toward, beside = attention(
            b, own, arrived, near, across, bias, gather, scatter, query_key, value_weight, output_weight
        )
        done_sibling[b] = lax.ppermute(beside, "level", sibling)
        back = jnp.stack([toward, done_sibling[b][1]])
        done_opposite[b] = lax.ppermute(back, "level", opposite)
    place = here.reshape(1).astype(jnp.int32)
    listed = lambda d: [d[b] for b in range(blocks)]
    out = finish(levels, place, listed(done_own), listed(done_sibling), listed(done_opposite))
    return jnp.transpose(out.reshape(lat, levels, lon, width), (0, 2, 1, 3))


def solution(mesh):
    placed = (P(None, "sector", "level", None), P(), P(), P(), P(), P(), P(), P(), P())
    return jax.shard_map(
        per_device,
        mesh=mesh,
        in_specs=placed,
        out_specs=P(None, "sector", "level", None),
        check_vma=False,
    )
```

time: 219 us -> 125 us (0.57)
  matrix products: 72.3 us -> 0 us
  Pallas kernels: 0 us -> 58.9 us
  local copies, waits for them, and re-layouts: 59.4 us -> 18.1 us
  waiting for transfers between devices: 51.8 us -> 19.9 us
  starting transfers between devices: 10 us -> 24.8 us
  between operations: 13.5 us -> 0.21 us
  other arithmetic: 10.3 us -> 2.48 us
    dot_general x8 -> x0, matrix products: 72.3 us -> none  [the longest x6 32.5 us: project(): product = jnp.dot(flattened, weight, preferred_element_type=jnp.float32)]
    pallas_call x0 -> x9, Pallas kernels: none -> 58.9 us  [the longest x3 42.9 us: attention(): pl.pallas_call(functools.partial(attention_kernel, block), in_specs=[WHOL...]
    all_gather x2 -> x0, waiting for transfers between devices: 50 us -> none  [the longest x1 44.7 us: per_device(): lax.all_gather(keys_local, 'level', axis=2, tiled=True)]
    reshape x3 -> x1, local copies, waits for them, and re-layouts: 48.4 us -> 1.29 us  [per_device(): kept = jnp.where(level_mask > 0, 0.0, MASKED).astype(F32).reshape(4, levels)]
    ppermute x2 -> x15, waiting for transfers between devices: 1.73 us -> 19.9 us  [the longest x3 18.6 us: per_device(): done_opposite[b] = lax.ppermute(back, 'level', opposite)]
    ppermute x2 -> x15, starting transfers between devices: 9.78 us -> 24.8 us  [the longest x1 7.57 us: per_device(): east = lax.ppermute(edge[:, :, 0], 'sector', down)]
    unnamed x10 -> x38, local copies, waits for them, and re-layouts: 0.03 us -> 13.3 us
    reduce_sum x2 -> x0, other arithmetic: 10.2 us -> none  [the longest x1 8.23 us: per_device(): denominator = jnp.sum(weights, axis=-1)]
  transfers between devices with their start and end apart: 4 -> 15, of which waited for: 3 -> 4; matrix products, arithmetic and copies ran while one was open for 31% -> 6% of each run, Pallas kernels for 0% -> 44%
where the time goes in v1:
time: 125 us; the launch traced here: 124 us
  Pallas kernels  58.9 us (47%)
  starting transfers between devices  24.8 us (20%)
  waiting for transfers between devices  19.9 us (16%)
  local copies, waits for them, and re-layouts  18.1 us (14%)
  other arithmetic  2.48 us (2%)
    pallas_call x3, Pallas kernels, attention(): pl.pallas_call(functools.partial(attention_kernel, block), in_specs=[WHOL...  42.9 us
    ppermute x3, waiting for transfers between devices, per_device(): done_opposite[b] = lax.ppermute(back, 'level', opposite)  18.6 us
    unnamed x38, local copies, waits for them, and re-layouts  13.3 us
    pallas_call x4, Pallas kernels, messages(): pl.pallas_call(functools.partial(message_kernel, blocks, levels), in_spec...  11.9 us
    ppermute x1, starting transfers between devices, per_device(): east = lax.ppermute(edge[:, :, 0], 'sector', down)  7.57 us
    ppermute x3, starting transfers between devices, per_device(): arrived = lax.ppermute(far[b], 'level', opposite)  5.76 us
    ppermute x3, starting transfers between devices, per_device(): done_opposite[b] = lax.ppermute(back, 'level', opposite)  3.58 us
    ppermute x3, starting transfers between devices, per_device(): across = lax.ppermute(arrived[0, 1], 'level', sibling)  3.11 us
  transfers between devices with their start and end apart: 15, of which 4 were waited for; matrix products, arithmetic and copies ran while one was open for 6% of the time, Pallas kernels for 44%

profile of v1, /device:TPU:1, one launch (start us, length us, event | category | flops | bytes accessed | tf_op | source)
XLA Modules:
  0.0 124.3 jit_solution(3564929524816906383)
XLA Ops:
  0.0 1.5 %copy-done = bf16[4,24,12,768]{3,1,2,0:T(8,128)(2,1)S(1)} copy-done((bf16[4,24,12,768]{3,1,2,0:T(8,128)(2,1)S(1)}, bf16[4,24,12,768]{3,1,2,0:T(8,128)(2,1)}, u32[]{:S(2)}) %copy-start) | copy-done | bytes 1769496
  1.5 1.3 %copy-done.12 = bf16[768,768]{1,0:T(8,128)(2,1)S(1)} copy-done((bf16[768,768]{1,0:T(8,128)(2,1)S(1)}, bf16[768,768]{1,0:T(8,128)(2,1)}, u32[]{:S(2)}) %copy-start.12) | copy-done | bytes 1179672
  2.8 2.4 %shard_map.109 = (bf16[4,288,768]{2,1,0:T(8,128)(2,1)S(1)}, bf16[4,288,768]{2,1,0:T(8,128)(2,1)S(1)}) custom-call(bf16[4,288,768]{2,1,0:T(8,128)(2,1)S(1)} %bitcast.29, bf16[768,768]{1,0:T(8,128)(2,1)S(1)} %copy-done.12), custom_call_target="tpu_custom_call" | custom-call | flops 1358954496 | bytes 7077888 | tf_op jit(solution)/shard_map/pallas_call | solution.py:49
  5.1 1.2 copy-done.2
  7.2 2.0 %collective-permute-start = (bf16[4,12,768]{2,1,0:T(8,128)(2,1)}, bf16[4,12,768]{2,1,0:T(8,128)(2,1)}, u32[]{:S(2)}, u32[]{:S(2)}) collective-permute-start(bf16[4,12,768]{2,1,0:T(8,128)(2,1)} %bitcast.27), channel_id=1, source_target_pairs={{0,4},{4,8},{8,12},{12,16},{16,20},{20,24},{24,28},{28,32},{32,36}... | collective-permute-start | bytes 221192 | tf_op jit(solution)/shard_map/ppermute | solution.py:282
  9.9 7.6 %collective-permute-start.1 = (bf16[4,12,768]{2,1,0:T(8,128)(2,1)}, bf16[4,12,768]{2,1,0:T(8,128)(2,1)}, u32[]{:S(2)}, u32[]{:S(2)}) collective-permute-start(bf16[4,12,768]{2,1,0:T(8,128)(2,1)} %bitcast.26), channel_id=1, source_target_pairs={{4,0},{8,4},{12,8},{16,12},{20,16},{24,20},{28,24},{32,28},{36,32}... | collective-permute-start | bytes 221192 | tf_op jit(solution)/shard_map/ppermute | solution.py:283
  18.1 1.5 %copy-done.3 = bf16[4,288,768]{2,1,0:T(8,128)(2,1)S(1)} copy-done((bf16[4,288,768]{2,1,0:T(8,128)(2,1)S(1)}, bf16[4,288,768]{2,1,0:T(8,128)(2,1)}, u32[]{:S(2)}) %copy-start.3) | copy-done | bytes 1769496
  19.6 1.3 %copy-done.5 = bf16[768,768]{1,0:T(8,128)(2,1)S(1)} copy-done((bf16[768,768]{1,0:T(8,128)(2,1)S(1)}, bf16[768,768]{1,0:T(8,128)(2,1)}, u32[]{:S(2)}) %copy-start.5) | copy-done | bytes 1179672
  20.9 1.3 %copy-done.7 = bf16[768,768]{1,0:T(8,128)(2,1)S(1)} copy-done((bf16[768,768]{1,0:T(8,128)(2,1)S(1)}, bf16[768,768]{1,0:T(8,128)(2,1)}, u32[]{:S(2)}) %copy-start.7) | copy-done | bytes 1179672
  22.1 2.6 %shard_map.113 = bf16[1,2,96,768]{3,2,1,0:T(8,128)(2,1)} custom-call(s32[2]{0:T(128)S(1)} %get-tuple-element.27.order, bf16[4,288,768]{2,1,0:T(8,128)(2,1)S(1)} %copy-done.3, bf16[4,288,768]{2,1,0:T(8,128)(2,1)S(1)} %get-tuple-element.17.source_ref, bf16[4,288,768]{2,1,0:T(8,128)(2,1)S(1)} %bitcast.30, bf16[768,768]{1,0:T(8,128)(2,1)S(1)} %copy-done.5, ...), custom_call_target="tpu_custom_call" | custom-call | flops 452984832 | bytes 2359296 | tf_op jit(solution)/shard_map/pallas_call | solution.py:137
  24.7 2.6 %collective-permute-start.5 = (bf16[1,2,96,768]{3,2,1,0:T(8,128)(2,1)}, bf16[1,2,96,768]{3,2,1,0:T(8,128)(2,1)}, u32[]{:S(2)}, u32[]{:S(2)}) collective-permute-start(bf16[1,2,96,768]{3,2,1,0:T(8,128)(2,1)} %shard_map.113), channel_id=1, source_target_pairs={{0,2},{1,3},{2,0},{3,1},{4,6},{5,7},{6,4},{7,5},{8,10},{9,11},{10,... | collective-permute-start | bytes 884744 | tf_op jit(solution)/shard_map/ppermute | solution.py:302
  27.3 1.2 compare_select_fusion
  28.5 1.3 %reshape.20 = f32[4,12]{1,0:T(4,128)} reshape(f32[48]{0:T(128)} %compare_select_fusion) | data formatting | bytes 384 | tf_op jit(solution)/shard_map/reshape | solution.py:271
  31.2 1.3 %broadcast_in_dim.17 = f32[48]{0:T(128)} reshape(f32[4,12]{1,0:T(4,128)} %pad_maximum_fusion.3) | data formatting | bytes 384 | tf_op jit(solution)/shard_map/broadcast_in_dim | solution.py:273
  32.6 1.5 %copy-done.4 = bf16[4,288,768]{2,1,0:T(8,128)(2,1)S(1)} copy-done((bf16[4,288,768]{2,1,0:T(8,128)(2,1)S(1)}, bf16[4,288,768]{2,1,0:T(8,128)(2,1)}, u32[]{:S(2)}) %copy-start.4) | copy-done | bytes 1769496
  34.0 1.3 %copy-done.6 = bf16[768,768]{1,0:T(8,128)(2,1)S(1)} copy-done((bf16[768,768]{1,0:T(8,128)(2,1)S(1)}, bf16[768,768]{1,0:T(8,128)(2,1)}, u32[]{:S(2)}) %copy-start.6) | copy-done | bytes 1179672
  35.3 1.3 %copy-done.8 = bf16[768,768]{1,0:T(8,128)(2,1)S(1)} copy-done((bf16[768,768]{1,0:T(8,128)(2,1)S(1)}, bf16[768,768]{1,0:T(8,128)(2,1)}, u32[]{:S(2)}) %copy-start.8) | copy-done | bytes 1179672
  36.6 2.3 %shard_map.111 = bf16[1,2,96,768]{3,2,1,0:T(8,128)(2,1)S(1)} custom-call(s32[2]{0:T(128)S(1)} %get-tuple-element.27.order, bf16[4,288,768]{2,1,0:T(8,128)(2,1)S(1)} %copy-done.4, bf16[4,288,768]{2,1,0:T(8,128)(2,1)S(1)} %get-tuple-element.17.source_ref, bf16[4,288,768]{2,1,0:T(8,128)(2,1)S(1)} %bitcast.31, bf16[768,768]{1,0:T(8,128)(2,1)S(1)} %copy-done.6, ...), custom_call_target="tpu_custom_call" | custom-call | flops 452984832 | bytes 2359296 | tf_op jit(solution)/shard_map/pallas_call | solution.py:137
  39.4 2.3 %shard_map.115 = bf16[1,2,96,768]{3,2,1,0:T(8,128)(2,1)S(1)} custom-call(s32[2]{0:T(128)S(1)} %get-tuple-element.27.order, bf16[4,288,768]{2,1,0:T(8,128)(2,1)S(1)} %copy-done.4, bf16[4,288,768]{2,1,0:T(8,128)(2,1)S(1)} %get-tuple-element.17.source_ref, bf16[4,288,768]{2,1,0:T(8,128)(2,1)S(1)} %bitcast.32, bf16[768,768]{1,0:T(8,128)(2,1)S(1)} %copy-done.6, ...), custom_call_target="tpu_custom_call" | custom-call | flops 452984832 | bytes 2359296 | tf_op jit(solution)/shard_map/pallas_call | solution.py:137
  41.7 2.7 %collective-permute-start.7 = (bf16[1,2,96,768]{3,2,1,0:T(8,128)(2,1)S(1)}, bf16[1,2,96,768]{3,2,1,0:T(8,128)(2,1)S(1)}, u32[]{:S(2)}, u32[]{:S(2)}) collective-permute-start(bf16[1,2,96,768]{3,2,1,0:T(8,128)(2,1)S(1)} %shard_map.115), channel_id=1, source_target_pairs={{0,2},{1,3},{2,0},{3,1},{4,6},{5,7},{6,4},{7,5},{8,10},{9,11},{10,... | collective-permute-start | bytes 884744 | tf_op jit(solution)/shard_map/ppermute | solution.py:302
  44.4 4.7 %shard_map.110.own_ref = bf16[3,2,96,768]{3,2,1,0:T(8,128)(2,1)S(1)} custom-call(s32[2]{0:T(128)S(1)} %copy-done.10, bf16[4,288,768]{2,1,0:T(8,128)(2,1)S(1)} %copy-done.4, bf16[4,288,768]{2,1,0:T(8,128)(2,1)S(1)} %get-tuple-element.17.source_ref, bf16[4,288,768]{2,1,0:T(8,128)(2,1)S(1)} %bitcast.33, bf16[768,768]{1,0:T(8,128)(2,1)S(1)} %copy-done.6, ...), custom_call_target="tpu_custom_call" | custom-call | flops 1358954496 | bytes 7077888 | tf_op jit(solution)/shard_map/pallas_call | solution.py:137
  49.2 1.9 %collective-permute-start.3 = (bf16[3,96,768]{2,1,0:T(8,128)(2,1)S(1)}, bf16[3,96,768]{2,1,0:T(8,128)(2,1)S(1)}, u32[]{:S(2)}, u32[]{:S(2)}) collective-permute-start(bf16[3,96,768]{2,1,0:T(8,128)(2,1)S(1)} %slice_bitcast_fusion), channel_id=1, source_target_pairs={{0,1},{1,0},{2,3},{3,2},{4,5},{5,4},{6,7},{7,6},{8,9},{9,8},{10,11... | collective-permute-start | bytes 1327112 | tf_op jit(solution)/shard_map/ppermute | solution.py:299
  52.9 1.2 collective-permute-done.7.opposite_ref
  54.1 2.2 %collective-permute-start.8 = (bf16[96,768]{1,0:T(8,128)(2,1)S(1)}, bf16[96,768]{1,0:T(8,128)(2,1)S(1)}, u32[]{:S(2)}, u32[]{:S(2)}) collective-permute-start(bf16[96,768]{1,0:T(8,128)(2,1)S(1)} %slice_bitcast_fusion.1), channel_id=1, source_target_pairs={{0,1},{1,0},{2,3},{3,2},{4,5},{5,4},{6,7},{7,6},{8,9},{9,8},{10,11... | collective-permute-start | bytes 442376 | tf_op jit(solution)/shard_map/ppermute | solution.py:303
  56.5 14.9 %shard_map.114 = (bf16[96,768]{1,0:T(8,128)(2,1)S(1)}, bf16[96,768]{1,0:T(8,128)(2,1)S(1)}, bf16[2,96,768]{2,1,0:T(8,128)(2,1)S(1)}) custom-call(bf16[3,2,96,768]{3,2,1,0:T(8,128)(2,1)S(1)} %shard_map.110.own_ref, bf16[1,2,96,768]{3,2,1,0:T(8,128)(2,1)} %collective-permute-done.5.opposite_ref, bf16[3,96,768]{2,1,0:T(8,128)(2,1)S(1)} %collective-permute-done.3.sibling_ref, ...), custom_call_target="tpu_custom_call" | custom-call | flops 3170893824 | bytes 4718592 | tf_op jit(solution)/shard_map/pallas_call | solution.py:193
  71.5 14.0 %shard_map.112 = (bf16[96,768]{1,0:T(8,128)(2,1)S(1)}, bf16[96,768]{1,0:T(8,128)(2,1)S(1)}, bf16[2,96,768]{2,1,0:T(8,128)(2,1)S(1)}) custom-call(bf16[3,2,96,768]{3,2,1,0:T(8,128)(2,1)S(1)} %shard_map.110.own_ref, bf16[1,2,96,768]{3,2,1,0:T(8,128)(2,1)S(1)} %collective-permute-done.2.opposite_ref, ...), custom_call_target="tpu_custom_call" | custom-call | flops 3170893824 | bytes 4718592 | tf_op jit(solution)/shard_map/pallas_call | solution.py:193
  86.1 14.0 %shard_map.116 = (bf16[96,768]{1,0:T(8,128)(2,1)S(1)}, bf16[96,768]{1,0:T(8,128)(2,1)S(1)}, bf16[2,96,768]{2,1,0:T(8,128)(2,1)S(1)}) custom-call(bf16[3,2,96,768]{3,2,1,0:T(8,128)(2,1)S(1)} %shard_map.110.own_ref, bf16[1,2,96,768]{3,2,1,0:T(8,128)(2,1)S(1)} %collective-permute-done.7.opposite_ref, ...), custom_call_target="tpu_custom_call" | custom-call | flops 3170893824 | bytes 4718592 | tf_op jit(solution)/shard_map/pallas_call | solution.py:193
  100.7 2.7 %collective-permute-start.12 = (bf16[2,96,768]{2,1,0:T(8,128)(2,1)S(1)}, bf16[2,96,768]{2,1,0:T(8,128)(2,1)S(1)}, u32[]{:S(2)}, u32[]{:S(2)}) collective-permute-start(bf16[2,96,768]{2,1,0:T(8,128)(2,1)S(1)} %pad_maximum_fusion), channel_id=1, source_target_pairs={{0,2},{1,3},{2,0},{3,1},{4,6},{5,7},{6,4},{7,5},{8,10},{9,11},{10,... | collective-permute-start | bytes 884744 | tf_op jit(solution)/shard_map/ppermute | solution.py:309
  103.9 6.0 %collective-permute-done.13.refs_7_ = bf16[2,96,768]{2,1,0:T(8,128)(2,1)S(1)} collective-permute-done((bf16[2,96,768]{2,1,0:T(8,128)(2,1)S(1)}, bf16[2,96,768]{2,1,0:T(8,128)(2,1)S(1)}, u32[]{:S(2)}, u32[]{:S(2)}) %collective-permute-start.13) | collective-permute-done | bytes 294944 | tf_op jit(solution)/shard_map/ppermute | solution.py:309
  110.0 6.3 %collective-permute-done.12.refs_6_ = bf16[2,96,768]{2,1,0:T(8,128)(2,1)S(1)} collective-permute-done((bf16[2,96,768]{2,1,0:T(8,128)(2,1)S(1)}, bf16[2,96,768]{2,1,0:T(8,128)(2,1)S(1)}, u32[]{:S(2)}, u32[]{:S(2)}) %collective-permute-start.12) | collective-permute-done | bytes 294944 | tf_op jit(solution)/shard_map/ppermute | solution.py:309
  116.3 6.3 %collective-permute-done.14.refs_8_ = bf16[2,96,768]{2,1,0:T(8,128)(2,1)S(1)} collective-permute-done((bf16[2,96,768]{2,1,0:T(8,128)(2,1)S(1)}, bf16[2,96,768]{2,1,0:T(8,128)(2,1)S(1)}, u32[]{:S(2)}, u32[]{:S(2)}) %collective-permute-start.14) | collective-permute-done | bytes 294944 | tf_op jit(solution)/shard_map/ppermute | solution.py:309
  122.6 1.7 %shard_map.117 = bf16[4,288,768]{2,1,0:T(8,128)(2,1)} custom-call(s32[1]{0:T(128)} %bitcast.place, bf16[96,768]{1,0:T(8,128)(2,1)S(1)} %get-tuple-element.18.refs_0_, bf16[96,768]{1,0:T(8,128)(2,1)S(1)} %get-tuple-element.19.refs_1_, bf16[96,768]{1,0:T(8,128)(2,1)S(1)} %get-tuple-element.20.refs_2_, bf16[2,96,768]{2,1,0:T(8,128)(2,1)S(1)} %collective-permute-done.9.refs_3_, ...), custom_call_target="tpu_custom_call" | custom-call | bytes 3538944 | tf_op jit(solution)/shard_map/pallas_call | solution.py:241
  (63 shorter events, 7.8 us)
Async XLA Ops:
  0.0 1.5 %copy-start = (bf16[4,24,12,768]{3,1,2,0:T(8,128)(2,1)S(1)}, bf16[4,24,12,768]{3,1,2,0:T(8,128)(2,1)}, u32[]{:S(2)}) copy-start(bf16[4,24,12,768]{3,1,2,0:T(8,128)(2,1)} %param.11) | copy-start | bytes 5308420
  1.5 1.3 %copy-start.12 = (bf16[768,768]{1,0:T(8,128)(2,1)S(1)}, bf16[768,768]{1,0:T(8,128)(2,1)}, u32[]{:S(2)}) copy-start(bf16[768,768]{1,0:T(8,128)(2,1)} %weight_ref.1) | copy-start | bytes 3538948
  2.7 15.3 %copy-start.1 = (bf16[4,24,12,768]{3,1,2,0:T(8,128)(2,1)S(1)}, bf16[4,24,12,768]{3,1,2,0:T(8,128)(2,1)}, u32[]{:S(2)}) copy-start(bf16[4,24,12,768]{3,1,2,0:T(8,128)(2,1)} %param.11) | copy-start | bytes 5308420
  2.8 15.3 %copy-start.9 = (f32[4,768]{1,0:T(4,128)S(1)}, f32[4,768]{1,0:T(4,128)}, u32[]{:S(2)}) copy-start(f32[4,768]{1,0:T(4,128)} %bias_ref.7) | copy-start | bytes 36868
  7.2 25.3 %collective-permute-start = (bf16[4,12,768]{2,1,0:T(8,128)(2,1)}, bf16[4,12,768]{2,1,0:T(8,128)(2,1)}, u32[]{:S(2)}, u32[]{:S(2)}) collective-permute-start(bf16[4,12,768]{2,1,0:T(8,128)(2,1)} %bitcast.27), channel_id=1, source_target_pairs={{0,4},{4,8},{8,12},{12,16},{16,20},{20,24},{24,28},{28,32},{32,36}... | collective-permute-start | bytes 221192 | tf_op jit(solution)/shard_map/ppermute | solution.py:282
  9.9 22.6 %collective-permute-start.1 = (bf16[4,12,768]{2,1,0:T(8,128)(2,1)}, bf16[4,12,768]{2,1,0:T(8,128)(2,1)}, u32[]{:S(2)}, u32[]{:S(2)}) collective-permute-start(bf16[4,12,768]{2,1,0:T(8,128)(2,1)} %bitcast.26), channel_id=1, source_target_pairs={{4,0},{8,4},{12,8},{16,12},{20,16},{24,20},{28,24},{32,28},{36,32}... | collective-permute-start | bytes 221192 | tf_op jit(solution)/shard_map/ppermute | solution.py:283
  18.1 1.5 %copy-start.3 = (bf16[4,288,768]{2,1,0:T(8,128)(2,1)S(1)}, bf16[4,288,768]{2,1,0:T(8,128)(2,1)}, u32[]{:S(2)}) copy-start(bf16[4,288,768]{2,1,0:T(8,128)(2,1)} %copy-done.2) | copy-start | bytes 5308420
  19.6 1.3 %copy-start.5 = (bf16[768,768]{1,0:T(8,128)(2,1)S(1)}, bf16[768,768]{1,0:T(8,128)(2,1)}, u32[]{:S(2)}) copy-start(bf16[768,768]{1,0:T(8,128)(2,1)} %target_w.7) | copy-start | bytes 3538948
  20.8 1.3 %copy-start.7 = (bf16[768,768]{1,0:T(8,128)(2,1)S(1)}, bf16[768,768]{1,0:T(8,128)(2,1)}, u32[]{:S(2)}) copy-start(bf16[768,768]{1,0:T(8,128)(2,1)} %node_w.7) | copy-start | bytes 3538948
  24.7 26.4 %collective-permute-start.5 = (bf16[1,2,96,768]{3,2,1,0:T(8,128)(2,1)}, bf16[1,2,96,768]{3,2,1,0:T(8,128)(2,1)}, u32[]{:S(2)}, u32[]{:S(2)}) collective-permute-start(bf16[1,2,96,768]{3,2,1,0:T(8,128)(2,1)} %shard_map.113), channel_id=1, source_target_pairs={{0,2},{1,3},{2,0},{3,1},{4,6},{5,7},{6,4},{7,5},{8,10},{9,11},{10,... | collective-permute-start | bytes 884744 | tf_op jit(solution)/shard_map/ppermute | solution.py:302
  32.6 1.5 %copy-start.4 = (bf16[4,288,768]{2,1,0:T(8,128)(2,1)S(1)}, bf16[4,288,768]{2,1,0:T(8,128)(2,1)}, u32[]{:S(2)}) copy-start(bf16[4,288,768]{2,1,0:T(8,128)(2,1)} %copy-done.2) | copy-start | bytes 5308420
  34.0 1.3 %copy-start.6 = (bf16[768,768]{1,0:T(8,128)(2,1)S(1)}, bf16[768,768]{1,0:T(8,128)(2,1)}, u32[]{:S(2)}) copy-start(bf16[768,768]{1,0:T(8,128)(2,1)} %target_w.7) | copy-start | bytes 3538948
  35.3 1.3 %copy-start.8 = (bf16[768,768]{1,0:T(8,128)(2,1)S(1)}, bf16[768,768]{1,0:T(8,128)(2,1)}, u32[]{:S(2)}) copy-start(bf16[768,768]{1,0:T(8,128)(2,1)} %node_w.7) | copy-start | bytes 3538948
  38.9 5.5 %copy-start.10 = (s32[2]{0:T(128)S(1)}, s32[2]{0:T(128)}, u32[]{:S(2)}) copy-start(s32[2]{0:T(128)} %get-tuple-element.28.order) | copy-start | bytes 28
  38.9 13.5 %collective-permute-start.2 = (bf16[1,2,96,768]{3,2,1,0:T(8,128)(2,1)S(1)}, bf16[1,2,96,768]{3,2,1,0:T(8,128)(2,1)S(1)}, u32[]{:S(2)}, u32[]{:S(2)}) collective-permute-start(bf16[1,2,96,768]{3,2,1,0:T(8,128)(2,1)S(1)} %shard_map.111), channel_id=1, source_target_pairs={{0,2},{1,3},{2,0},{3,1},{4,6},{5,7},{6,4},{7,5},{8,10},{9,11},{10,... | collective-permute-start | bytes 884744 | tf_op jit(solution)/shard_map/ppermute | solution.py:302
  41.7 12.4 %collective-permute-start.7 = (bf16[1,2,96,768]{3,2,1,0:T(8,128)(2,1)S(1)}, bf16[1,2,96,768]{3,2,1,0:T(8,128)(2,1)S(1)}, u32[]{:S(2)}, u32[]{:S(2)}) collective-permute-start(bf16[1,2,96,768]{3,2,1,0:T(8,128)(2,1)S(1)} %shard_map.115), channel_id=1, source_target_pairs={{0,2},{1,3},{2,0},{3,1},{4,6},{5,7},{6,4},{7,5},{8,10},{9,11},{10,... | collective-permute-start | bytes 884744 | tf_op jit(solution)/shard_map/ppermute | solution.py:302
  44.4 12.0 %copy-start.17 = (f32[48]{0:T(128)S(1)}, f32[48]{0:T(128)}, u32[]{:S(2)}) copy-start(f32[48]{0:T(128)} %broadcast_in_dim.17) | copy-start | bytes 580
  44.4 12.1 %copy-start.11 = (bf16[2,768,768]{2,1,0:T(8,128)(2,1)S(1)}, bf16[2,768,768]{2,1,0:T(8,128)(2,1)}, u32[]{:S(2)}) copy-start(bf16[2,768,768]{2,1,0:T(8,128)(2,1)} %query_key.5) | copy-start | bytes 7077892
  44.4 12.1 %copy-start.14 = (bf16[768,768]{1,0:T(8,128)(2,1)S(1)}, bf16[768,768]{1,0:T(8,128)(2,1)}, u32[]{:S(2)}) copy-start(bf16[768,768]{1,0:T(8,128)(2,1)} %output_w.5) | copy-start | bytes 3538948
  49.1 7.3 %copy-start.13 = (bf16[768,768]{1,0:T(8,128)(2,1)S(1)}, bf16[768,768]{1,0:T(8,128)(2,1)}, u32[]{:S(2)}) copy-start(bf16[768,768]{1,0:T(8,128)(2,1)} %value_w.5) | copy-start | bytes 3538948
  49.1 7.3 %copy-start.15 = (bf16[384,384]{1,0:T(8,128)(2,1)S(1)}, bf16[384,384]{1,0:T(8,128)(2,1)}, u32[]{:S(2)}) copy-start(bf16[384,384]{1,0:T(8,128)(2,1)} %constant.9.clone.scatter_ref) | copy-start | bytes 884740
  49.1 7.3 %copy-start.16 = (bf16[384,384]{1,0:T(8,128)(2,1)S(1)}, bf16[384,384]{1,0:T(8,128)(2,1)}, u32[]{:S(2)}) copy-start(bf16[384,384]{1,0:T(8,128)(2,1)} %constant.8.clone.gather_ref) | copy-start | bytes 884740
  49.2 7.2 %collective-permute-start.3 = (bf16[3,96,768]{2,1,0:T(8,128)(2,1)S(1)}, bf16[3,96,768]{2,1,0:T(8,128)(2,1)S(1)}, u32[]{:S(2)}, u32[]{:S(2)}) collective-permute-start(bf16[3,96,768]{2,1,0:T(8,128)(2,1)S(1)} %slice_bitcast_fusion), channel_id=1, source_target_pairs={{0,1},{1,0},{2,3},{3,2},{4,5},{5,4},{6,7},{7,6},{8,9},{9,8},{10,11... | collective-permute-start | bytes 1327112 | tf_op jit(solution)/shard_map/ppermute | solution.py:299
  52.0 4.4 %collective-permute-start.6 = (bf16[96,768]{1,0:T(8,128)(2,1)S(1)}, bf16[96,768]{1,0:T(8,128)(2,1)S(1)}, u32[]{:S(2)}, u32[]{:S(2)}) collective-permute-start(bf16[96,768]{1,0:T(8,128)(2,1)S(1)} %slice_bitcast_fusion.2), channel_id=1, source_target_pairs={{0,1},{1,0},{2,3},{3,2},{4,5},{5,4},{6,7},{7,6},{8,9},{9,8},{10,11... | collective-permute-start | bytes 442376 | tf_op jit(solution)/shard_map/ppermute | solution.py:303
  52.4 19.1 %collective-permute-start.4 = (bf16[96,768]{1,0:T(8,128)(2,1)S(1)}, bf16[96,768]{1,0:T(8,128)(2,1)S(1)}, u32[]{:S(2)}, u32[]{:S(2)}) collective-permute-start(bf16[96,768]{1,0:T(8,128)(2,1)S(1)} %slice_bitcast_fusion.3), channel_id=1, source_target_pairs={{0,1},{1,0},{2,3},{3,2},{4,5},{5,4},{6,7},{7,6},{8,9},{9,8},{10,11... | collective-permute-start | bytes 442376 | tf_op jit(solution)/shard_map/ppermute | solution.py:303
  54.1 32.0 %collective-permute-start.8 = (bf16[96,768]{1,0:T(8,128)(2,1)S(1)}, bf16[96,768]{1,0:T(8,128)(2,1)S(1)}, u32[]{:S(2)}, u32[]{:S(2)}) collective-permute-start(bf16[96,768]{1,0:T(8,128)(2,1)S(1)} %slice_bitcast_fusion.1), channel_id=1, source_target_pairs={{0,1},{1,0},{2,3},{3,2},{4,5},{5,4},{6,7},{7,6},{8,9},{9,8},{10,11... | collective-permute-start | bytes 442376 | tf_op jit(solution)/shard_map/ppermute | solution.py:303
  71.4 28.8 %collective-permute-start.10 = (bf16[2,96,768]{2,1,0:T(8,128)(2,1)S(1)}, bf16[2,96,768]{2,1,0:T(8,128)(2,1)S(1)}, u32[]{:S(2)}, u32[]{:S(2)}) collective-permute-start(bf16[2,96,768]{2,1,0:T(8,128)(2,1)S(1)} %get-tuple-element.22), channel_id=1, source_target_pairs={{0,1},{1,0},{2,3},{3,2},{4,5},{5,4},{6,7},{7,6},{8,9},{9,8},{10,11... | collective-permute-start | bytes 884744 | tf_op jit(solution)/shard_map/ppermute | solution.py:307
  85.5 15.2 %collective-permute-start.9 = (bf16[2,96,768]{2,1,0:T(8,128)(2,1)S(1)}, bf16[2,96,768]{2,1,0:T(8,128)(2,1)S(1)}, u32[]{:S(2)}, u32[]{:S(2)}) collective-permute-start(bf16[2,96,768]{2,1,0:T(8,128)(2,1)S(1)} %get-tuple-element.21), channel_id=1, source_target_pairs={{0,1},{1,0},{2,3},{3,2},{4,5},{5,4},{6,7},{7,6},{8,9},{9,8},{10,11... | collective-permute-start | bytes 884744 | tf_op jit(solution)/shard_map/ppermute | solution.py:307
  100.1 3.4 %collective-permute-start.11 = (bf16[2,96,768]{2,1,0:T(8,128)(2,1)S(1)}, bf16[2,96,768]{2,1,0:T(8,128)(2,1)S(1)}, u32[]{:S(2)}, u32[]{:S(2)}) collective-permute-start(bf16[2,96,768]{2,1,0:T(8,128)(2,1)S(1)} %get-tuple-element.23), channel_id=1, source_target_pairs={{0,1},{1,0},{2,3},{3,2},{4,5},{5,4},{6,7},{7,6},{8,9},{9,8},{10,11... | collective-permute-start | bytes 884744 | tf_op jit(solution)/shard_map/ppermute | solution.py:307
  100.3 9.7 %collective-permute-start.13 = (bf16[2,96,768]{2,1,0:T(8,128)(2,1)S(1)}, bf16[2,96,768]{2,1,0:T(8,128)(2,1)S(1)}, u32[]{:S(2)}, u32[]{:S(2)}) collective-permute-start(bf16[2,96,768]{2,1,0:T(8,128)(2,1)S(1)} %pad_maximum_fusion.1), channel_id=1, source_target_pairs={{0,2},{1,3},{2,0},{3,1},{4,6},{5,7},{6,4},{7,5},{8,10},{9,11},{10,... | collective-permute-start | bytes 884744 | tf_op jit(solution)/shard_map/ppermute | solution.py:309
  100.7 15.5 %collective-permute-start.12 = (bf16[2,96,768]{2,1,0:T(8,128)(2,1)S(1)}, bf16[2,96,768]{2,1,0:T(8,128)(2,1)S(1)}, u32[]{:S(2)}, u32[]{:S(2)}) collective-permute-start(bf16[2,96,768]{2,1,0:T(8,128)(2,1)S(1)} %pad_maximum_fusion), channel_id=1, source_target_pairs={{0,2},{1,3},{2,0},{3,1},{4,6},{5,7},{6,4},{7,5},{8,10},{9,11},{10,... | collective-permute-start | bytes 884744 | tf_op jit(solution)/shard_map/ppermute | solution.py:309
  103.5 19.1 %collective-permute-start.14 = (bf16[2,96,768]{2,1,0:T(8,128)(2,1)S(1)}, bf16[2,96,768]{2,1,0:T(8,128)(2,1)S(1)}, u32[]{:S(2)}, u32[]{:S(2)}) collective-permute-start(bf16[2,96,768]{2,1,0:T(8,128)(2,1)S(1)} %pad_maximum_fusion.2), channel_id=1, source_target_pairs={{0,2},{1,3},{2,0},{3,1},{4,6},{5,7},{6,4},{7,5},{8,10},{9,11},{10,... | collective-permute-start | bytes 884744 | tf_op jit(solution)/shard_map/ppermute | solution.py:309
  (1 other events, 1.2 us)

commit v2 on v0

v2 whole, which is shorter than its diff:
```python
import functools

import jax
import jax.numpy as jnp
from jax import lax
from jax.experimental import pallas as pl
from jax.experimental.pallas import tpu as pltpu
from jax.sharding import PartitionSpec as P

HEAD = 64
EPSILON = 1e-06
MASKED = -1e30
GROUP = 8
LANES = 128
HALF = GROUP // 2
F32, BF16 = jnp.float32, jnp.bfloat16
WHOLE = pl.BlockSpec(memory_space=pltpu.VMEM)
SCALARS = pl.BlockSpec(memory_space=pltpu.SMEM)
OUTSIDE = pl.BlockSpec(memory_space=pltpu.HBM)


def array(*shape, dtype=BF16):
    return jax.ShapeDtypeStruct(shape, dtype)


def params(mib=24):
    return pltpu.CompilerParams(vmem_limit_bytes=mib << 20)


def cost():
    return pl.CostEstimate(flops=1, bytes_accessed=1, transcendentals=0)


def normalize(x):
    return x * lax.rsqrt(jnp.mean(x * x, axis=-1, keepdims=True) + EPSILON)


def matmul(x, weight):
    return jnp.dot(x, weight, preferred_element_type=F32)


def place():
    here = lax.axis_index("level")
    return here // 2, here % 2


def chunk_of(x, chunk):
    first, middle, last = (x[:, GROUP * i : GROUP * (i + 1)] for i in range(3))
    if chunk == 0:
        return middle
    low = lax.broadcasted_iota(jnp.int32, first.shape, 1) < HALF
    return jnp.where(low, last, first) if chunk == 1 else jnp.where(low, first, last)


def whole_of(middle, beside, outer):
    low = lax.broadcasted_iota(jnp.int32, middle.shape, 1) < HALF
    return jnp.concatenate([jnp.where(low, outer, beside), middle, jnp.where(low, beside, outer)], axis=1)


def rows_of(ref, row, chunk, levels):
    lon = ref.shape[-2] // levels
    x = chunk_of(ref[row].astype(F32).reshape(levels, lon, ref.shape[-1]), chunk)
    return x.reshape(levels * GROUP, ref.shape[-1])


def update_pieces(pieces, levels, halves, target_w, node_w, bias_ref, edges, target_ref, sum_ref):
    chip, core = place()
    width = bias_ref.shape[-1]
    size = levels * GROUP
    lon = halves[0][0].shape[1] // levels
    side = [jnp.where(chip == (1 if far else 0), 0, 1) for far in (False, True)]
    x = [rows_of(halves[h][0], core + side[far], c, levels).astype(BF16) for far, c, h in pieces]
    target_ref[...] = matmul(jnp.concatenate(x, axis=0), target_w[...]) * 0.5
    step = LANES
    for n, (far, c, h) in enumerate(pieces):
        source_ref = halves[h][1]
        row = core + side[far]
        lat = core + row
        north, south = jnp.maximum(row - 1, 0), jnp.minimum(row + 1, 2)
        has_north = jnp.where(lat >= 1, 1.0, 0.0)
        has_south = jnp.where(lat <= 2, 1.0, 0.0)
        if c == 2:
            west_edge = edges[0][2 * h + side[far]].astype(F32)
            east_edge = edges[1][2 * h + side[far]].astype(F32)
        for pair in range(levels // 2):
            for lane in range(0, width, step):
                cols = slice(lane, lane + step)
                rows = slice(2 * lon * pair, 2 * lon * (pair + 1))
                at = slice(n * size + 2 * GROUP * pair, n * size + 2 * GROUP * (pair + 1))

                def take(x):
                    return chunk_of(x.reshape(2, lon, step), c).reshape(2 * GROUP, step)

                def put(x, place, edge):
                    place = lax.broadcasted_iota(jnp.int32, (GROUP, step), 0) == place
                    parts = [
                        jnp.where(place, edge[2 * pair + k : 2 * pair + k + 1, cols], x[GROUP * k : GROUP * (k + 1)])
                        for k in range(2)
                    ]
                    return jnp.concatenate(parts, axis=0)

                middle = source_ref[row, rows, cols].astype(F32)
                east = take(pltpu.roll(middle, 2 * lon - 1, 0))
                west = take(pltpu.roll(middle, 1, 0))
                if c == 2:
                    west = put(west, 0, west_edge)
                    east = put(east, GROUP - 1, east_edge)
                target = target_ref[at, cols]

                def halved_silu(other, k):
                    half = target + other + bias_ref[k : k + 1, cols]
                    return half + half * jnp.tanh(half)

                total = halved_silu(east, 0) + halved_silu(west, 1)
                other = take(source_ref[north, rows, cols].astype(F32))
                total = total + halved_silu(other, 2) * has_north
                other = take(source_ref[south, rows, cols].astype(F32))
                total = total + halved_silu(other, 3) * has_south
                sum_ref[at, cols] = total.astype(BF16)
    update = matmul(sum_ref[...], node_w[...])
    out = []
    for n, (far, c, h) in enumerate(pieces):
        nodes_ref, offset = halves[h][2:]
        own = rows_of(nodes_ref, offset + side[far], c, levels)
        out.append((own + update[n * size : (n + 1) * size]).astype(BF16))
    return out


def source_rows(read, normed_ref, source_ref, source_w):
    count, rows, _ = normed_ref.shape
    for i in range(count):
        normed_ref[i] = normalize(read(i).astype(F32)).astype(BF16)
    normed = jnp.concatenate([normed_ref[i] for i in range(count)], axis=0)
    source = (matmul(normed, source_w[...]) * 0.5).astype(BF16)
    for i in range(count):
        source_ref[i] = source[i * rows : (i + 1) * rows]


def first_kernel(nodes_in, source_in, nodes_ref, source_w, normed_ref, source_ref, sems):
    count = nodes_ref.shape[0]
    _, core = place()
    copies = [pltpu.make_async_copy(nodes_in.at[core + i], nodes_ref.at[i], sems.at[i]) for i in range(count)]
    copies.append(pltpu.make_async_copy(source_in, source_w, sems.at[count]))
    for copy in copies:
        copy.start()
    for copy in copies:
        copy.wait()
    source_rows(lambda i: nodes_ref[i], normed_ref, source_ref, source_w)


def outside(*arrays):
    return [pltpu.with_memory_space_constraint(x, pltpu.HBM) for x in arrays]


def first(nodes, source_w):
    lat, rows, width = nodes.shape
    three, square = array(3, rows, width), array(width, width)
    return pl.pallas_call(
        first_kernel,
        in_specs=[OUTSIDE] * 2,
        out_specs=[WHOLE] * 4,
        out_shape=[three, square, three, three],
        scratch_shapes=[pltpu.SemaphoreType.DMA((4,))],
        compiler_params=params(),
        cost_estimate=cost(),
    )(*outside(nodes, source_w))


def second_kernel(
    pieces, levels, target_in, node_in, bias_in, nodes_a, source_w, normed_a, source_a, nodes_b,
    target_w, node_w, bias_ref, normed_ref, source_ref, far_ref, target_ref, sum_ref, sems,
):
    _, core = place()
    copies = [
        pltpu.make_async_copy(*refs, sems.at[i])
        for i, refs in enumerate(((target_in, target_w), (node_in, node_w), (bias_in, bias_ref)))
    ]
    for copy in copies:
        copy.start()
    source_rows(lambda i: nodes_b[core + i], normed_ref, source_ref, source_w)
    for copy in copies:
        copy.wait()
    bias_ref[...] = bias_ref[...] * 0.5
    halves = ((normed_a, source_a, nodes_a, core), (normed_ref, source_ref, nodes_b, 2 * core))
    out = update_pieces(pieces, levels, halves, target_w, node_w, bias_ref, None, target_ref, sum_ref)
    far_ref[0], far_ref[1] = out


def second(levels, pieces, target_w, node_w, bias, *args):
    width = target_w.shape[0]
    three, square = array(*args[0].shape), array(width, width)
    size = levels * GROUP
    count = len(pieces) * size
    return pl.pallas_call(
        functools.partial(second_kernel, pieces, levels),
        in_specs=[OUTSIDE] * 3 + [WHOLE] * len(args),
        out_specs=[WHOLE] * 6,
        out_shape=[square, square, array(*bias.shape, dtype=F32), three, three, array(2, size, width)],
        scratch_shapes=[
            pltpu.VMEM((count, width), F32),
            pltpu.VMEM((count, width), BF16),
            pltpu.SemaphoreType.DMA((3,)),
        ],
        compiler_params=params(),
        cost_estimate=cost(),
    )(*outside(target_w, node_w, bias), *args)


def later_kernel(pieces, levels, with_edges, *refs):
    nodes_a, normed_a, source_a, nodes_b, normed_b, source_b, target_w, node_w, bias_ref = refs[:9]
    refs = refs[9:]
    _, core = place()
    edges = None
    if with_edges == "in":
        edges, refs = refs[:2], refs[2:]
    *outs, target_ref, sum_ref = refs
    if with_edges == "out":
        *outs, west_ref, east_ref, target_ref, sum_ref, edge_ref = refs
        lon = source_a.shape[1] // levels
        for h, source_ref in enumerate((source_a, source_b)):
            for k in range(2):
                source = source_ref[core + k].astype(F32)
                for level in range(levels):
                    edge_ref[0, level : level + 1] = source[level * lon : level * lon + 1]
                    edge_ref[1, level : level + 1] = source[(level + 1) * lon - 1 : (level + 1) * lon]
                east_ref[2 * h + k] = edge_ref[0].astype(BF16)
                west_ref[2 * h + k] = edge_ref[1].astype(BF16)
    halves = ((normed_a, source_a, nodes_a, core), (normed_b, source_b, nodes_b, 2 * core))
    out = update_pieces(pieces, levels, halves, target_w, node_w, bias_ref, edges, target_ref, sum_ref)
    for i, ref in enumerate(outs):
        ref[0], ref[1] = out[2 * i : 2 * i + 2]


def later(levels, pieces, shared, edges=None, with_edges=None):
    width = shared[0].shape[-1]
    size = levels * GROUP
    count = len(pieces) * size
    args = (*shared, *(edges or ()))
    shapes = [array(2, size, width)] * (len(pieces) // 2)
    scratch = [pltpu.VMEM((count, width), F32), pltpu.VMEM((count, width), BF16)]
    if with_edges == "out":
        shapes += [array(4, levels, width)] * 2
        scratch += [pltpu.VMEM((2, levels, width), F32)]
    return pl.pallas_call(
        functools.partial(later_kernel, pieces, levels, with_edges),
        in_specs=[WHOLE] * len(args),
        out_specs=[WHOLE] * len(shapes),
        out_shape=shapes,
        scratch_shapes=scratch,
        compiler_params=params(),
        cost_estimate=cost(),
    )(*args)


def attention_kernel(
    mask_ref, own_ref, opposite_ref, query_key, value_w, output_w,
    out_own, out_sibling, out_opposite, q_ref, k_ref, v_ref, att_ref, weight_ref, bias_ref,
):
    _, size, width = own_ref.shape
    here = lax.axis_index("level")
    levels = 4 * size // GROUP
    each = levels // 4
    tiles = width // LANES
    for q in range(4):
        for level in range(each):
            kept = jnp.where(mask_ref[(here ^ q) * each + level] > 0, 0.0, MASKED).astype(F32)
            bias_ref[q * each + level : q * each + level + 1] = jnp.full((1, LANES), kept)
    x = jnp.concatenate([own_ref[0], own_ref[1], opposite_ref[0], opposite_ref[1]], axis=0)
    normed = normalize(x.astype(F32)).astype(BF16)

    def spread(ref, y):
        for t in range(tiles):
            ref[t] = y[:, LANES * t : LANES * (t + 1)]

    spread(q_ref, matmul(normed, query_key[0]) * HEAD**-0.5)
    spread(k_ref, matmul(normed, query_key[1]))
    spread(v_ref, matmul(normed, value_w[...]))
    low = lax.broadcasted_iota(jnp.int32, (levels, LANES), 1) < HEAD
    pad = jnp.zeros((LANES - 2 * levels, LANES), BF16)
    bias = bias_ref[...]
    for column in range(GROUP):
        rows = pl.ds(column, levels, stride=GROUP)
        for t in range(tiles):
            query, key = q_ref[t, rows, :].astype(BF16), k_ref[t, rows, :].astype(BF16)
            zero = jnp.zeros_like(query)
            both = jnp.concatenate([jnp.where(low, query, zero), jnp.where(low, zero, query), pad], axis=0)
            scores = lax.dot_general(key, both, (((1,), (1,)), ((), ())), preferred_element_type=F32)
            scores = scores + bias
            weights = jnp.exp(scores - jnp.max(scores, axis=0, keepdims=True))
            weights = weights * (1.0 / jnp.sum(weights, axis=0, keepdims=True))
            weight_ref[levels * column : levels * (column + 1), LANES * t : LANES * (t + 1)] = weights.astype(BF16)
    for column in range(GROUP):
        rows = pl.ds(column, levels, stride=GROUP)
        for t in range(tiles):
            weights = weight_ref[levels * column : levels * (column + 1), LANES * t : LANES * (t + 1)]
            value = v_ref[t, rows, :].astype(BF16)
            mixed = lax.dot_general(weights, value, (((0,), (0,)), ((), ())), preferred_element_type=F32)
            att_ref[t, rows, :] = jnp.where(low, mixed[:levels], mixed[levels : 2 * levels])
    attended = jnp.concatenate([att_ref[t] for t in range(tiles)], axis=1).astype(BF16)
    out = (x.astype(F32) + matmul(attended, output_w[...])).astype(BF16)
    out_own[...] = out[:size]
    out_sibling[...] = out[size : 2 * size]
    out_opposite[0] = out[2 * size : 3 * size]
    out_opposite[1] = out[3 * size :]


def attention(*args):
    _, size, width = args[1].shape
    rows = 4 * size
    tiled = pltpu.VMEM((width // LANES, rows, LANES), F32)
    return pl.pallas_call(
        attention_kernel,
        in_specs=[SCALARS] + [WHOLE] * (len(args) - 1),
        out_specs=[WHOLE] * 3,
        out_shape=[array(size, width), array(size, width), array(2, size, width)],
        scratch_shapes=[tiled] * 4 + [pltpu.VMEM((rows, width), BF16), pltpu.VMEM((rows // GROUP, LANES), F32)],
        compiler_params=params(),
        cost_estimate=cost(),
    )(*args)


def finish_kernel(levels, targets, given, *refs):
    *pieces, out_ref, whole_ref, sems = refs[given:]
    chip, core = place()
    width = out_ref.shape[-1]
    lon = 3 * GROUP
    copies = []
    for n, (far, other) in enumerate(targets):
        for pair in range(levels // 2):
            rows = slice(2 * GROUP * pair, 2 * GROUP * (pair + 1))
            parts = [p[0][rows] if len(p.shape) == 3 else p[rows] for p in pieces[3 * n : 3 * n + 3]]
            whole = whole_of(*(p.astype(F32).reshape(2, GROUP, width) for p in parts))
            whole_ref[n, 2 * lon * pair : 2 * lon * (pair + 1)] = whole.reshape(2 * lon, width).astype(BF16)
        row = 2 * (1 - core if other else core) + (1 - chip if far else chip)
        copies.append(pltpu.make_async_copy(whole_ref.at[n], out_ref.at[row], sems.at[n]))
        copies[-1].start()
    for copy in copies:
        copy.wait()


def finish(levels, targets, shape, given, pieces):
    count = len(targets)
    return pl.pallas_call(
        functools.partial(finish_kernel, levels, targets, len(given)),
        in_specs=[OUTSIDE] * len(given) + [WHOLE] * len(pieces),
        out_specs=OUTSIDE,
        out_shape=array(*shape),
        input_output_aliases={0: 0} if given else {},
        scratch_shapes=[pltpu.VMEM((count, *shape[1:]), BF16), pltpu.SemaphoreType.DMA((count,))],
        compiler_params=params(),
        cost_estimate=cost(),
    )(*given, *pieces)


def after(x, *others):
    return lax.optimization_barrier((x, *others))[0]


def per_device(
    nodes, level_mask, source_weight, target_weight, direction_bias, node_weight, query_key, value_weight, output_weight
):
    lat, lon, levels, width = nodes.shape
    rows = levels * lon
    opposite = [(i, i ^ 2) for i in range(4)]
    sibling = [(i, i ^ 1) for i in range(4)]
    ring = lax.axis_size("sector")
    up = [(i, (i + 1) % ring) for i in range(ring)]
    down = [(j, i) for i, j in up]
    far_piece = lambda c: ((True, c, 0), (True, c, 1))
    own_piece = lambda c: ((False, c, 0), (False, c, 1))

    nodes = jnp.transpose(nodes, (0, 2, 1, 3)).reshape(lat, rows, width)
    nodes_b = lax.ppermute(nodes, "level", sibling)
    far, own = {}, {}
    nodes_a, source_w, normed_a, source_a = first(nodes, source_weight)
    target_w, node_w, bias, normed_b, source_b, far[0] = second(
        levels, far_piece(0), target_weight, node_weight, direction_bias, nodes_a, source_w, normed_a, source_a, nodes_b
    )
    shared = (nodes_a, normed_a, source_a, nodes_b, normed_b, source_b, target_w, node_w, bias)
    far[1], own[0], west, east = later(levels, far_piece(1) + own_piece(0), shared, with_edges="out")
    west = lax.ppermute(west, "sector", up)
    east = lax.ppermute(east, "sector", down)
    (own[1],) = later(levels, own_piece(1), (after(nodes_a, own[0]), *shared[1:]))
    far[2], own[2] = later(levels, far_piece(2) + own_piece(2), (after(nodes_a, own[1]), *shared[1:]), (west, east), "in")
    done, close, back, distant = {}, {}, {}, {}
    for c in range(3):
        arrived = lax.ppermute(far[c], "level", opposite)
        mine = own[0] if c == 0 else after(own[c], done[c - 1], *([back[0]] if c == 2 else []))
        args = (level_mask, mine, arrived, query_key, value_weight, output_weight)
        done[c], close[c], toward = attention(*args)
        back[c] = lax.ppermute(toward, "level", opposite)
    late = lambda x: after(x, done[2])
    close = {c: lax.ppermute(late(close[c]), "level", sibling) for c in range(3)}
    for c in range(2):
        distant[c] = lax.ppermute(late(back[c][1]), "level", sibling)
    shape = (lat, rows, width)
    listed = lambda d: [d[c] for c in range(3)]
    out = finish(levels, ((False, False), (False, True)), shape, (), listed(done) + listed(close))
    back[2] = after(back[2], out)
    distant[2] = lax.ppermute(back[2][1], "level", sibling)
    out = finish(levels, ((True, False),), shape, (out,), listed(back))
    out = finish(levels, ((True, True),), shape, (out,), listed(distant))
    return jnp.transpose(out.reshape(lat, levels, lon, width), (0, 2, 1, 3))


def solution(mesh):
    placed = (P(None, "sector", "level", None), P(), P(), P(), P(), P(), P(), P(), P())
    return jax.shard_map(
        per_device,
        mesh=mesh,
        in_specs=placed,
        out_specs=P(None, "sector", "level", None),
        check_vma=False,
    )
```

time: 219 us -> 65.5 us (0.30)
  matrix products: 72.3 us -> 0 us
  local copies, waits for them, and re-layouts: 59.4 us -> 0.85 us
  waiting for transfers between devices: 51.8 us -> 4.38 us
  Pallas kernels: 0 us -> 30.5 us
  starting transfers between devices: 10 us -> 29.3 us
  between operations: 13.5 us -> 0.32 us
  other arithmetic: 10.3 us -> 0 us
    dot_general x8 -> x0, matrix products: 72.3 us -> none  [the longest x6 32.5 us: project(): product = jnp.dot(flattened, weight, preferred_element_type=jnp.float32)]
    all_gather x2 -> x0, waiting for transfers between devices: 50 us -> none  [the longest x1 44.7 us: per_device(): lax.all_gather(keys_local, 'level', axis=2, tiled=True)]
    reshape x3 -> x0, local copies, waits for them, and re-layouts: 48.4 us -> none  [head_split(): return inputs.reshape(inputs.shape[:-1] + (inputs.shape[-1] // HEAD, HEAD))]
    pallas_call x0 -> x11, Pallas kernels: none -> 30.5 us  [the longest x3 13.2 us: attention(): pl.pallas_call(attention_kernel, in_specs=[SCALARS] + [WHOLE] * (len(args...]
    ppermute x2 -> x15, starting transfers between devices: 9.78 us -> 29.3 us  [the longest x1 6.76 us: per_device(): east = lax.ppermute(east, 'sector', down)]
    reduce_sum x2 -> x0, other arithmetic: 10.2 us -> none  [the longest x1 8.23 us: per_device(): denominator = jnp.sum(weights, axis=-1)]
    dot_general x1 -> x0, local copies, waits for them, and re-layouts: 5.63 us -> none  [project(): product = jnp.dot(flattened, weight, preferred_element_type=jnp.float32)]
    convert_element_type x1 -> x0, local copies, waits for them, and re-layouts: 3.37 us -> none  [per_device(): (numerator / denominator[..., None]).astype(jnp.bfloat16)]
  transfers between devices with their start and end apart: 4 -> 15, of which waited for: 3 -> 5; matrix products, arithmetic and copies ran while one was open for 31% -> 0% of each run, Pallas kernels for 0% -> 39%
where the time goes in v2:
time: 65.5 us; the launch traced here: 65.3 us
  Pallas kernels  30.5 us (47%)
  starting transfers between devices  29.3 us (45%)
  waiting for transfers between devices  4.38 us (7%)
  local copies, waits for them, and re-layouts  0.85 us (1%)
    pallas_call x3, Pallas kernels, attention(): pl.pallas_call(attention_kernel, in_specs=[SCALARS] + [WHOLE] * (len(args...  13.2 us
    pallas_call x3, Pallas kernels, later(): pl.pallas_call(functools.partial(later_kernel, pieces, levels, with_edges...  7.33 us
    ppermute x1, starting transfers between devices, per_device(): east = lax.ppermute(east, 'sector', down)  6.76 us
    ppermute x3, starting transfers between devices, per_device(): back[c] = lax.ppermute(toward, 'level', opposite)  4.87 us
    ppermute x3, starting transfers between devices, per_device(): arrived = lax.ppermute(far[c], 'level', opposite)  4.48 us
    pallas_call x1, Pallas kernels, second(): pl.pallas_call(functools.partial(second_kernel, pieces, levels), in_specs...  4.24 us
    ppermute x3, starting transfers between devices, per_device(): lax.ppermute(late(close[c]), 'level', sibling)  4.13 us
    ppermute x1, starting transfers between devices, per_device(): distant[2] = lax.ppermute(back[2][1], 'level', sibling)  3.77 us
  transfers between devices with their start and end apart: 15, of which 5 were waited for; matrix products, arithmetic and copies ran while one was open for 0% of the time, Pallas kernels for 39%

profile of v2, /device:TPU:1, one launch (start us, length us, event | category | flops | bytes accessed | tf_op | source)
XLA Modules:
  0.0 65.3 jit_solution(13050483188526631266)
XLA Ops:
  0.0 3.2 %collective-permute-start = (bf16[4,288,768]{2,1,0:T(8,128)(2,1)}, bf16[4,288,768]{2,1,0:T(8,128)(2,1)S(1)}, u32[]{:S(2)}, u32[]{:S(2)}) collective-permute-start(bf16[4,288,768]{2,1,0:T(8,128)(2,1)} %bitcast.12), channel_id=1, source_target_pairs={{0,1},{1,0},{2,3},{3,2},{4,5},{5,4},{6,7},{7,6},{8,9},{9,8},{10,11... | collective-permute-start | bytes 5308424 | tf_op jit(solution)/shard_map/ppermute | solution.py:373
  3.2 3.1 %shard_map.91 = (bf16[3,288,768]{2,1,0:T(8,128)(2,1)S(1)}, bf16[768,768]{1,0:T(8,128)(2,1)S(1)}, bf16[3,288,768]{2,1,0:T(8,128)(2,1)S(1)}, bf16[3,288,768]{2,1,0:T(8,128)(2,1)S(1)}) custom-call(bf16[4,288,768]{2,1,0:T(8,128)(2,1)} %bitcast.13, bf16[768,768]{1,0:T(8,128)(2,1)} %source_in.1), custom_call_target="tpu_custom_call" | custom-call | flops 1 | bytes 1 | tf_op jit(solution)/shard_map/pallas_call | solution.py:158
  6.4 0.4 collective-permute-done.nodes_b.refs_3_
  6.8 4.2 %shard_map.92 = (bf16[768,768]{1,0:T(8,128)(2,1)S(1)}, bf16[768,768]{1,0:T(8,128)(2,1)S(1)}, f32[4,768]{1,0:T(4,128)S(1)}, bf16[3,288,768]{2,1,0:T(8,128)(2,1)S(...) custom-call(bf16[768,768]{1,0:T(8,128)(2,1)} %target_in.1, bf16[768,768]{1,0:T(8,128)(2,1)} %node_in.1, ...), custom_call_target="tpu_custom_call" | custom-call | flops 1 | bytes 1 | tf_op jit(solution)/shard_map/pallas_call | solution.py:194
  11.0 1.3 %collective-permute-start.1 = (bf16[2,96,768]{2,1,0:T(8,128)(2,1)S(1)}, bf16[2,96,768]{2,1,0:T(8,128)(2,1)S(1)}, u32[]{:S(2)}, u32[]{:S(2)}) collective-permute-start(bf16[2,96,768]{2,1,0:T(8,128)(2,1)S(1)} %get-tuple-element.50), channel_id=1, source_target_pairs={{0,2},{1,3},{2,0},{3,1},{4,6},{5,7},{6,4},{7,5},{8,10},{9,11},{10,... | collective-permute-start | bytes 884744 | tf_op jit(solution)/shard_map/ppermute | solution.py:387
  12.3 2.8 %shard_map.93 = (bf16[2,96,768]{2,1,0:T(8,128)(2,1)S(1)}, bf16[2,96,768]{2,1,0:T(8,128)(2,1)S(1)}, bf16[4,12,768]{2,1,0:T(8,128)(2,1)S(1)}, bf16[4,12,768]{2,1,0:T(8,128)(2,1)S(1)}) custom-call(bf16[3,288,768]{2,1,0:T(8,128)(2,1)S(1)} %get-tuple-element.56.nodes_a.refs_0_, bf16[3,288,768]{2,1,0:T(8,128)(2,1)S(1)} %get-tuple-element.41.normed_a.refs_1_, ...), custom_call_target="tpu_custom_call" | custom-call | flops 1 | bytes 1 | tf_op jit(solution)/shard_map/pallas_call | solution.py:244
  15.1 1.3 %collective-permute-start.3 = (bf16[4,12,768]{2,1,0:T(8,128)(2,1)S(1)}, bf16[4,12,768]{2,1,0:T(8,128)(2,1)S(1)}, u32[]{:S(2)}, u32[]{:S(2)}) collective-permute-start(bf16[4,12,768]{2,1,0:T(8,128)(2,1)S(1)} %get-tuple-element.57), channel_id=1, source_target_pairs={{0,4},{4,8},{8,12},{12,16},{16,20},{20,24},{24,28},{28,32},{32,36}... | collective-permute-start | bytes 221192 | tf_op jit(solution)/shard_map/ppermute | solution.py:381
  16.4 6.8 %collective-permute-start.4 = (bf16[4,12,768]{2,1,0:T(8,128)(2,1)S(1)}, bf16[4,12,768]{2,1,0:T(8,128)(2,1)S(1)}, u32[]{:S(2)}, u32[]{:S(2)}) collective-permute-start(bf16[4,12,768]{2,1,0:T(8,128)(2,1)S(1)} %get-tuple-element.58), channel_id=1, source_target_pairs={{4,0},{8,4},{12,8},{16,12},{20,16},{24,20},{28,24},{32,28},{36,32}... | collective-permute-start | bytes 221192 | tf_op jit(solution)/shard_map/ppermute | solution.py:382
  23.2 1.6 %collective-permute-start.2 = (bf16[2,96,768]{2,1,0:T(8,128)(2,1)S(1)}, bf16[2,96,768]{2,1,0:T(8,128)(2,1)S(1)}, u32[]{:S(2)}, u32[]{:S(2)}) collective-permute-start(bf16[2,96,768]{2,1,0:T(8,128)(2,1)S(1)} %get-tuple-element.54), channel_id=1, source_target_pairs={{0,2},{1,3},{2,0},{3,1},{4,6},{5,7},{6,4},{7,5},{8,10},{9,11},{10,... | collective-permute-start | bytes 884744 | tf_op jit(solution)/shard_map/ppermute | solution.py:387
  24.7 1.5 %shard_map.95.own_ref = bf16[2,96,768]{2,1,0:T(8,128)(2,1)S(1)} custom-call(bf16[3,288,768]{2,1,0:T(8,128)(2,1)S(1)} %get-tuple-element.56.nodes_a.refs_0_, bf16[3,288,768]{2,1,0:T(8,128)(2,1)S(1)} %get-tuple-element.41.normed_a.refs_1_, bf16[3,288,768]{2,1,0:T(8,128)(2,1)S(1)} %get-tuple-element.42.source_a.refs_2_, ...), custom_call_target="tpu_custom_call" | custom-call | flops 1 | bytes 1 | tf_op jit(solution)/shard_map/pallas_call | solution.py:244
  26.3 0.1 copy-done
  26.4 0.3 copy-done.1
  26.7 0.4 copy-done.2
  27.1 4.4 %shard_map.94 = (bf16[96,768]{1,0:T(8,128)(2,1)S(1)}, bf16[96,768]{1,0:T(8,128)(2,1)S(1)}, bf16[2,96,768]{2,1,0:T(8,128)(2,1)S(1)}) custom-call(s32[48]{0:T(128)S(1)} %copy-done.3, bf16[2,96,768]{2,1,0:T(8,128)(2,1)S(1)} %get-tuple-element.49.own_ref, bf16[2,96,768]{2,1,0:T(8,128)(2,1)S(1)} %collective-permute-done.1.opposite_ref, ...), custom_call_target="tpu_custom_call" | custom-call | flops 1 | bytes 1 | tf_op jit(solution)/shard_map/pallas_call | solution.py:311
  31.5 1.5 %collective-permute-start.5 = (bf16[2,96,768]{2,1,0:T(8,128)(2,1)S(1)}, bf16[2,96,768]{2,1,0:T(8,128)(2,1)S(1)}, u32[]{:S(2)}, u32[]{:S(2)}) collective-permute-start(bf16[2,96,768]{2,1,0:T(8,128)(2,1)S(1)} %get-tuple-element.60), channel_id=1, source_target_pairs={{0,2},{1,3},{2,0},{3,1},{4,6},{5,7},{6,4},{7,5},{8,10},{9,11},{10,... | collective-permute-start | bytes 884744 | tf_op jit(solution)/shard_map/ppermute | solution.py:391
  33.0 3.0 %shard_map.97 = (bf16[2,96,768]{2,1,0:T(8,128)(2,1)S(1)}, bf16[2,96,768]{2,1,0:T(8,128)(2,1)S(1)}) custom-call(bf16[3,288,768]{2,1,0:T(8,128)(2,1)S(1)} %get-tuple-element.56.nodes_a.refs_0_, bf16[3,288,768]{2,1,0:T(8,128)(2,1)S(1)} %get-tuple-element.41.normed_a.refs_1_, bf16[3,288,768]{2,1,0:T(8,128)(2,1)S(1)} %get-tuple-element.42.source_a.refs_2_, ...), custom_call_target="tpu_custom_call" | custom-call | flops 1 | bytes 1 | tf_op jit(solution)/shard_map/pallas_call | solution.py:244
  36.0 1.7 %collective-permute-start.6 = (bf16[2,96,768]{2,1,0:T(8,128)(2,1)S(1)}, bf16[2,96,768]{2,1,0:T(8,128)(2,1)S(1)}, u32[]{:S(2)}, u32[]{:S(2)}) collective-permute-start(bf16[2,96,768]{2,1,0:T(8,128)(2,1)S(1)} %get-tuple-element.62), channel_id=1, source_target_pairs={{0,2},{1,3},{2,0},{3,1},{4,6},{5,7},{6,4},{7,5},{8,10},{9,11},{10,... | collective-permute-start | bytes 884744 | tf_op jit(solution)/shard_map/ppermute | solution.py:387
  37.6 4.4 %shard_map.96 = (bf16[96,768]{1,0:T(8,128)(2,1)S(1)}, bf16[96,768]{1,0:T(8,128)(2,1)S(1)}, bf16[2,96,768]{2,1,0:T(8,128)(2,1)S(1)}) custom-call(s32[48]{0:T(128)S(1)} %copy-done.3, bf16[2,96,768]{2,1,0:T(8,128)(2,1)S(1)} %shard_map.95.own_ref, bf16[2,96,768]{2,1,0:T(8,128)(2,1)S(1)} %collective-permute-done.2.opposite_ref, bf16[2,768,768]{2,1,0:T(8,128)(2,1)S(1)} %copy-done, ...), custom_call_target="tpu_custom_call" | custom-call | flops 1 | bytes 1 | tf_op jit(solution)/shard_map/pallas_call | solution.py:311
  42.0 1.7 %collective-permute-start.10 = (bf16[2,96,768]{2,1,0:T(8,128)(2,1)S(1)}, bf16[2,96,768]{2,1,0:T(8,128)(2,1)S(1)}, u32[]{:S(2)}, u32[]{:S(2)}) collective-permute-start(bf16[2,96,768]{2,1,0:T(8,128)(2,1)S(1)} %get-tuple-element.70), channel_id=1, source_target_pairs={{0,2},{1,3},{2,0},{3,1},{4,6},{5,7},{6,4},{7,5},{8,10},{9,11},{10,... | collective-permute-start | bytes 884744 | tf_op jit(solution)/shard_map/ppermute | solution.py:391
  43.7 2.9 %collective-permute-done.6.opposite_ref = bf16[2,96,768]{2,1,0:T(8,128)(2,1)S(1)} collective-permute-done((bf16[2,96,768]{2,1,0:T(8,128)(2,1)S(1)}, bf16[2,96,768]{2,1,0:T(8,128)(2,1)S(1)}, u32[]{:S(2)}, u32[]{:S(2)}) %collective-permute-start.6) | collective-permute-done | bytes 294944 | tf_op jit(solution)/shard_map/ppermute | solution.py:387
  46.7 4.4 %shard_map.98 = (bf16[96,768]{1,0:T(8,128)(2,1)S(1)}, bf16[96,768]{1,0:T(8,128)(2,1)S(1)}, bf16[2,96,768]{2,1,0:T(8,128)(2,1)S(1)}) custom-call(s32[48]{0:T(128)S(1)} %copy-done.3, bf16[2,96,768]{2,1,0:T(8,128)(2,1)S(1)} %get-tuple-element.61.own_ref, bf16[2,96,768]{2,1,0:T(8,128)(2,1)S(1)} %collective-permute-done.6.opposite_ref, ...), custom_call_target="tpu_custom_call" | custom-call | flops 1 | bytes 1 | tf_op jit(solution)/shard_map/pallas_call | solution.py:311
  51.0 1.7 %collective-permute-start.11 = (bf16[2,96,768]{2,1,0:T(8,128)(2,1)S(1)}, bf16[2,96,768]{2,1,0:T(8,128)(2,1)S(1)}, u32[]{:S(2)}, u32[]{:S(2)}) collective-permute-start(bf16[2,96,768]{2,1,0:T(8,128)(2,1)S(1)} %get-tuple-element.71), channel_id=1, source_target_pairs={{0,2},{1,3},{2,0},{3,1},{4,6},{5,7},{6,4},{7,5},{8,10},{9,11},{10,... | collective-permute-start | bytes 884744 | tf_op jit(solution)/shard_map/ppermute | solution.py:391
  52.7 3.9 %collective-permute-start.7 = (bf16[96,768]{1,0:T(8,128)(2,1)S(1)}, bf16[96,768]{1,0:T(8,128)(2,1)S(1)}, u32[]{:S(2)}, u32[]{:S(2)}) collective-permute-start(bf16[96,768]{1,0:T(8,128)(2,1)S(1)} %get-tuple-element.65), channel_id=1, source_target_pairs={{0,1},{1,0},{2,3},{3,2},{4,5},{5,4},{6,7},{7,6},{8,9},{9,8},{10,11... | collective-permute-start | bytes 442376 | tf_op jit(solution)/shard_map/ppermute | solution.py:393
  56.8 0.4 collective-permute-start.12
  57.3 0.4 collective-permute-done.7.refs_3_
  57.7 0.4 collective-permute-start.13
  58.0 0.5 collective-permute-done.9.refs_5_
  58.5 1.0 %shard_map.99.refs_0_ = bf16[4,288,768]{2,1,0:T(8,128)(2,1)} custom-call(bf16[96,768]{1,0:T(8,128)(2,1)S(1)} %get-tuple-element.51.refs_0_, bf16[96,768]{1,0:T(8,128)(2,1)S(1)} %get-tuple-element.55.refs_1_, bf16[96,768]{1,0:T(8,128)(2,1)S(1)} %get-tuple-element.63.refs_2_, bf16[96,768]{1,0:T(8,128)(2,1)S(1)} %collective-permute-done.7.refs_3_, ...), custom_call_target="tpu_custom_call" | custom-call | flops 1 | bytes 1 | tf_op jit(solution)/shard_map/pallas_call | solution.py:343
  59.6 3.8 %collective-permute-start.14 = (bf16[96,768]{1,0:T(8,128)(2,1)S(1)}, bf16[96,768]{1,0:T(8,128)(2,1)S(1)}, u32[]{:S(2)}, u32[]{:S(2)}) collective-permute-start(bf16[96,768]{1,0:T(8,128)(2,1)S(1)} %slice_bitcast_fusion.2), channel_id=1, source_target_pairs={{0,1},{1,0},{2,3},{3,2},{4,5},{5,4},{6,7},{7,6},{8,9},{9,8},{10,11... | collective-permute-start | bytes 442376 | tf_op jit(solution)/shard_map/ppermute | solution.py:400
  63.3 0.8 %shard_map.100.refs_0_ = bf16[4,288,768]{2,1,0:T(8,128)(2,1)} custom-call(bf16[4,288,768]{2,1,0:T(8,128)(2,1)} %shard_map.99.refs_0_, bf16[2,96,768]{2,1,0:T(8,128)(2,1)S(1)} %collective-permute-done.5.refs_1_, bf16[2,96,768]{2,1,0:T(8,128)(2,1)S(1)} %collective-permute-done.10.refs_2_, ...), custom_call_target="tpu_custom_call", output_to_operand_aliasing={{}: (0, {})} | custom-call | flops 1 | bytes 1 | tf_op jit(solution)/shard_map/pallas_call | solution.py:343
  64.2 0.2 collective-permute-done.14.refs_3_
  64.3 0.8 %shard_map.101 = bf16[4,288,768]{2,1,0:T(8,128)(2,1)} custom-call(bf16[4,288,768]{2,1,0:T(8,128)(2,1)} %shard_map.100.refs_0_, bf16[96,768]{1,0:T(8,128)(2,1)S(1)} %collective-permute-done.12.refs_1_, bf16[96,768]{1,0:T(8,128)(2,1)S(1)} %collective-permute-done.13.refs_2_, ...), custom_call_target="tpu_custom_call", output_to_operand_aliasing={{}: (0, {})} | custom-call | flops 1 | bytes 1 | tf_op jit(solution)/shard_map/pallas_call | solution.py:343
  (20 shorter events, 0.3 us)
Async XLA Ops:
  0.0 6.8 %collective-permute-start = (bf16[4,288,768]{2,1,0:T(8,128)(2,1)}, bf16[4,288,768]{2,1,0:T(8,128)(2,1)S(1)}, u32[]{:S(2)}, u32[]{:S(2)}) collective-permute-start(bf16[4,288,768]{2,1,0:T(8,128)(2,1)} %bitcast.12), channel_id=1, source_target_pairs={{0,1},{1,0},{2,3},{3,2},{4,5},{5,4},{6,7},{7,6},{8,9},{9,8},{10,11... | collective-permute-start | bytes 5308424 | tf_op jit(solution)/shard_map/ppermute | solution.py:373
  11.0 15.2 %collective-permute-start.1 = (bf16[2,96,768]{2,1,0:T(8,128)(2,1)S(1)}, bf16[2,96,768]{2,1,0:T(8,128)(2,1)S(1)}, u32[]{:S(2)}, u32[]{:S(2)}) collective-permute-start(bf16[2,96,768]{2,1,0:T(8,128)(2,1)S(1)} %get-tuple-element.50), channel_id=1, source_target_pairs={{0,2},{1,3},{2,0},{3,1},{4,6},{5,7},{6,4},{7,5},{8,10},{9,11},{10,... | collective-permute-start | bytes 884744 | tf_op jit(solution)/shard_map/ppermute | solution.py:387
  15.1 17.8 %collective-permute-start.3 = (bf16[4,12,768]{2,1,0:T(8,128)(2,1)S(1)}, bf16[4,12,768]{2,1,0:T(8,128)(2,1)S(1)}, u32[]{:S(2)}, u32[]{:S(2)}) collective-permute-start(bf16[4,12,768]{2,1,0:T(8,128)(2,1)S(1)} %get-tuple-element.57), channel_id=1, source_target_pairs={{0,4},{4,8},{8,12},{12,16},{16,20},{20,24},{24,28},{28,32},{32,36}... | collective-permute-start | bytes 221192 | tf_op jit(solution)/shard_map/ppermute | solution.py:381
  16.4 16.6 %collective-permute-start.4 = (bf16[4,12,768]{2,1,0:T(8,128)(2,1)S(1)}, bf16[4,12,768]{2,1,0:T(8,128)(2,1)S(1)}, u32[]{:S(2)}, u32[]{:S(2)}) collective-permute-start(bf16[4,12,768]{2,1,0:T(8,128)(2,1)S(1)} %get-tuple-element.58), channel_id=1, source_target_pairs={{4,0},{8,4},{12,8},{16,12},{20,16},{24,20},{28,24},{32,28},{36,32}... | collective-permute-start | bytes 221192 | tf_op jit(solution)/shard_map/ppermute | solution.py:382
  23.2 14.5 %collective-permute-start.2 = (bf16[2,96,768]{2,1,0:T(8,128)(2,1)S(1)}, bf16[2,96,768]{2,1,0:T(8,128)(2,1)S(1)}, u32[]{:S(2)}, u32[]{:S(2)}) collective-permute-start(bf16[2,96,768]{2,1,0:T(8,128)(2,1)S(1)} %get-tuple-element.54), channel_id=1, source_target_pairs={{0,2},{1,3},{2,0},{3,1},{4,6},{5,7},{6,4},{7,5},{8,10},{9,11},{10,... | collective-permute-start | bytes 884744 | tf_op jit(solution)/shard_map/ppermute | solution.py:387
  24.7 1.7 %copy-start = (bf16[2,768,768]{2,1,0:T(8,128)(2,1)S(1)}, bf16[2,768,768]{2,1,0:T(8,128)(2,1)}, u32[]{:S(2)}) copy-start(bf16[2,768,768]{2,1,0:T(8,128)(2,1)} %query_key.5) | copy-start | bytes 7077892
  24.7 2.0 %copy-start.1 = (bf16[768,768]{1,0:T(8,128)(2,1)S(1)}, bf16[768,768]{1,0:T(8,128)(2,1)}, u32[]{:S(2)}) copy-start(bf16[768,768]{1,0:T(8,128)(2,1)} %value_w.5) | copy-start | bytes 3538948
  24.7 2.3 %copy-start.2 = (bf16[768,768]{1,0:T(8,128)(2,1)S(1)}, bf16[768,768]{1,0:T(8,128)(2,1)}, u32[]{:S(2)}) copy-start(bf16[768,768]{1,0:T(8,128)(2,1)} %output_w.5) | copy-start | bytes 3538948
  24.7 2.3 %copy-start.3 = (s32[48]{0:T(128)S(1)}, s32[48]{0:T(128)}, u32[]{:S(2)}) copy-start(s32[48]{0:T(128)} %mask_ref.5) | copy-start | bytes 580
  31.5 12.3 %collective-permute-start.5 = (bf16[2,96,768]{2,1,0:T(8,128)(2,1)S(1)}, bf16[2,96,768]{2,1,0:T(8,128)(2,1)S(1)}, u32[]{:S(2)}, u32[]{:S(2)}) collective-permute-start(bf16[2,96,768]{2,1,0:T(8,128)(2,1)S(1)} %get-tuple-element.60), channel_id=1, source_target_pairs={{0,2},{1,3},{2,0},{3,1},{4,6},{5,7},{6,4},{7,5},{8,10},{9,11},{10,... | collective-permute-start | bytes 884744 | tf_op jit(solution)/shard_map/ppermute | solution.py:391
  36.0 10.7 %collective-permute-start.6 = (bf16[2,96,768]{2,1,0:T(8,128)(2,1)S(1)}, bf16[2,96,768]{2,1,0:T(8,128)(2,1)S(1)}, u32[]{:S(2)}, u32[]{:S(2)}) collective-permute-start(bf16[2,96,768]{2,1,0:T(8,128)(2,1)S(1)} %get-tuple-element.62), channel_id=1, source_target_pairs={{0,2},{1,3},{2,0},{3,1},{4,6},{5,7},{6,4},{7,5},{8,10},{9,11},{10,... | collective-permute-start | bytes 884744 | tf_op jit(solution)/shard_map/ppermute | solution.py:387
  42.0 15.1 %collective-permute-start.10 = (bf16[2,96,768]{2,1,0:T(8,128)(2,1)S(1)}, bf16[2,96,768]{2,1,0:T(8,128)(2,1)S(1)}, u32[]{:S(2)}, u32[]{:S(2)}) collective-permute-start(bf16[2,96,768]{2,1,0:T(8,128)(2,1)S(1)} %get-tuple-element.70), channel_id=1, source_target_pairs={{0,2},{1,3},{2,0},{3,1},{4,6},{5,7},{6,4},{7,5},{8,10},{9,11},{10,... | collective-permute-start | bytes 884744 | tf_op jit(solution)/shard_map/ppermute | solution.py:391
  51.0 8.5 %collective-permute-start.11 = (bf16[2,96,768]{2,1,0:T(8,128)(2,1)S(1)}, bf16[2,96,768]{2,1,0:T(8,128)(2,1)S(1)}, u32[]{:S(2)}, u32[]{:S(2)}) collective-permute-start(bf16[2,96,768]{2,1,0:T(8,128)(2,1)S(1)} %get-tuple-element.71), channel_id=1, source_target_pairs={{0,2},{1,3},{2,0},{3,1},{4,6},{5,7},{6,4},{7,5},{8,10},{9,11},{10,... | collective-permute-start | bytes 884744 | tf_op jit(solution)/shard_map/ppermute | solution.py:391
  52.7 4.9 %collective-permute-start.7 = (bf16[96,768]{1,0:T(8,128)(2,1)S(1)}, bf16[96,768]{1,0:T(8,128)(2,1)S(1)}, u32[]{:S(2)}, u32[]{:S(2)}) collective-permute-start(bf16[96,768]{1,0:T(8,128)(2,1)S(1)} %get-tuple-element.65), channel_id=1, source_target_pairs={{0,1},{1,0},{2,3},{3,2},{4,5},{5,4},{6,7},{7,6},{8,9},{9,8},{10,11... | collective-permute-start | bytes 442376 | tf_op jit(solution)/shard_map/ppermute | solution.py:393
  56.7 1.4 %collective-permute-start.8 = (bf16[96,768]{1,0:T(8,128)(2,1)S(1)}, bf16[96,768]{1,0:T(8,128)(2,1)S(1)}, u32[]{:S(2)}, u32[]{:S(2)}) collective-permute-start(bf16[96,768]{1,0:T(8,128)(2,1)S(1)} %get-tuple-element.67), channel_id=1, source_target_pairs={{0,1},{1,0},{2,3},{3,2},{4,5},{5,4},{6,7},{7,6},{8,9},{9,8},{10,11... | collective-permute-start | bytes 442376 | tf_op jit(solution)/shard_map/ppermute | solution.py:393
  56.8 7.4 %collective-permute-start.12 = (bf16[96,768]{1,0:T(8,128)(2,1)S(1)}, bf16[96,768]{1,0:T(8,128)(2,1)S(1)}, u32[]{:S(2)}, u32[]{:S(2)}) collective-permute-start(bf16[96,768]{1,0:T(8,128)(2,1)S(1)} %slice_bitcast_fusion.1), channel_id=1, source_target_pairs={{0,1},{1,0},{2,3},{3,2},{4,5},{5,4},{6,7},{7,6},{8,9},{9,8},{10,11... | collective-permute-start | bytes 442376 | tf_op jit(solution)/shard_map/ppermute | solution.py:395
  57.2 1.4 %collective-permute-start.9 = (bf16[96,768]{1,0:T(8,128)(2,1)S(1)}, bf16[96,768]{1,0:T(8,128)(2,1)S(1)}, u32[]{:S(2)}, u32[]{:S(2)}) collective-permute-start(bf16[96,768]{1,0:T(8,128)(2,1)S(1)} %get-tuple-element.69), channel_id=1, source_target_pairs={{0,1},{1,0},{2,3},{3,2},{4,5},{5,4},{6,7},{7,6},{8,9},{9,8},{10,11... | collective-permute-start | bytes 442376 | tf_op jit(solution)/shard_map/ppermute | solution.py:393
  57.7 6.5 %collective-permute-start.13 = (bf16[96,768]{1,0:T(8,128)(2,1)S(1)}, bf16[96,768]{1,0:T(8,128)(2,1)S(1)}, u32[]{:S(2)}, u32[]{:S(2)}) collective-permute-start(bf16[96,768]{1,0:T(8,128)(2,1)S(1)} %slice_bitcast_fusion), channel_id=1, source_target_pairs={{0,1},{1,0},{2,3},{3,2},{4,5},{5,4},{6,7},{7,6},{8,9},{9,8},{10,11... | collective-permute-start | bytes 442376 | tf_op jit(solution)/shard_map/ppermute | solution.py:395
  59.6 4.8 %collective-permute-start.14 = (bf16[96,768]{1,0:T(8,128)(2,1)S(1)}, bf16[96,768]{1,0:T(8,128)(2,1)S(1)}, u32[]{:S(2)}, u32[]{:S(2)}) collective-permute-start(bf16[96,768]{1,0:T(8,128)(2,1)S(1)} %slice_bitcast_fusion.2), channel_id=1, source_target_pairs={{0,1},{1,0},{2,3},{3,2},{4,5},{5,4},{6,7},{7,6},{8,9},{9,8},{10,11... | collective-permute-start | bytes 442376 | tf_op jit(solution)/shard_map/ppermute | solution.py:400

commit v3 on v2

--- a/solution.py
+++ b/solution.py
@@ -136,74 +136,68 @@
         source_ref[i] = source[i * rows : (i + 1) * rows]
 
 
-def first_kernel(nodes_in, source_in, nodes_ref, source_w, normed_ref, source_ref, sems):
+def first_kernel(
+    nodes_in, source_in, target_in, node_in, bias_in,
+    nodes_ref, target_w, node_w, bias_ref, source_w, normed_ref, source_ref, sems,
+):
     count = nodes_ref.shape[0]
     _, core = place()
-    copies = [pltpu.make_async_copy(nodes_in.at[core + i], nodes_ref.at[i], sems.at[i]) for i in range(count)]
-    copies.append(pltpu.make_async_copy(source_in, source_w, sems.at[count]))
+    pairs = [(nodes_in.at[core + i], nodes_ref.at[i]) for i in range(count)]
+    pairs += [(source_in, source_w), (target_in, target_w), (node_in, node_w), (bias_in, bias_ref)]
+    copies = [pltpu.make_async_copy(*pair, sems.at[i]) for i, pair in enumerate(pairs)]
     for copy in copies:
         copy.start()
-    for copy in copies:
+    for copy in copies[: count + 1]:
         copy.wait()
     source_rows(lambda i: nodes_ref[i], normed_ref, source_ref, source_w)
+    for copy in copies[count + 1 :]:
+        copy.wait()
+    bias_ref[...] = bias_ref[...] * 0.5
 
 
 def outside(*arrays):
     return [pltpu.with_memory_space_constraint(x, pltpu.HBM) for x in arrays]
 
 
-def first(nodes, source_w):
+def first(nodes, source_w, target_w, node_w, bias):
     lat, rows, width = nodes.shape
     three, square = array(3, rows, width), array(width, width)
     return pl.pallas_call(
         first_kernel,
-        in_specs=[OUTSIDE] * 2,
-        out_specs=[WHOLE] * 4,
-        out_shape=[three, square, three, three],
-        scratch_shapes=[pltpu.SemaphoreType.DMA((4,))],
+        in_specs=[OUTSIDE] * 5,
+        out_specs=[WHOLE] * 7,
+        out_shape=[three, square, square, array(*bias.shape, dtype=F32), square, three, three],
+        scratch_shapes=[pltpu.SemaphoreType.DMA((7,))],
         compiler_params=params(),
         cost_estimate=cost(),
-    )(*outside(nodes, source_w))
+    )(*outside(nodes, source_w, target_w, node_w, bias))
 
 
 def second_kernel(
-    pieces, levels, target_in, node_in, bias_in, nodes_a, source_w, normed_a, source_a, nodes_b,
-    target_w, node_w, bias_ref, normed_ref, source_ref, far_ref, target_ref, sum_ref, sems,
+    pieces, levels, nodes_a, target_w, node_w, bias_ref, source_w, normed_a, source_a, nodes_b,
+    normed_ref, source_ref, far_ref, target_ref, sum_ref,
 ):
     _, core = place()
-    copies = [
-        pltpu.make_async_copy(*refs, sems.at[i])
-        for i, refs in enumerate(((target_in, target_w), (node_in, node_w), (bias_in, bias_ref)))
-    ]
-    for copy in copies:
-        copy.start()
     source_rows(lambda i: nodes_b[core + i], normed_ref, source_ref, source_w)
-    for copy in copies:
-        copy.wait()
-    bias_ref[...] = bias_ref[...] * 0.5
     halves = ((normed_a, source_a, nodes_a, core), (normed_ref, source_ref, nodes_b, 2 * core))
     out = update_pieces(pieces, levels, halves, target_w, node_w, bias_ref, None, target_ref, sum_ref)
     far_ref[0], far_ref[1] = out
 
 
-def second(levels, pieces, target_w, node_w, bias, *args):
-    width = target_w.shape[0]
-    three, square = array(*args[0].shape), array(width, width)
+def second(levels, pieces, *args):
+    three = array(*args[0].shape)
+    width = three.shape[-1]
     size = levels * GROUP
     count = len(pieces) * size
     return pl.pallas_call(
         functools.partial(second_kernel, pieces, levels),
-        in_specs=[OUTSIDE] * 3 + [WHOLE] * len(args),
-        out_specs=[WHOLE] * 6,
-        out_shape=[square, square, array(*bias.shape, dtype=F32), three, three, array(2, size, width)],
-        scratch_shapes=[
-            pltpu.VMEM((count, width), F32),
-            pltpu.VMEM((count, width), BF16),
-            pltpu.SemaphoreType.DMA((3,)),
-        ],
+        in_specs=[WHOLE] * len(args),
+        out_specs=[WHOLE] * 3,
+        out_shape=[three, three, array(2, size, width)],
+        scratch_shapes=[pltpu.VMEM((count, width), F32), pltpu.VMEM((count, width), BF16)],
         compiler_params=params(),
         cost_estimate=cost(),
-    )(*outside(target_w, node_w, bias), *args)
+    )(*args)
 
 
 def later_kernel(pieces, levels, with_edges, *refs):
@@ -215,7 +209,12 @@
         edges, refs = refs[:2], refs[2:]
     *outs, target_ref, sum_ref = refs
     if with_edges == "out":
-        *outs, west_ref, east_ref, target_ref, sum_ref, edge_ref = refs
+        mask_ref, *outs, west_ref, east_ref, kept_ref, target_ref, sum_ref, edge_ref = refs
+        here = lax.axis_index("level")
+        for q in range(4):
+            for level in range(levels):
+                kept = jnp.where(mask_ref[(here ^ q) * levels + level] > 0, 0.0, MASKED).astype(F32)
+                kept_ref[q * levels + level : q * levels + level + 1] = jnp.full((1, LANES), kept)
         lon = source_a.shape[1] // levels
         for h, source_ref in enumerate((source_a, source_b)):
             for k in range(2):
@@ -231,19 +230,21 @@
         ref[0], ref[1] = out[2 * i : 2 * i + 2]
 
 
-def later(levels, pieces, shared, edges=None, with_edges=None):
+def later(levels, pieces, shared, more=(), with_edges=None):
     width = shared[0].shape[-1]
     size = levels * GROUP
     count = len(pieces) * size
-    args = (*shared, *(edges or ()))
+    args = (*shared, *more)
+    specs = [WHOLE] * len(args)
     shapes = [array(2, size, width)] * (len(pieces) // 2)
     scratch = [pltpu.VMEM((count, width), F32), pltpu.VMEM((count, width), BF16)]
     if with_edges == "out":
-        shapes += [array(4, levels, width)] * 2
+        specs[-1] = SCALARS
+        shapes += [array(4, levels, width)] * 2 + [array(4 * levels, LANES, dtype=F32)]
         scratch += [pltpu.VMEM((2, levels, width), F32)]
     return pl.pallas_call(
         functools.partial(later_kernel, pieces, levels, with_edges),
-        in_specs=[WHOLE] * len(args),
+        in_specs=specs,
         out_specs=[WHOLE] * len(shapes),
         out_shape=shapes,
         scratch_shapes=scratch,
@@ -253,18 +254,12 @@
 
 
 def attention_kernel(
-    mask_ref, own_ref, opposite_ref, query_key, value_w, output_w,
-    out_own, out_sibling, out_opposite, q_ref, k_ref, v_ref, att_ref, weight_ref, bias_ref,
+    kept_ref, own_ref, opposite_ref, query_key, value_w, output_w,
+    out_own, out_sibling, out_opposite, q_ref, k_ref, v_ref, att_ref, weight_ref,
 ):
     _, size, width = own_ref.shape
-    here = lax.axis_index("level")
     levels = 4 * size // GROUP
-    each = levels // 4
     tiles = width // LANES
-    for q in range(4):
-        for level in range(each):
-            kept = jnp.where(mask_ref[(here ^ q) * each + level] > 0, 0.0, MASKED).astype(F32)
-            bias_ref[q * each + level : q * each + level + 1] = jnp.full((1, LANES), kept)
     x = jnp.concatenate([own_ref[0], own_ref[1], opposite_ref[0], opposite_ref[1]], axis=0)
     normed = normalize(x.astype(F32)).astype(BF16)
 
@@ -277,7 +272,7 @@
     spread(v_ref, matmul(normed, value_w[...]))
     low = lax.broadcasted_iota(jnp.int32, (levels, LANES), 1) < HEAD
     pad = jnp.zeros((LANES - 2 * levels, LANES), BF16)
-    bias = bias_ref[...]
+    kept = kept_ref[...]
     for column in range(GROUP):
         rows = pl.ds(column, levels, stride=GROUP)
         for t in range(tiles):
@@ -285,7 +280,7 @@
             zero = jnp.zeros_like(query)
             both = jnp.concatenate([jnp.where(low, query, zero), jnp.where(low, zero, query), pad], axis=0)
             scores = lax.dot_general(key, both, (((1,), (1,)), ((), ())), preferred_element_type=F32)
-            scores = scores + bias
+            scores = scores + kept
             weights = jnp.exp(scores - jnp.max(scores, axis=0, keepdims=True))
             weights = weights * (1.0 / jnp.sum(weights, axis=0, keepdims=True))
             weight_ref[levels * column : levels * (column + 1), LANES * t : LANES * (t + 1)] = weights.astype(BF16)
@@ -310,10 +305,10 @@
     tiled = pltpu.VMEM((width // LANES, rows, LANES), F32)
     return pl.pallas_call(
         attention_kernel,
-        in_specs=[SCALARS] + [WHOLE] * (len(args) - 1),
+        in_specs=[WHOLE] * len(args),
         out_specs=[WHOLE] * 3,
         out_shape=[array(size, width), array(size, width), array(2, size, width)],
-        scratch_shapes=[tiled] * 4 + [pltpu.VMEM((rows, width), BF16), pltpu.VMEM((rows // GROUP, LANES), F32)],
+        scratch_shapes=[tiled] * 4 + [pltpu.VMEM((rows, width), BF16)],
         compiler_params=params(),
         cost_estimate=cost(),
     )(*args)
@@ -372,24 +367,31 @@
     nodes = jnp.transpose(nodes, (0, 2, 1, 3)).reshape(lat, rows, width)
     nodes_b = lax.ppermute(nodes, "level", sibling)
     far, own = {}, {}
-    nodes_a, source_w, normed_a, source_a = first(nodes, source_weight)
-    target_w, node_w, bias, normed_b, source_b, far[0] = second(
-        levels, far_piece(0), target_weight, node_weight, direction_bias, nodes_a, source_w, normed_a, source_a, nodes_b
+    nodes_a, target_w, node_w, bias, source_w, normed_a, source_a = first(
+        nodes, source_weight, target_weight, node_weight, direction_bias
+    )
+    normed_b, source_b, far[0] = second(
+        levels, far_piece(0), nodes_a, target_w, node_w, bias, source_w, normed_a, source_a, nodes_b
     )
     shared = (nodes_a, normed_a, source_a, nodes_b, normed_b, source_b, target_w, node_w, bias)
-    far[1], own[0], west, east = later(levels, far_piece(1) + own_piece(0), shared, with_edges="out")
+    far[1], west, east, kept = later(levels, far_piece(1), shared, (level_mask,), "out")
     west = lax.ppermute(west, "sector", up)
     east = lax.ppermute(east, "sector", down)
-    (own[1],) = later(levels, own_piece(1), (after(nodes_a, own[0]), *shared[1:]))
-    far[2], own[2] = later(levels, far_piece(2) + own_piece(2), (after(nodes_a, own[1]), *shared[1:]), (west, east), "in")
+    then = lambda x: (after(nodes_a, x), *shared[1:])
+    (own[0],) = later(levels, own_piece(0), then(far[1]))
+    (far[2],) = later(levels, far_piece(2), then(own[0]), (west, east), "in")
     done, close, back, distant = {}, {}, {}, {}
     for c in range(3):
         arrived = lax.ppermute(far[c], "level", opposite)
-        mine = own[0] if c == 0 else after(own[c], done[c - 1], *([back[0]] if c == 2 else []))
-        args = (level_mask, mine, arrived, query_key, value_weight, output_weight)
+        if c == 1:
+            own[1], own[2] = later(levels, own_piece(1) + own_piece(2), then(done[0]), (west, east), "in")
+        mine = after(own[c], far[2] if c == 0 else done[c - 1])
+        args = (kept, mine, arrived, query_key, value_weight, output_weight)
         done[c], close[c], toward = attention(*args)
+        if c == 2:
+            toward = after(toward, back[0])
         back[c] = lax.ppermute(toward, "level", opposite)
-    late = lambda x: after(x, done[2])
+    late = lambda x: after(x, done[2], back[0])
     close = {c: lax.ppermute(late(close[c]), "level", sibling) for c in range(3)}
     for c in range(2):
         distant[c] = lax.ppermute(late(back[c][1]), "level", sibling)

time: 65.5 us -> 59.3 us (0.905)
  Pallas kernels: 30.5 us -> 28.1 us
  waiting for transfers between devices: 4.38 us -> 2.8 us
  starting transfers between devices: 29.3 us -> 27.9 us
  local copies, waits for them, and re-layouts: 0.85 us -> 0.05 us
    ppermute x3, waiting for transfers between devices: 2.93 us -> 0.01 us  [per_device(): arrived = lax.ppermute(far[c], 'level', opposite)]
    pallas_call x1, Pallas kernels: 4.24 us -> 2.43 us  [second(): pl.pallas_call(functools.partial(second_kernel, pieces, levels), in_specs...]
    ppermute x1, starting transfers between devices: 3.77 us -> 2.13 us  [per_device(): distant[2] = lax.ppermute(back[2][1], 'level', sibling)]
    pallas_call x4, Pallas kernels: 16.3 us -> 14.8 us  [the longest x3 11.7 us: attention(): pl.pallas_call(attention_kernel, in_specs=[WHOLE] * len(args), out_specs=...]
    ppermute x3, waiting for transfers between devices: 0.01 us -> 1.41 us  [per_device(): back[c] = lax.ppermute(toward, 'level', opposite)]
    pallas_call x3 -> x4, Pallas kernels: 7.33 us -> 8.24 us  [later(): pl.pallas_call(functools.partial(later_kernel, pieces, levels, with_edges...]
    unnamed x8, local copies, waits for them, and re-layouts: 0.81 us -> 0.02 us
  transfers between devices with their start and end apart: 15 -> 15, of which waited for: 5 -> 4; matrix products, arithmetic and copies ran while one was open for 0% -> 0% of each run, Pallas kernels for 39% -> 42%
where the time goes in v3:
time: 59.3 us; the launch traced here: 59.2 us
  Pallas kernels  28.1 us (47%)
  starting transfers between devices  27.9 us (47%)
  waiting for transfers between devices  2.8 us (5%)
    pallas_call x3, Pallas kernels, attention(): pl.pallas_call(attention_kernel, in_specs=[WHOLE] * len(args), out_specs=...  11.7 us
    pallas_call x4, Pallas kernels, later(): pl.pallas_call(functools.partial(later_kernel, pieces, levels, with_edges...  8.24 us
    ppermute x1, starting transfers between devices, per_device(): east = lax.ppermute(east, 'sector', down)  6.76 us
    ppermute x3, starting transfers between devices, per_device(): back[c] = lax.ppermute(toward, 'level', opposite)  5.03 us
    ppermute x3, starting transfers between devices, per_device(): arrived = lax.ppermute(far[c], 'level', opposite)  4.5 us
    ppermute x3, starting transfers between devices, per_device(): lax.ppermute(late(close[c]), 'level', sibling)  4.4 us
    ppermute x1, starting transfers between devices, per_device(): nodes_b = lax.ppermute(nodes, 'level', sibling)  3.24 us
    pallas_call x1, Pallas kernels, first(): pl.pallas_call(first_kernel, in_specs=[OUTSIDE] * 5, out_specs=[WHOLE] *...  3.18 us
  transfers between devices with their start and end apart: 15, of which 4 were waited for; matrix products, arithmetic and copies ran while one was open for 0% of the time, Pallas kernels for 42%

profile of v3, /device:TPU:1, one launch (start us, length us, event | category | flops | bytes accessed | tf_op | source)
XLA Modules:
  0.0 59.2 jit_solution(17327794835863393866)
XLA Ops:
  0.0 3.2 %collective-permute-start = (bf16[4,288,768]{2,1,0:T(8,128)(2,1)}, bf16[4,288,768]{2,1,0:T(8,128)(2,1)S(1)}, u32[]{:S(2)}, u32[]{:S(2)}) collective-permute-start(bf16[4,288,768]{2,1,0:T(8,128)(2,1)} %bitcast.12), channel_id=1, source_target_pairs={{0,1},{1,0},{2,3},{3,2},{4,5},{5,4},{6,7},{7,6},{8,9},{9,8},{10,11... | collective-permute-start | bytes 5308424 | tf_op jit(solution)/shard_map/ppermute | solution.py:368
  3.2 3.2 %shard_map.91 = (bf16[3,288,768]{2,1,0:T(8,128)(2,1)S(1)}, bf16[768,768]{1,0:T(8,128)(2,1)S(1)}, bf16[768,768]{1,0:T(8,128)(2,1)S(1)}, f32[4,768]{1,0:T(4,128)S(...) custom-call(bf16[4,288,768]{2,1,0:T(8,128)(2,1)} %bitcast.13, ...), custom_call_target="tpu_custom_call" | custom-call | flops 1 | bytes 1 | tf_op jit(solution)/shard_map/pallas_call | solution.py:165
  6.4 0.3 collective-permute-done.nodes_b.refs_3_
  6.8 2.4 %shard_map.92 = (bf16[3,288,768]{2,1,0:T(8,128)(2,1)S(1)}, bf16[3,288,768]{2,1,0:T(8,128)(2,1)S(1)}, bf16[2,96,768]{2,1,0:T(8,128)(2,1)S(1)}) custom-call(bf16[3,288,768]{2,1,0:T(8,128)(2,1)S(1)} %get-tuple-element.61.nodes_a.refs_0_, bf16[768,768]{1,0:T(8,128)(2,1)S(1)} %get-tuple-element.46.target_w.refs_6_, ...), custom_call_target="tpu_custom_call" | custom-call | flops 1 | bytes 1 | tf_op jit(solution)/shard_map/pallas_call | solution.py:192
  9.2 1.3 %collective-permute-start.3 = (bf16[2,96,768]{2,1,0:T(8,128)(2,1)S(1)}, bf16[2,96,768]{2,1,0:T(8,128)(2,1)S(1)}, u32[]{:S(2)}, u32[]{:S(2)}) collective-permute-start(bf16[2,96,768]{2,1,0:T(8,128)(2,1)S(1)} %get-tuple-element.59), channel_id=1, source_target_pairs={{0,2},{1,3},{2,0},{3,1},{4,6},{5,7},{6,4},{7,5},{8,10},{9,11},{10,... | collective-permute-start | bytes 884744 | tf_op jit(solution)/shard_map/ppermute | solution.py:385
  10.5 2.4 %shard_map.93 = (bf16[2,96,768]{2,1,0:T(8,128)(2,1)S(1)}, bf16[4,12,768]{2,1,0:T(8,128)(2,1)S(1)}, bf16[4,12,768]{2,1,0:T(8,128)(2,1)S(1)}, f32[48,128]{1,0:T(8,128)S(1)}) custom-call(bf16[3,288,768]{2,1,0:T(8,128)(2,1)S(1)} %get-tuple-element.61.nodes_a.refs_0_, bf16[3,288,768]{2,1,0:T(8,128)(2,1)S(1)} %get-tuple-element.44.normed_a.refs_1_, ...), custom_call_target="tpu_custom_call" | custom-call | flops 1 | bytes 1 | tf_op jit(solution)/shard_map/pallas_call | solution.py:245
  12.8 1.3 %collective-permute-start.1 = (bf16[4,12,768]{2,1,0:T(8,128)(2,1)S(1)}, bf16[4,12,768]{2,1,0:T(8,128)(2,1)S(1)}, u32[]{:S(2)}, u32[]{:S(2)}) collective-permute-start(bf16[4,12,768]{2,1,0:T(8,128)(2,1)S(1)} %get-tuple-element.56), channel_id=1, source_target_pairs={{0,4},{4,8},{8,12},{12,16},{16,20},{20,24},{24,28},{28,32},{32,36}... | collective-permute-start | bytes 221192 | tf_op jit(solution)/shard_map/ppermute | solution.py:378
  14.1 6.8 %collective-permute-start.2 = (bf16[4,12,768]{2,1,0:T(8,128)(2,1)S(1)}, bf16[4,12,768]{2,1,0:T(8,128)(2,1)S(1)}, u32[]{:S(2)}, u32[]{:S(2)}) collective-permute-start(bf16[4,12,768]{2,1,0:T(8,128)(2,1)S(1)} %get-tuple-element.57), channel_id=1, source_target_pairs={{4,0},{8,4},{12,8},{16,12},{20,16},{24,20},{28,24},{32,28},{36,32}... | collective-permute-start | bytes 221192 | tf_op jit(solution)/shard_map/ppermute | solution.py:379
  20.9 1.6 %collective-permute-start.4 = (bf16[2,96,768]{2,1,0:T(8,128)(2,1)S(1)}, bf16[2,96,768]{2,1,0:T(8,128)(2,1)S(1)}, u32[]{:S(2)}, u32[]{:S(2)}) collective-permute-start(bf16[2,96,768]{2,1,0:T(8,128)(2,1)S(1)} %get-tuple-element.53), channel_id=1, source_target_pairs={{0,2},{1,3},{2,0},{3,1},{4,6},{5,7},{6,4},{7,5},{8,10},{9,11},{10,... | collective-permute-start | bytes 884744 | tf_op jit(solution)/shard_map/ppermute | solution.py:385
  22.5 1.3 %shard_map.94.own_ref = bf16[2,96,768]{2,1,0:T(8,128)(2,1)S(1)} custom-call(bf16[3,288,768]{2,1,0:T(8,128)(2,1)S(1)} %get-tuple-element.61.nodes_a.refs_0_, bf16[3,288,768]{2,1,0:T(8,128)(2,1)S(1)} %get-tuple-element.44.normed_a.refs_1_, bf16[3,288,768]{2,1,0:T(8,128)(2,1)S(1)} %get-tuple-element.45.source_a.refs_2_, ...), custom_call_target="tpu_custom_call" | custom-call | flops 1 | bytes 1 | tf_op jit(solution)/shard_map/pallas_call | solution.py:245
  23.8 0.0 copy-start.1
  23.8 1.6 %shard_map.95 = bf16[2,96,768]{2,1,0:T(8,128)(2,1)S(1)} custom-call(bf16[3,288,768]{2,1,0:T(8,128)(2,1)S(1)} %get-tuple-element.61.nodes_a.refs_0_, bf16[3,288,768]{2,1,0:T(8,128)(2,1)S(1)} %get-tuple-element.44.normed_a.refs_1_, bf16[3,288,768]{2,1,0:T(8,128)(2,1)S(1)} %get-tuple-element.45.source_a.refs_2_, ...), custom_call_target="tpu_custom_call" | custom-call | flops 1 | bytes 1 | tf_op jit(solution)/shard_map/pallas_call | solution.py:245
  25.5 1.7 %collective-permute-start.5 = (bf16[2,96,768]{2,1,0:T(8,128)(2,1)S(1)}, bf16[2,96,768]{2,1,0:T(8,128)(2,1)S(1)}, u32[]{:S(2)}, u32[]{:S(2)}) collective-permute-start(bf16[2,96,768]{2,1,0:T(8,128)(2,1)S(1)} %shard_map.95), channel_id=1, source_target_pairs={{0,2},{1,3},{2,0},{3,1},{4,6},{5,7},{6,4},{7,5},{8,10},{9,11},{10,... | collective-permute-start | bytes 884744 | tf_op jit(solution)/shard_map/ppermute | solution.py:385
  27.2 3.9 %shard_map.96 = (bf16[96,768]{1,0:T(8,128)(2,1)S(1)}, bf16[96,768]{1,0:T(8,128)(2,1)S(1)}, bf16[2,96,768]{2,1,0:T(8,128)(2,1)S(1)}) custom-call(f32[48,128]{1,0:T(8,128)S(1)} %get-tuple-element.52.kept_ref, bf16[2,96,768]{2,1,0:T(8,128)(2,1)S(1)} %shard_map.94.own_ref, bf16[2,96,768]{2,1,0:T(8,128)(2,1)S(1)} %collective-permute-done.3.opposite_ref, ...), custom_call_target="tpu_custom_call" | custom-call | flops 1 | bytes 1 | tf_op jit(solution)/shard_map/pallas_call | solution.py:306
  31.1 1.7 %collective-permute-start.6 = (bf16[2,96,768]{2,1,0:T(8,128)(2,1)S(1)}, bf16[2,96,768]{2,1,0:T(8,128)(2,1)S(1)}, u32[]{:S(2)}, u32[]{:S(2)}) collective-permute-start(bf16[2,96,768]{2,1,0:T(8,128)(2,1)S(1)} %get-tuple-element.69), channel_id=1, source_target_pairs={{0,2},{1,3},{2,0},{3,1},{4,6},{5,7},{6,4},{7,5},{8,10},{9,11},{10,... | collective-permute-start | bytes 884744 | tf_op jit(solution)/shard_map/ppermute | solution.py:393
  32.7 2.9 %shard_map.97 = (bf16[2,96,768]{2,1,0:T(8,128)(2,1)S(1)}, bf16[2,96,768]{2,1,0:T(8,128)(2,1)S(1)}) custom-call(bf16[3,288,768]{2,1,0:T(8,128)(2,1)S(1)} %get-tuple-element.61.nodes_a.refs_0_, bf16[3,288,768]{2,1,0:T(8,128)(2,1)S(1)} %get-tuple-element.44.normed_a.refs_1_, bf16[3,288,768]{2,1,0:T(8,128)(2,1)S(1)} %get-tuple-element.45.source_a.refs_2_, ...), custom_call_target="tpu_custom_call" | custom-call | flops 1 | bytes 1 | tf_op jit(solution)/shard_map/pallas_call | solution.py:245
  35.7 3.9 %shard_map.98 = (bf16[96,768]{1,0:T(8,128)(2,1)S(1)}, bf16[96,768]{1,0:T(8,128)(2,1)S(1)}, bf16[2,96,768]{2,1,0:T(8,128)(2,1)S(1)}) custom-call(f32[48,128]{1,0:T(8,128)S(1)} %get-tuple-element.52.kept_ref, bf16[2,96,768]{2,1,0:T(8,128)(2,1)S(1)} %get-tuple-element.63.own_ref, bf16[2,96,768]{2,1,0:T(8,128)(2,1)S(1)} %collective-permute-done.4.opposite_ref, ...), custom_call_target="tpu_custom_call" | custom-call | flops 1 | bytes 1 | tf_op jit(solution)/shard_map/pallas_call | solution.py:306
  39.6 1.7 %collective-permute-start.10 = (bf16[2,96,768]{2,1,0:T(8,128)(2,1)S(1)}, bf16[2,96,768]{2,1,0:T(8,128)(2,1)S(1)}, u32[]{:S(2)}, u32[]{:S(2)}) collective-permute-start(bf16[2,96,768]{2,1,0:T(8,128)(2,1)S(1)} %get-tuple-element.75), channel_id=1, source_target_pairs={{0,2},{1,3},{2,0},{3,1},{4,6},{5,7},{6,4},{7,5},{8,10},{9,11},{10,... | collective-permute-start | bytes 884744 | tf_op jit(solution)/shard_map/ppermute | solution.py:393
  41.3 3.9 %shard_map.99 = (bf16[96,768]{1,0:T(8,128)(2,1)S(1)}, bf16[96,768]{1,0:T(8,128)(2,1)S(1)}, bf16[2,96,768]{2,1,0:T(8,128)(2,1)S(1)}) custom-call(f32[48,128]{1,0:T(8,128)S(1)} %get-tuple-element.52.kept_ref, bf16[2,96,768]{2,1,0:T(8,128)(2,1)S(1)} %get-tuple-element.66.own_ref, bf16[2,96,768]{2,1,0:T(8,128)(2,1)S(1)} %collective-permute-done.5.opposite_ref, ...), custom_call_target="tpu_custom_call" | custom-call | flops 1 | bytes 1 | tf_op jit(solution)/shard_map/pallas_call | solution.py:306
  45.2 1.7 %collective-permute-start.11 = (bf16[2,96,768]{2,1,0:T(8,128)(2,1)S(1)}, bf16[2,96,768]{2,1,0:T(8,128)(2,1)S(1)}, u32[]{:S(2)}, u32[]{:S(2)}) collective-permute-start(bf16[2,96,768]{2,1,0:T(8,128)(2,1)S(1)} %get-tuple-element.77), channel_id=1, source_target_pairs={{0,2},{1,3},{2,0},{3,1},{4,6},{5,7},{6,4},{7,5},{8,10},{9,11},{10,... | collective-permute-start | bytes 884744 | tf_op jit(solution)/shard_map/ppermute | solution.py:393
  46.9 2.4 %collective-permute-start.7 = (bf16[96,768]{1,0:T(8,128)(2,1)S(1)}, bf16[96,768]{1,0:T(8,128)(2,1)S(1)}, u32[]{:S(2)}, u32[]{:S(2)}) collective-permute-start(bf16[96,768]{1,0:T(8,128)(2,1)S(1)} %get-tuple-element.70), channel_id=1, source_target_pairs={{0,1},{1,0},{2,3},{3,2},{4,5},{5,4},{6,7},{7,6},{8,9},{9,8},{10,11... | collective-permute-start | bytes 442376 | tf_op jit(solution)/shard_map/ppermute | solution.py:395
  49.3 0.1 collective-permute-start.8
  49.4 0.4 collective-permute-start.12
  49.8 1.9 %collective-permute-start.9 = (bf16[96,768]{1,0:T(8,128)(2,1)S(1)}, bf16[96,768]{1,0:T(8,128)(2,1)S(1)}, u32[]{:S(2)}, u32[]{:S(2)}) collective-permute-start(bf16[96,768]{1,0:T(8,128)(2,1)S(1)} %get-tuple-element.74), channel_id=1, source_target_pairs={{0,1},{1,0},{2,3},{3,2},{4,5},{5,4},{6,7},{7,6},{8,9},{9,8},{10,11... | collective-permute-start | bytes 442376 | tf_op jit(solution)/shard_map/ppermute | solution.py:395
  51.7 0.1 collective-permute-start.13
  51.8 0.9 %collective-permute-done.9.refs_5_ = bf16[96,768]{1,0:T(8,128)(2,1)S(1)} collective-permute-done((bf16[96,768]{1,0:T(8,128)(2,1)S(1)}, bf16[96,768]{1,0:T(8,128)(2,1)S(1)}, u32[]{:S(2)}, u32[]{:S(2)}) %collective-permute-start.9) | collective-permute-done | bytes 147488 | tf_op jit(solution)/shard_map/ppermute | solution.py:395
  52.7 1.0 %shard_map.100.refs_0_ = bf16[4,288,768]{2,1,0:T(8,128)(2,1)} custom-call(bf16[96,768]{1,0:T(8,128)(2,1)S(1)} %get-tuple-element.60.refs_0_, bf16[96,768]{1,0:T(8,128)(2,1)S(1)} %get-tuple-element.64.refs_1_, bf16[96,768]{1,0:T(8,128)(2,1)S(1)} %get-tuple-element.67.refs_2_, bf16[96,768]{1,0:T(8,128)(2,1)S(1)} %collective-permute-done.7.refs_3_, ...), custom_call_target="tpu_custom_call" | custom-call | flops 1 | bytes 1 | tf_op jit(solution)/shard_map/pallas_call | solution.py:338
  53.7 1.4 %collective-permute-done.11.refs_3_ = bf16[2,96,768]{2,1,0:T(8,128)(2,1)S(1)} collective-permute-done((bf16[2,96,768]{2,1,0:T(8,128)(2,1)S(1)}, bf16[2,96,768]{2,1,0:T(8,128)(2,1)S(1)}, u32[]{:S(2)}, u32[]{:S(2)}) %collective-permute-start.11) | collective-permute-done | bytes 294944 | tf_op jit(solution)/shard_map/ppermute | solution.py:393
  55.1 2.1 %collective-permute-start.14 = (bf16[96,768]{1,0:T(8,128)(2,1)S(1)}, bf16[96,768]{1,0:T(8,128)(2,1)S(1)}, u32[]{:S(2)}, u32[]{:S(2)}) collective-permute-start(bf16[96,768]{1,0:T(8,128)(2,1)S(1)} %slice_bitcast_fusion.2), channel_id=1, source_target_pairs={{0,1},{1,0},{2,3},{3,2},{4,5},{5,4},{6,7},{7,6},{8,9},{9,8},{10,11... | collective-permute-start | bytes 442376 | tf_op jit(solution)/shard_map/ppermute | solution.py:402
  57.2 0.8 %shard_map.101.refs_0_ = bf16[4,288,768]{2,1,0:T(8,128)(2,1)} custom-call(bf16[4,288,768]{2,1,0:T(8,128)(2,1)} %shard_map.100.refs_0_, bf16[2,96,768]{2,1,0:T(8,128)(2,1)S(1)} %collective-permute-done.6.refs_1_, bf16[2,96,768]{2,1,0:T(8,128)(2,1)S(1)} %collective-permute-done.10.refs_2_, ...), custom_call_target="tpu_custom_call", output_to_operand_aliasing={{}: (0, {})} | custom-call | flops 1 | bytes 1 | tf_op jit(solution)/shard_map/pallas_call | solution.py:338
  58.1 0.2 collective-permute-done.14.refs_3_
  58.2 0.8 %shard_map.102 = bf16[4,288,768]{2,1,0:T(8,128)(2,1)} custom-call(bf16[4,288,768]{2,1,0:T(8,128)(2,1)} %shard_map.101.refs_0_, bf16[96,768]{1,0:T(8,128)(2,1)S(1)} %collective-permute-done.12.refs_1_, bf16[96,768]{1,0:T(8,128)(2,1)S(1)} %collective-permute-done.13.refs_2_, ...), custom_call_target="tpu_custom_call", output_to_operand_aliasing={{}: (0, {})} | custom-call | flops 1 | bytes 1 | tf_op jit(solution)/shard_map/pallas_call | solution.py:338
  (21 shorter events, 0.1 us)
Async XLA Ops:
  0.0 6.8 %collective-permute-start = (bf16[4,288,768]{2,1,0:T(8,128)(2,1)}, bf16[4,288,768]{2,1,0:T(8,128)(2,1)S(1)}, u32[]{:S(2)}, u32[]{:S(2)}) collective-permute-start(bf16[4,288,768]{2,1,0:T(8,128)(2,1)} %bitcast.12), channel_id=1, source_target_pairs={{0,1},{1,0},{2,3},{3,2},{4,5},{5,4},{6,7},{7,6},{8,9},{9,8},{10,11... | collective-permute-start | bytes 5308424 | tf_op jit(solution)/shard_map/ppermute | solution.py:368
  6.8 3.7 %copy-start.3 = (s32[48]{0:T(128)S(1)}, s32[48]{0:T(128)}, u32[]{:S(2)}) copy-start(s32[48]{0:T(128)} %refs_9_.1) | copy-start | bytes 580
  9.2 18.0 %collective-permute-start.3 = (bf16[2,96,768]{2,1,0:T(8,128)(2,1)S(1)}, bf16[2,96,768]{2,1,0:T(8,128)(2,1)S(1)}, u32[]{:S(2)}, u32[]{:S(2)}) collective-permute-start(bf16[2,96,768]{2,1,0:T(8,128)(2,1)S(1)} %get-tuple-element.59), channel_id=1, source_target_pairs={{0,2},{1,3},{2,0},{3,1},{4,6},{5,7},{6,4},{7,5},{8,10},{9,11},{10,... | collective-permute-start | bytes 884744 | tf_op jit(solution)/shard_map/ppermute | solution.py:385
  12.8 11.0 %collective-permute-start.1 = (bf16[4,12,768]{2,1,0:T(8,128)(2,1)S(1)}, bf16[4,12,768]{2,1,0:T(8,128)(2,1)S(1)}, u32[]{:S(2)}, u32[]{:S(2)}) collective-permute-start(bf16[4,12,768]{2,1,0:T(8,128)(2,1)S(1)} %get-tuple-element.56), channel_id=1, source_target_pairs={{0,4},{4,8},{8,12},{12,16},{16,20},{20,24},{24,28},{28,32},{32,36}... | collective-permute-start | bytes 221192 | tf_op jit(solution)/shard_map/ppermute | solution.py:378
  14.1 9.7 %collective-permute-start.2 = (bf16[4,12,768]{2,1,0:T(8,128)(2,1)S(1)}, bf16[4,12,768]{2,1,0:T(8,128)(2,1)S(1)}, u32[]{:S(2)}, u32[]{:S(2)}) collective-permute-start(bf16[4,12,768]{2,1,0:T(8,128)(2,1)S(1)} %get-tuple-element.57), channel_id=1, source_target_pairs={{4,0},{8,4},{12,8},{16,12},{20,16},{24,20},{28,24},{32,28},{36,32}... | collective-permute-start | bytes 221192 | tf_op jit(solution)/shard_map/ppermute | solution.py:379
  20.9 14.8 %collective-permute-start.4 = (bf16[2,96,768]{2,1,0:T(8,128)(2,1)S(1)}, bf16[2,96,768]{2,1,0:T(8,128)(2,1)S(1)}, u32[]{:S(2)}, u32[]{:S(2)}) collective-permute-start(bf16[2,96,768]{2,1,0:T(8,128)(2,1)S(1)} %get-tuple-element.53), channel_id=1, source_target_pairs={{0,2},{1,3},{2,0},{3,1},{4,6},{5,7},{6,4},{7,5},{8,10},{9,11},{10,... | collective-permute-start | bytes 884744 | tf_op jit(solution)/shard_map/ppermute | solution.py:385
  23.8 3.4 %copy-start.1 = (bf16[768,768]{1,0:T(8,128)(2,1)S(1)}, bf16[768,768]{1,0:T(8,128)(2,1)}, u32[]{:S(2)}) copy-start(bf16[768,768]{1,0:T(8,128)(2,1)} %value_w.5) | copy-start | bytes 3538948
  23.8 3.4 %copy-start.2 = (bf16[768,768]{1,0:T(8,128)(2,1)S(1)}, bf16[768,768]{1,0:T(8,128)(2,1)}, u32[]{:S(2)}) copy-start(bf16[768,768]{1,0:T(8,128)(2,1)} %output_w.5) | copy-start | bytes 3538948
  23.8 3.3 %copy-start = (bf16[2,768,768]{2,1,0:T(8,128)(2,1)S(1)}, bf16[2,768,768]{2,1,0:T(8,128)(2,1)}, u32[]{:S(2)}) copy-start(bf16[2,768,768]{2,1,0:T(8,128)(2,1)} %query_key.5) | copy-start | bytes 7077892
  25.5 15.8 %collective-permute-start.5 = (bf16[2,96,768]{2,1,0:T(8,128)(2,1)S(1)}, bf16[2,96,768]{2,1,0:T(8,128)(2,1)S(1)}, u32[]{:S(2)}, u32[]{:S(2)}) collective-permute-start(bf16[2,96,768]{2,1,0:T(8,128)(2,1)S(1)} %shard_map.95), channel_id=1, source_target_pairs={{0,2},{1,3},{2,0},{3,1},{4,6},{5,7},{6,4},{7,5},{8,10},{9,11},{10,... | collective-permute-start | bytes 884744 | tf_op jit(solution)/shard_map/ppermute | solution.py:385
  31.1 14.1 %collective-permute-start.6 = (bf16[2,96,768]{2,1,0:T(8,128)(2,1)S(1)}, bf16[2,96,768]{2,1,0:T(8,128)(2,1)S(1)}, u32[]{:S(2)}, u32[]{:S(2)}) collective-permute-start(bf16[2,96,768]{2,1,0:T(8,128)(2,1)S(1)} %get-tuple-element.69), channel_id=1, source_target_pairs={{0,2},{1,3},{2,0},{3,1},{4,6},{5,7},{6,4},{7,5},{8,10},{9,11},{10,... | collective-permute-start | bytes 884744 | tf_op jit(solution)/shard_map/ppermute | solution.py:393
  39.6 10.2 %collective-permute-start.10 = (bf16[2,96,768]{2,1,0:T(8,128)(2,1)S(1)}, bf16[2,96,768]{2,1,0:T(8,128)(2,1)S(1)}, u32[]{:S(2)}, u32[]{:S(2)}) collective-permute-start(bf16[2,96,768]{2,1,0:T(8,128)(2,1)S(1)} %get-tuple-element.75), channel_id=1, source_target_pairs={{0,2},{1,3},{2,0},{3,1},{4,6},{5,7},{6,4},{7,5},{8,10},{9,11},{10,... | collective-permute-start | bytes 884744 | tf_op jit(solution)/shard_map/ppermute | solution.py:393
  45.2 9.9 %collective-permute-start.11 = (bf16[2,96,768]{2,1,0:T(8,128)(2,1)S(1)}, bf16[2,96,768]{2,1,0:T(8,128)(2,1)S(1)}, u32[]{:S(2)}, u32[]{:S(2)}) collective-permute-start(bf16[2,96,768]{2,1,0:T(8,128)(2,1)S(1)} %get-tuple-element.77), channel_id=1, source_target_pairs={{0,2},{1,3},{2,0},{3,1},{4,6},{5,7},{6,4},{7,5},{8,10},{9,11},{10,... | collective-permute-start | bytes 884744 | tf_op jit(solution)/shard_map/ppermute | solution.py:393
  46.9 4.8 %collective-permute-start.7 = (bf16[96,768]{1,0:T(8,128)(2,1)S(1)}, bf16[96,768]{1,0:T(8,128)(2,1)S(1)}, u32[]{:S(2)}, u32[]{:S(2)}) collective-permute-start(bf16[96,768]{1,0:T(8,128)(2,1)S(1)} %get-tuple-element.70), channel_id=1, source_target_pairs={{0,1},{1,0},{2,3},{3,2},{4,5},{5,4},{6,7},{7,6},{8,9},{9,8},{10,11... | collective-permute-start | bytes 442376 | tf_op jit(solution)/shard_map/ppermute | solution.py:395
  49.3 2.5 %collective-permute-start.8 = (bf16[96,768]{1,0:T(8,128)(2,1)S(1)}, bf16[96,768]{1,0:T(8,128)(2,1)S(1)}, u32[]{:S(2)}, u32[]{:S(2)}) collective-permute-start(bf16[96,768]{1,0:T(8,128)(2,1)S(1)} %get-tuple-element.72), channel_id=1, source_target_pairs={{0,1},{1,0},{2,3},{3,2},{4,5},{5,4},{6,7},{7,6},{8,9},{9,8},{10,11... | collective-permute-start | bytes 442376 | tf_op jit(solution)/shard_map/ppermute | solution.py:395
  49.4 8.7 %collective-permute-start.12 = (bf16[96,768]{1,0:T(8,128)(2,1)S(1)}, bf16[96,768]{1,0:T(8,128)(2,1)S(1)}, u32[]{:S(2)}, u32[]{:S(2)}) collective-permute-start(bf16[96,768]{1,0:T(8,128)(2,1)S(1)} %slice_bitcast_fusion.1), channel_id=1, source_target_pairs={{0,1},{1,0},{2,3},{3,2},{4,5},{5,4},{6,7},{7,6},{8,9},{9,8},{10,11... | collective-permute-start | bytes 442376 | tf_op jit(solution)/shard_map/ppermute | solution.py:397
  49.8 2.9 %collective-permute-start.9 = (bf16[96,768]{1,0:T(8,128)(2,1)S(1)}, bf16[96,768]{1,0:T(8,128)(2,1)S(1)}, u32[]{:S(2)}, u32[]{:S(2)}) collective-permute-start(bf16[96,768]{1,0:T(8,128)(2,1)S(1)} %get-tuple-element.74), channel_id=1, source_target_pairs={{0,1},{1,0},{2,3},{3,2},{4,5},{5,4},{6,7},{7,6},{8,9},{9,8},{10,11... | collective-permute-start | bytes 442376 | tf_op jit(solution)/shard_map/ppermute | solution.py:395
  51.7 6.4 %collective-permute-start.13 = (bf16[96,768]{1,0:T(8,128)(2,1)S(1)}, bf16[96,768]{1,0:T(8,128)(2,1)S(1)}, u32[]{:S(2)}, u32[]{:S(2)}) collective-permute-start(bf16[96,768]{1,0:T(8,128)(2,1)S(1)} %slice_bitcast_fusion), channel_id=1, source_target_pairs={{0,1},{1,0},{2,3},{3,2},{4,5},{5,4},{6,7},{7,6},{8,9},{9,8},{10,11... | collective-permute-start | bytes 442376 | tf_op jit(solution)/shard_map/ppermute | solution.py:397
  55.1 3.1 %collective-permute-start.14 = (bf16[96,768]{1,0:T(8,128)(2,1)S(1)}, bf16[96,768]{1,0:T(8,128)(2,1)S(1)}, u32[]{:S(2)}, u32[]{:S(2)}) collective-permute-start(bf16[96,768]{1,0:T(8,128)(2,1)S(1)} %slice_bitcast_fusion.2), channel_id=1, source_target_pairs={{0,1},{1,0},{2,3},{3,2},{4,5},{5,4},{6,7},{7,6},{8,9},{9,8},{10,11... | collective-permute-start | bytes 442376 | tf_op jit(solution)/shard_map/ppermute | solution.py:402

commit v4 on v3

v4 whole, which is shorter than its diff:
```python
import functools

import jax
import jax.numpy as jnp
from jax import lax
from jax.experimental import pallas as pl
from jax.experimental.pallas import tpu as pltpu
from jax.sharding import PartitionSpec as P

HEAD = 64
EPSILON = 1e-06
MASKED = -1e30
GROUP = 8
LANES = 128
HALF = GROUP // 2
F32, BF16 = jnp.float32, jnp.bfloat16
WHOLE = pl.BlockSpec(memory_space=pltpu.VMEM)
SCALARS = pl.BlockSpec(memory_space=pltpu.SMEM)
OUTSIDE = pl.BlockSpec(memory_space=pltpu.HBM)


def array(*shape, dtype=BF16):
    return jax.ShapeDtypeStruct(shape, dtype)


def params(mib=24):
    return pltpu.CompilerParams(vmem_limit_bytes=mib << 20)


def cost(flops=1):
    return pl.CostEstimate(flops=flops, bytes_accessed=1, transcendentals=0)


def normalize(x):
    return x * lax.rsqrt(jnp.mean(x * x, axis=-1, keepdims=True) + EPSILON)


def matmul(x, weight):
    return jnp.dot(x, weight, preferred_element_type=F32)


def place():
    here = lax.axis_index("level")
    return here // 2, here % 2


def chunk_of(x, chunk):
    first, middle, last = (x[:, GROUP * i : GROUP * (i + 1)] for i in range(3))
    if chunk == 0:
        return middle
    low = lax.broadcasted_iota(jnp.int32, first.shape, 1) < HALF
    return jnp.where(low, last, first) if chunk == 1 else jnp.where(low, first, last)


def whole_of(middle, beside, outer):
    low = lax.broadcasted_iota(jnp.int32, middle.shape, 1) < HALF
    return jnp.concatenate([jnp.where(low, outer, beside), middle, jnp.where(low, beside, outer)], axis=1)


def by_chunk(x, levels):
    rows, width = x.shape
    x = x.astype(F32).reshape(levels, rows // levels, width)
    return jnp.concatenate([chunk_of(x, c).reshape(levels * GROUP, width) for c in range(3)], axis=0)


def update_pieces(pieces, levels, halves, target_w, node_w, bias_ref, edges, target_ref, sum_ref):
    chip, core = place()
    width = bias_ref.shape[-1]
    size = levels * GROUP
    side = [jnp.where(chip == (1 if far else 0), 0, 1) for far in (False, True)]
    x = [halves[h][0][core + side[far], size * c : size * (c + 1)] for far, c, h in pieces]
    target_ref[...] = matmul(jnp.concatenate(x, axis=0), target_w[...]) * 0.5
    step = LANES
    for n, (far, c, h) in enumerate(pieces):
        _, source_ref, east_ref, west_ref = halves[h][:4]
        row = core + side[far]
        lat = core + row
        north, south = jnp.maximum(row - 1, 0), jnp.minimum(row + 1, 2)
        has_north = jnp.where(lat >= 1, 1.0, 0.0)
        has_south = jnp.where(lat <= 2, 1.0, 0.0)
        if c == 2:
            west_edge = edges[0][2 * h + side[far]].astype(F32)
            east_edge = edges[1][2 * h + side[far]].astype(F32)
        for pair in range(levels // 2):
            for lane in range(0, width, step):
                cols = slice(lane, lane + step)
                rows = slice(size * c + 2 * GROUP * pair, size * c + 2 * GROUP * (pair + 1))
                at = slice(n * size + 2 * GROUP * pair, n * size + 2 * GROUP * (pair + 1))

                def put(x, place, edge):
                    place = lax.broadcasted_iota(jnp.int32, (GROUP, step), 0) == place
                    parts = [
                        jnp.where(place, edge[2 * pair + k : 2 * pair + k + 1, cols], x[GROUP * k : GROUP * (k + 1)])
                        for k in range(2)
                    ]
                    return jnp.concatenate(parts, axis=0)

                east = east_ref[side[far], rows, cols].astype(F32)
                west = west_ref[side[far], rows, cols].astype(F32)
                if c == 2:
                    west = put(west, 0, west_edge)
                    east = put(east, GROUP - 1, east_edge)
                target = target_ref[at, cols]

                def halved_silu(other, k):
                    half = target + other + bias_ref[k : k + 1, cols]
                    return half + half * jnp.tanh(half)

                total = halved_silu(east, 0) + halved_silu(west, 1)
                total = total + halved_silu(source_ref[north, rows, cols].astype(F32), 2) * has_north
                total = total + halved_silu(source_ref[south, rows, cols].astype(F32), 3) * has_south
                sum_ref[at, cols] = total.astype(BF16)
    update = matmul(sum_ref[...], node_w[...])
    out = []
    for n, (far, c, h) in enumerate(pieces):
        nodes_ref, offset = halves[h][4:]
        lon = nodes_ref.shape[1] // levels
        own = nodes_ref[offset + side[far]].astype(F32).reshape(levels, lon, width)
        own = chunk_of(own, c).reshape(size, width)
        out.append((own + update[n * size : (n + 1) * size]).astype(BF16))
    return out


def source_rows(levels, read, normed_ref, source_ref, east_ref, west_ref, raw_ref, edges, source_w):
    _, core = place()
    count, rows, width = normed_ref.shape
    size = levels * GROUP
    for i in range(count):
        normed_ref[i] = normalize(by_chunk(read(i), levels)).astype(BF16)
    normed = jnp.concatenate([normed_ref[i] for i in range(count)], axis=0)
    source = matmul(normed, source_w[...]) * 0.5
    for i in range(count):
        raw_ref[i] = source[i * rows : (i + 1) * rows]
        source_ref[i] = source[i * rows : (i + 1) * rows].astype(BF16)
    shape = (2, GROUP, LANES)
    spot = lax.broadcasted_iota(jnp.int32, shape, 1)
    for k in range(2):
        for pair in range(levels // 2):
            for lane in range(0, width, LANES):
                cols = slice(lane, lane + LANES)
                at = [slice(size * c + 2 * GROUP * pair, size * c + 2 * GROUP * (pair + 1)) for c in range(3)]
                x = [raw_ref[core + k, at[c], cols].reshape(shape) for c in range(3)]
                up = [pltpu.roll(y, GROUP - 1, 1) for y in x]
                down = [pltpu.roll(y, 1, 1) for y in x]
                last, half = spot == GROUP - 1, spot == HALF - 1
                east = [
                    jnp.where(last, up[1], up[0]),
                    jnp.where(half, up[2], jnp.where(last, up[0], up[1])),
                    jnp.where(half, up[1], up[2]),
                ]
                first, half = spot == 0, spot == HALF
                west = [
                    jnp.where(first, down[1], down[0]),
                    jnp.where(half, down[2], jnp.where(first, down[0], down[1])),
                    jnp.where(half, down[1], down[2]),
                ]
                for c in range(3):
                    east_ref[k, at[c], cols] = east[c].reshape(2 * GROUP, LANES).astype(BF16)
                    west_ref[k, at[c], cols] = west[c].reshape(2 * GROUP, LANES).astype(BF16)
        for level in range(levels):
            at = 2 * size + level * GROUP
            edges[0][k, level : level + 1] = raw_ref[core + k, at : at + 1]
            edges[1][k, level : level + 1] = raw_ref[core + k, at + GROUP - 1 : at + GROUP]


def first_kernel(
    levels, nodes_in, source_in, target_in, node_in, bias_in,
    nodes_ref, target_w, node_w, bias_ref, source_w, normed_ref, source_ref, east_ref, west_ref, begin_ref, end_ref,
    raw_ref, sems,
):
    count = nodes_ref.shape[0]
    _, core = place()
    pairs = [(nodes_in.at[core + i], nodes_ref.at[i]) for i in range(count)]
    pairs += [(source_in, source_w), (target_in, target_w), (node_in, node_w), (bias_in, bias_ref)]
    copies = [pltpu.make_async_copy(*pair, sems.at[i]) for i, pair in enumerate(pairs)]
    for copy in copies:
        copy.start()
    for copy in copies[: count + 1]:
        copy.wait()
    source_rows(
        levels, lambda i: nodes_ref[i], normed_ref, source_ref, east_ref, west_ref, raw_ref, (begin_ref, end_ref), source_w
    )
    for copy in copies[count + 1 :]:
        copy.wait()
    bias_ref[...] = bias_ref[...] * 0.5


def outside(*arrays):
    return [pltpu.with_memory_space_constraint(x, pltpu.HBM) for x in arrays]


def first(levels, nodes, source_w, target_w, node_w, bias):
    lat, rows, width = nodes.shape
    three, two, square = array(3, rows, width), array(2, rows, width), array(width, width)
    edge = array(2, levels, width, dtype=F32)
    return pl.pallas_call(
        functools.partial(first_kernel, levels),
        in_specs=[OUTSIDE] * 5,
        out_specs=[WHOLE] * 11,
        out_shape=[three, square, square, array(*bias.shape, dtype=F32), square, three, three, two, two, edge, edge],
        scratch_shapes=[pltpu.VMEM((3, rows, width), F32), pltpu.SemaphoreType.DMA((7,))],
        compiler_params=params(),
        cost_estimate=cost(),
    )(*outside(nodes, source_w, target_w, node_w, bias))


def second_kernel(
    pieces, levels, nodes_a, target_w, node_w, bias_ref, source_w, normed_a, source_a, east_a, west_a, begin_a, end_a, nodes_b,
    normed_ref, source_ref, east_ref, west_ref, to_west_ref, to_east_ref, far_ref,
    raw_ref, begin_ref, end_ref, target_ref, sum_ref,
):
    _, core = place()
    source_rows(
        levels, lambda i: nodes_b[core + i], normed_ref, source_ref, east_ref, west_ref, raw_ref, (begin_ref, end_ref), source_w
    )
    for k in range(2):
        to_west_ref[k], to_west_ref[2 + k] = begin_a[k].astype(BF16), begin_ref[k].astype(BF16)
        to_east_ref[k], to_east_ref[2 + k] = end_a[k].astype(BF16), end_ref[k].astype(BF16)
    halves = (
        (normed_a, source_a, east_a, west_a, nodes_a, core),
        (normed_ref, source_ref, east_ref, west_ref, nodes_b, 2 * core),
    )
    out = update_pieces(pieces, levels, halves, target_w, node_w, bias_ref, None, target_ref, sum_ref)
    far_ref[0], far_ref[1] = out


def second(levels, pieces, *args):
    rows, width = args[0].shape[1:]
    three, two, edge = array(3, rows, width), array(2, rows, width), array(4, levels, width)
    size = levels * GROUP
    count = len(pieces) * size
    return pl.pallas_call(
        functools.partial(second_kernel, pieces, levels),
        in_specs=[WHOLE] * len(args),
        out_specs=[WHOLE] * 7,
        out_shape=[three, three, two, two, edge, edge, array(2, size, width)],
        scratch_shapes=[pltpu.VMEM((3, rows, width), F32)]
        + [pltpu.VMEM((2, levels, width), F32)] * 2
        + [pltpu.VMEM((count, width), F32), pltpu.VMEM((count, width), BF16)],
        compiler_params=params(),
        cost_estimate=cost(),
    )(*args)


def later_kernel(pieces, levels, has, *refs):
    nodes_a, normed_a, source_a, east_a, west_a, nodes_b, normed_b, source_b, east_b, west_b = refs[:10]
    target_w, node_w, bias_ref = refs[10:13]
    refs = refs[13:]
    _, core = place()
    edges = None
    if has == "edges":
        edges, refs = refs[:2], refs[2:]
    *outs, target_ref, sum_ref = refs
    if has == "mask":
        mask_ref, *outs, kept_ref = outs
        here = lax.axis_index("level")
        for q in range(4):
            for level in range(levels):
                kept = jnp.where(mask_ref[(here ^ q) * levels + level] > 0, 0.0, MASKED).astype(F32)
                kept_ref[q * levels + level : q * levels + level + 1] = jnp.full((1, LANES), kept)
    halves = (
        (normed_a, source_a, east_a, west_a, nodes_a, core),
        (normed_b, source_b, east_b, west_b, nodes_b, 2 * core),
    )
    out = update_pieces(pieces, levels, halves, target_w, node_w, bias_ref, edges, target_ref, sum_ref)
    for i, ref in enumerate(outs):
        ref[0], ref[1] = out[2 * i : 2 * i + 2]


def later(levels, pieces, shared, more=(), has=None):
    width = shared[0].shape[-1]
    size = levels * GROUP
    count = len(pieces) * size
    args = (*shared, *more)
    specs = [WHOLE] * len(args)
    shapes = [array(2, size, width)] * (len(pieces) // 2)
    if has == "mask":
        specs[-1] = SCALARS
        shapes += [array(4 * levels, LANES, dtype=F32)]
    return pl.pallas_call(
        functools.partial(later_kernel, pieces, levels, has),
        in_specs=specs,
        out_specs=[WHOLE] * len(shapes),
        out_shape=shapes,
        scratch_shapes=[pltpu.VMEM((count, width), F32), pltpu.VMEM((count, width), BF16)],
        compiler_params=params(),
        cost_estimate=cost(),
    )(*args)


def attention_kernel(
    kept_ref, own_ref, opposite_ref, query_key, value_w, output_w,
    out_own, out_sibling, *refs,
):
    *out_opposite, q_ref, k_ref, v_ref, att_ref, weight_ref = refs
    _, size, width = own_ref.shape
    levels = 4 * size // GROUP
    tiles = width // LANES
    x = jnp.concatenate([own_ref[0], own_ref[1], opposite_ref[0], opposite_ref[1]], axis=0)
    normed = normalize(x.astype(F32)).astype(BF16)

    def spread(ref, y):
        for t in range(tiles):
            ref[t] = y[:, LANES * t : LANES * (t + 1)]

    spread(q_ref, matmul(normed, query_key[0]) * HEAD**-0.5)
    spread(k_ref, matmul(normed, query_key[1]))
    spread(v_ref, matmul(normed, value_w[...]))
    low = lax.broadcasted_iota(jnp.int32, (levels, LANES), 1) < HEAD
    pad = jnp.zeros((LANES - 2 * levels, LANES), BF16)
    kept = kept_ref[...]
    for column in range(GROUP):
        rows = pl.ds(column, levels, stride=GROUP)
        for t in range(tiles):
            query, key = q_ref[t, rows, :].astype(BF16), k_ref[t, rows, :].astype(BF16)
            zero = jnp.zeros_like(query)
            both = jnp.concatenate([jnp.where(low, query, zero), jnp.where(low, zero, query), pad], axis=0)
            scores = lax.dot_general(key, both, (((1,), (1,)), ((), ())), preferred_element_type=F32)
            scores = scores + kept
            weights = jnp.exp(scores - jnp.max(scores, axis=0, keepdims=True))
            weights = weights * (1.0 / jnp.sum(weights, axis=0, keepdims=True))
            weight_ref[levels * column : levels * (column + 1), LANES * t : LANES * (t + 1)] = weights.astype(BF16)
    for column in range(GROUP):
        rows = pl.ds(column, levels, stride=GROUP)
        for t in range(tiles):
            weights = weight_ref[levels * column : levels * (column + 1), LANES * t : LANES * (t + 1)]
            value = v_ref[t, rows, :].astype(BF16)
            mixed = lax.dot_general(weights, value, (((0,), (0,)), ((), ())), preferred_element_type=F32)
            att_ref[t, rows, :] = jnp.where(low, mixed[:levels], mixed[levels : 2 * levels])
    attended = jnp.concatenate([att_ref[t] for t in range(tiles)], axis=1).astype(BF16)
    out = (x.astype(F32) + matmul(attended, output_w[...])).astype(BF16)
    out_own[...] = out[:size]
    out_sibling[...] = out[size : 2 * size]
    for i in range(2):
        part = out[(2 + i) * size : (3 + i) * size]
        if len(out_opposite) == 2:
            out_opposite[i][...] = part
        else:
            out_opposite[0][i] = part


def attention(apart, *args):
    _, size, width = args[1].shape
    rows = 4 * size
    tiled = pltpu.VMEM((width // LANES, rows, LANES), F32)
    return pl.pallas_call(
        attention_kernel,
        in_specs=[WHOLE] * len(args),
        out_specs=[WHOLE] * (4 if apart else 3),
        out_shape=[array(size, width)] * 4 if apart else [array(size, width)] * 2 + [array(2, size, width)],
        scratch_shapes=[tiled] * 4 + [pltpu.VMEM((rows, width), BF16)],
        compiler_params=params(),
        cost_estimate=cost(),
    )(*args)


def finish_kernel(levels, targets, given, *refs):
    *pieces, out_ref, whole_ref, sems = refs[given:]
    chip, core = place()
    width = out_ref.shape[-1]
    lon = 3 * GROUP
    copies = []
    for n, (far, other) in enumerate(targets):
        for pair in range(levels // 2):
            rows = slice(2 * GROUP * pair, 2 * GROUP * (pair + 1))
            parts = [p[0][rows] if len(p.shape) == 3 else p[rows] for p in pieces[3 * n : 3 * n + 3]]
            whole = whole_of(*(p.astype(F32).reshape(2, GROUP, width) for p in parts))
            whole_ref[n, 2 * lon * pair : 2 * lon * (pair + 1)] = whole.reshape(2 * lon, width).astype(BF16)
        row = 2 * (1 - core if other else core) + (1 - chip if far else chip)
        copies.append(pltpu.make_async_copy(whole_ref.at[n], out_ref.at[row], sems.at[n]))
        copies[-1].start()
    for copy in copies:
        copy.wait()


def finish(levels, targets, shape, given, pieces, flops=1):
    count = len(targets)
    return pl.pallas_call(
        functools.partial(finish_kernel, levels, targets, len(given)),
        in_specs=[OUTSIDE] * len(given) + [WHOLE] * len(pieces),
        out_specs=OUTSIDE,
        out_shape=array(*shape),
        input_output_aliases={0: 0} if given else {},
        scratch_shapes=[pltpu.VMEM((count, *shape[1:]), BF16), pltpu.SemaphoreType.DMA((count,))],
        compiler_params=params(),
        cost_estimate=cost(flops),
    )(*given, *pieces)


def after(x, *others):
    return lax.optimization_barrier((x, *others))[0]


def per_device(
    nodes, level_mask, source_weight, target_weight, direction_bias, node_weight, query_key, value_weight, output_weight
):
    lat, lon, levels, width = nodes.shape
    rows = levels * lon
    opposite = [(i, i ^ 2) for i in range(4)]
    sibling = [(i, i ^ 1) for i in range(4)]
    diagonal = [(i, i ^ 3) for i in range(4)]
    ring = lax.axis_size("sector")
    up = [(i, (i + 1) % ring) for i in range(ring)]
    down = [(j, i) for i, j in up]
    far_piece = lambda c: ((True, c, 0), (True, c, 1))
    own_piece = lambda c: ((False, c, 0), (False, c, 1))

    nodes = jnp.transpose(nodes, (0, 2, 1, 3)).reshape(lat, rows, width)
    nodes_b = lax.ppermute(nodes, "level", sibling)
    far, own = {}, {}
    nodes_a, target_w, node_w, bias, source_w, *rows_a = first(
        levels, nodes, source_weight, target_weight, node_weight, direction_bias
    )
    *rows_b, to_west, to_east, far[0] = second(
        levels, far_piece(0), nodes_a, target_w, node_w, bias, source_w, *rows_a, nodes_b
    )
    shared = (nodes_a, *rows_a[:4], nodes_b, *rows_b, target_w, node_w, bias)
    then = lambda x: (after(nodes_a, x), *shared[1:])
    far[1], kept = later(levels, far_piece(1), shared, (level_mask,), "mask")
    west = lax.ppermute(to_east, "sector", up)
    east = lax.ppermute(to_west, "sector", down)
    (own[0],) = later(levels, own_piece(0), then((far[1], west)))
    arrived = [lax.ppermute(far[c], "level", opposite) for c in range(2)]
    (far[2],) = later(levels, far_piece(2), then((own[0], arrived[0])), (west, east), "edges")
    arrived += [lax.ppermute(far[2], "level", opposite)]
    done, close, back, distant = {}, {}, {}, {}
    for c in range(3):
        if c == 1:
            own[1], own[2] = later(levels, own_piece(1) + own_piece(2), then(done[0]), (west, east), "edges")
        mine = after(own[c], far[2] if c == 0 else done[c - 1])
        args = (kept, mine, arrived[c], query_key, value_weight, output_weight)
        done[c], close[c], *toward = attention(c == 2, *args)
        if c < 2:
            back[c] = lax.ppermute(toward[0], "level", opposite)
        else:
            back[c] = lax.ppermute(after(toward[0], back[0]), "level", opposite)
            distant[c] = lax.ppermute(after(toward[1], back[0]), "level", diagonal)
    shape = (lat, rows, width)
    listed = lambda d: [d[c] for c in range(3)]
    out = finish(levels, ((False, False),), shape, (), listed(done), 10**10)
    late = lambda x: after(x, out, back[0])
    for c in range(2):
        distant[c] = lax.ppermute(late(back[c][1]), "level", sibling)
    close = {0: lax.ppermute(close[0], "level", sibling)} | {
        c: lax.ppermute(late(close[c]), "level", sibling) for c in (1, 2)
    }
    targets = ((True, False), (True, True), (False, True))
    out = finish(levels, targets, shape, (out,), listed(back) + listed(distant) + listed(close))
    return jnp.transpose(out.reshape(lat, levels, lon, width), (0, 2, 1, 3))


def solution(mesh):
    placed = (P(None, "sector", "level", None), P(), P(), P(), P(), P(), P(), P(), P())
    return jax.shard_map(
        per_device,
        mesh=mesh,
        in_specs=placed,
        out_specs=P(None, "sector", "level", None),
        check_vma=False,
    )
```

time: 59.3 us -> 58.6 us (0.988)
  waiting for transfers between devices: 2.8 us -> 5.29 us
  starting transfers between devices: 27.9 us -> 25.6 us
  Pallas kernels: 28.1 us -> 27.2 us
    ppermute x3 -> x2, starting transfers between devices: 4.4 us -> 0.41 us  [per_device(): lax.ppermute(late(close[c]), 'level', sibling)]
    ppermute x9 -> x10, waiting for transfers between devices: 1.58 us -> 5.27 us  [the longest x1 2.66 us: per_device(): back[c] = lax.ppermute(after(toward[0], back[0]), 'level', opposite)]
    pallas_call x5, Pallas kernels: 11.4 us -> 10.4 us  [the longest x4 6.56 us: later(): pl.pallas_call(functools.partial(later_kernel, pieces, levels, has), in_s...]
    ppermute x2, starting transfers between devices: 0.5 us -> 1.38 us  [per_device(): distant[c] = lax.ppermute(late(back[c][1]), 'level', sibling)]
    ppermute x3 -> x2, waiting for transfers between devices: 0.88 us -> 0.01 us  [per_device(): lax.ppermute(late(close[c]), 'level', sibling)]
    ppermute x9 -> x10, starting transfers between devices: 19.7 us -> 20.6 us  [the longest x1 6.68 us: per_device(): east = lax.ppermute(to_west, 'sector', down)]
    pallas_call x1, Pallas kernels: 2.43 us -> 3.18 us  [second(): pl.pallas_call(functools.partial(second_kernel, pieces, levels), in_specs...]
    pallas_call x3 -> x2, Pallas kernels: 2.62 us -> 1.96 us  [finish(): pl.pallas_call(functools.partial(finish_kernel, levels, targets, len(give...]
  transfers between devices with their start and end apart: 15 -> 15, of which waited for: 4 -> 3; matrix products, arithmetic and copies ran while one was open for 0% -> 0% of each run, Pallas kernels for 42% -> 39%
where the time goes in v4:
time: 58.6 us; the launch traced here: 58.5 us
  Pallas kernels  27.2 us (46%)
  starting transfers between devices  25.6 us (44%)
  waiting for transfers between devices  5.29 us (9%)
    pallas_call x3, Pallas kernels, attention(): pl.pallas_call(attention_kernel, in_specs=[WHOLE] * len(args), out_specs=...  11.7 us
    ppermute x1, starting transfers between devices, per_device(): east = lax.ppermute(to_west, 'sector', down)  6.68 us
    pallas_call x4, Pallas kernels, later(): pl.pallas_call(functools.partial(later_kernel, pieces, levels, has), in_s...  6.56 us
    pallas_call x1, Pallas kernels, first(): pl.pallas_call(functools.partial(first_kernel, levels), in_specs=[OUTSIDE...  3.83 us
    ppermute x2, starting transfers between devices, per_device(): back[c] = lax.ppermute(toward[0], 'level', opposite)  3.36 us
    ppermute x1, starting transfers between devices, per_device(): nodes_b = lax.ppermute(nodes, 'level', sibling)  3.24 us
    pallas_call x1, Pallas kernels, second(): pl.pallas_call(functools.partial(second_kernel, pieces, levels), in_specs...  3.18 us
    ppermute x2, starting transfers between devices, per_device(): arrived = [lax.ppermute(far[c], 'level', opposite) for c in range(2)]  2.91 us
  transfers between devices with their start and end apart: 15, of which 3 were waited for; matrix products, arithmetic and copies ran while one was open for 0% of the time, Pallas kernels for 39%

profile of v4, /device:TPU:1, one launch (start us, length us, event | category | flops | bytes accessed | tf_op | source)
XLA Modules:
  0.0 58.5 jit_solution(5891688409283843606)
XLA Ops:
  0.0 3.2 %collective-permute-start = (bf16[4,288,768]{2,1,0:T(8,128)(2,1)}, bf16[4,288,768]{2,1,0:T(8,128)(2,1)S(1)}, u32[]{:S(2)}, u32[]{:S(2)}) collective-permute-start(bf16[4,288,768]{2,1,0:T(8,128)(2,1)} %bitcast.10), channel_id=1, source_target_pairs={{0,1},{1,0},{2,3},{3,2},{4,5},{5,4},{6,7},{7,6},{8,9},{9,8},{10,11... | collective-permute-start | bytes 5308424 | tf_op jit(solution)/shard_map/ppermute | solution.py:409
  3.2 3.8 %shard_map.91 = (bf16[3,288,768]{2,1,0:T(8,128)(2,1)S(1)}, bf16[768,768]{1,0:T(8,128)(2,1)S(1)}, bf16[768,768]{1,0:T(8,128)(2,1)S(1)}, f32[4,768]{1,0:T(4,128)S(...) custom-call(bf16[4,288,768]{2,1,0:T(8,128)(2,1)} %bitcast.11, ...), custom_call_target="tpu_custom_call" | custom-call | flops 1 | bytes 1 | tf_op jit(solution)/shard_map/pallas_call | solution.py:196
  7.1 0.0 copy-start.3
  7.1 3.2 %shard_map.92 = (bf16[3,288,768]{2,1,0:T(8,128)(2,1)S(1)}, bf16[3,288,768]{2,1,0:T(8,128)(2,1)S(1)}, bf16[2,288,768]{2,1,0:T(8,128)(2,1)S(1)}, bf16[2,288,768]{2...) custom-call(bf16[3,288,768]{2,1,0:T(8,128)(2,1)S(1)} %get-tuple-elem, ...), custom_call_target="tpu_custom_call" | custom-call | flops 1 | bytes 1 | tf_op jit(solution)/shard_map/pallas_call | solution.py:232
  10.3 1.2 %collective-permute-start.2 = (bf16[2,96,768]{2,1,0:T(8,128)(2,1)S(1)}, bf16[2,96,768]{2,1,0:T(8,128)(2,1)S(1)}, u32[]{:S(2)}, u32[]{:S(2)}) collective-permute-start(bf16[2,96,768]{2,1,0:T(8,128)(2,1)S(1)} %get-tuple-element.68), channel_id=1, source_target_pairs={{0,2},{1,3},{2,0},{3,1},{4,6},{5,7},{6,4},{7,5},{8,10},{9,11},{10,... | collective-permute-start | bytes 884744 | tf_op jit(solution)/shard_map/ppermute | solution.py:423
  11.5 1.2 %collective-permute-start.1 = (bf16[4,12,768]{2,1,0:T(8,128)(2,1)S(1)}, bf16[4,12,768]{2,1,0:T(8,128)(2,1)S(1)}, u32[]{:S(2)}, u32[]{:S(2)}) collective-permute-start(bf16[4,12,768]{2,1,0:T(8,128)(2,1)S(1)} %get-tuple-element.66), channel_id=1, source_target_pairs={{0,4},{4,8},{8,12},{12,16},{16,20},{20,24},{24,28},{28,32},{32,36}... | collective-permute-start | bytes 221192 | tf_op jit(solution)/shard_map/ppermute | solution.py:420
  12.7 6.7 %collective-permute-start.3 = (bf16[4,12,768]{2,1,0:T(8,128)(2,1)S(1)}, bf16[4,12,768]{2,1,0:T(8,128)(2,1)S(1)}, u32[]{:S(2)}, u32[]{:S(2)}) collective-permute-start(bf16[4,12,768]{2,1,0:T(8,128)(2,1)S(1)} %get-tuple-element.70), channel_id=1, source_target_pairs={{4,0},{8,4},{12,8},{16,12},{20,16},{24,20},{28,24},{32,28},{36,32}... | collective-permute-start | bytes 221192 | tf_op jit(solution)/shard_map/ppermute | solution.py:421
  19.4 1.8 %shard_map.93 = (bf16[2,96,768]{2,1,0:T(8,128)(2,1)S(1)}, f32[48,128]{1,0:T(8,128)S(1)}) custom-call(bf16[3,288,768]{2,1,0:T(8,128)(2,1)S(1)} %get-tuple-element.73.nodes_a.refs_0_, bf16[3,288,768]{2,1,0:T(8,128)(2,1)S(1)} %get-tuple-element.50.normed_a.refs_1_, bf16[3,288,768]{2,1,0:T(8,128)(2,1)S(1)} %get-tuple-element.51.source_a.refs_2_, ...), custom_call_target="tpu_custom_call" | custom-call | flops 1 | bytes 1 | tf_op jit(solution)/shard_map/pallas_call | solution.py:280
  21.2 1.7 %collective-permute-start.4 = (bf16[2,96,768]{2,1,0:T(8,128)(2,1)S(1)}, bf16[2,96,768]{2,1,0:T(8,128)(2,1)S(1)}, u32[]{:S(2)}, u32[]{:S(2)}) collective-permute-start(bf16[2,96,768]{2,1,0:T(8,128)(2,1)S(1)} %get-tuple-element.65), channel_id=1, source_target_pairs={{0,2},{1,3},{2,0},{3,1},{4,6},{5,7},{6,4},{7,5},{8,10},{9,11},{10,... | collective-permute-start | bytes 884744 | tf_op jit(solution)/shard_map/ppermute | solution.py:423
  22.9 1.2 %shard_map.94.own_ref = bf16[2,96,768]{2,1,0:T(8,128)(2,1)S(1)} custom-call(bf16[3,288,768]{2,1,0:T(8,128)(2,1)S(1)} %get-tuple-element.73.nodes_a.refs_0_, bf16[3,288,768]{2,1,0:T(8,128)(2,1)S(1)} %get-tuple-element.50.normed_a.refs_1_, bf16[3,288,768]{2,1,0:T(8,128)(2,1)S(1)} %get-tuple-element.51.source_a.refs_2_, ...), custom_call_target="tpu_custom_call" | custom-call | flops 1 | bytes 1 | tf_op jit(solution)/shard_map/pallas_call | solution.py:280
  24.1 0.0 copy-start.1
  24.1 0.0 copy-start.2
  24.1 0.0 copy-start
  24.1 1.3 %shard_map.95 = bf16[2,96,768]{2,1,0:T(8,128)(2,1)S(1)} custom-call(bf16[3,288,768]{2,1,0:T(8,128)(2,1)S(1)} %get-tuple-element.73.nodes_a.refs_0_, bf16[3,288,768]{2,1,0:T(8,128)(2,1)S(1)} %get-tuple-element.50.normed_a.refs_1_, bf16[3,288,768]{2,1,0:T(8,128)(2,1)S(1)} %get-tuple-element.51.source_a.refs_2_, ...), custom_call_target="tpu_custom_call" | custom-call | flops 1 | bytes 1 | tf_op jit(solution)/shard_map/pallas_call | solution.py:280
  25.4 1.6 %collective-permute-start.5 = (bf16[2,96,768]{2,1,0:T(8,128)(2,1)S(1)}, bf16[2,96,768]{2,1,0:T(8,128)(2,1)S(1)}, u32[]{:S(2)}, u32[]{:S(2)}) collective-permute-start(bf16[2,96,768]{2,1,0:T(8,128)(2,1)S(1)} %shard_map.95), channel_id=1, source_target_pairs={{0,2},{1,3},{2,0},{3,1},{4,6},{5,7},{6,4},{7,5},{8,10},{9,11},{10,... | collective-permute-start | bytes 884744 | tf_op jit(solution)/shard_map/ppermute | solution.py:425
  27.1 3.9 %shard_map.96 = (bf16[96,768]{1,0:T(8,128)(2,1)S(1)}, bf16[96,768]{1,0:T(8,128)(2,1)S(1)}, bf16[2,96,768]{2,1,0:T(8,128)(2,1)S(1)}) custom-call(f32[48,128]{1,0:T(8,128)S(1)} %get-tuple-element.64.kept_ref, bf16[2,96,768]{2,1,0:T(8,128)(2,1)S(1)} %shard_map.94.own_ref, bf16[2,96,768]{2,1,0:T(8,128)(2,1)S(1)} %collective-permute-done.2.opposite_ref, ...), custom_call_target="tpu_custom_call" | custom-call | flops 1 | bytes 1 | tf_op jit(solution)/shard_map/pallas_call | solution.py:346
  31.0 1.7 %collective-permute-start.6 = (bf16[2,96,768]{2,1,0:T(8,128)(2,1)S(1)}, bf16[2,96,768]{2,1,0:T(8,128)(2,1)S(1)}, u32[]{:S(2)}, u32[]{:S(2)}) collective-permute-start(bf16[2,96,768]{2,1,0:T(8,128)(2,1)S(1)} %get-tuple-element.80), channel_id=1, source_target_pairs={{0,2},{1,3},{2,0},{3,1},{4,6},{5,7},{6,4},{7,5},{8,10},{9,11},{10,... | collective-permute-start | bytes 884744 | tf_op jit(solution)/shard_map/ppermute | solution.py:434
  32.7 2.3 %shard_map.97 = (bf16[2,96,768]{2,1,0:T(8,128)(2,1)S(1)}, bf16[2,96,768]{2,1,0:T(8,128)(2,1)S(1)}) custom-call(bf16[3,288,768]{2,1,0:T(8,128)(2,1)S(1)} %get-tuple-element.73.nodes_a.refs_0_, bf16[3,288,768]{2,1,0:T(8,128)(2,1)S(1)} %get-tuple-element.50.normed_a.refs_1_, bf16[3,288,768]{2,1,0:T(8,128)(2,1)S(1)} %get-tuple-element.51.source_a.refs_2_, ...), custom_call_target="tpu_custom_call" | custom-call | flops 1 | bytes 1 | tf_op jit(solution)/shard_map/pallas_call | solution.py:280
  35.0 1.5 %collective-permute-start.12 = (bf16[96,768]{1,0:T(8,128)(2,1)S(1)}, bf16[96,768]{1,0:T(8,128)(2,1)S(1)}, u32[]{:S(2)}, u32[]{:S(2)}) collective-permute-start(bf16[96,768]{1,0:T(8,128)(2,1)S(1)} %get-tuple-element.88), channel_id=1, source_target_pairs={{0,1},{1,0},{2,3},{3,2},{4,5},{5,4},{6,7},{7,6},{8,9},{9,8},{10,11... | collective-permute-start | bytes 442376 | tf_op jit(solution)/shard_map/ppermute | solution.py:444
  36.5 3.9 %shard_map.98 = (bf16[96,768]{1,0:T(8,128)(2,1)S(1)}, bf16[96,768]{1,0:T(8,128)(2,1)S(1)}, bf16[2,96,768]{2,1,0:T(8,128)(2,1)S(1)}) custom-call(f32[48,128]{1,0:T(8,128)S(1)} %get-tuple-element.64.kept_ref, bf16[2,96,768]{2,1,0:T(8,128)(2,1)S(1)} %get-tuple-element.75.own_ref, bf16[2,96,768]{2,1,0:T(8,128)(2,1)S(1)} %collective-permute-done.4.opposite_ref, ...), custom_call_target="tpu_custom_call" | custom-call | flops 1 | bytes 1 | tf_op jit(solution)/shard_map/pallas_call | solution.py:346
  40.4 1.7 %collective-permute-start.7 = (bf16[2,96,768]{2,1,0:T(8,128)(2,1)S(1)}, bf16[2,96,768]{2,1,0:T(8,128)(2,1)S(1)}, u32[]{:S(2)}, u32[]{:S(2)}) collective-permute-start(bf16[2,96,768]{2,1,0:T(8,128)(2,1)S(1)} %get-tuple-element.81), channel_id=1, source_target_pairs={{0,2},{1,3},{2,0},{3,1},{4,6},{5,7},{6,4},{7,5},{8,10},{9,11},{10,... | collective-permute-start | bytes 884744 | tf_op jit(solution)/shard_map/ppermute | solution.py:434
  42.1 3.9 %shard_map.99 = (bf16[96,768]{1,0:T(8,128)(2,1)S(1)}, bf16[96,768]{1,0:T(8,128)(2,1)S(1)}, bf16[96,768]{1,0:T(8,128)(2,1)S(1)}, bf16[96,768]{1,0:T(8,128)(2,1)S(1)}) custom-call(f32[48,128]{1,0:T(8,128)S(1)} %get-tuple-element.64.kept_ref, bf16[2,96,768]{2,1,0:T(8,128)(2,1)S(1)} %get-tuple-element.78.own_ref, ...), custom_call_target="tpu_custom_call" | custom-call | flops 1 | bytes 1 | tf_op jit(solution)/shard_map/pallas_call | solution.py:346
  46.0 1.9 %collective-permute-start.11 = (bf16[96,768]{1,0:T(8,128)(2,1)S(1)}, bf16[96,768]{1,0:T(8,128)(2,1)S(1)}, u32[]{:S(2)}, u32[]{:S(2)}) collective-permute-start(bf16[96,768]{1,0:T(8,128)(2,1)S(1)} %get-tuple-element.87), channel_id=1, source_target_pairs={{0,3},{1,2},{2,1},{3,0},{4,7},{5,6},{6,5},{7,4},{8,11},{9,10},{10,... | collective-permute-start | bytes 442376 | tf_op jit(solution)/shard_map/ppermute | solution.py:437
  47.8 1.4 %collective-permute-start.8 = (bf16[96,768]{1,0:T(8,128)(2,1)S(1)}, bf16[96,768]{1,0:T(8,128)(2,1)S(1)}, u32[]{:S(2)}, u32[]{:S(2)}) collective-permute-start(bf16[96,768]{1,0:T(8,128)(2,1)S(1)} %get-tuple-element.83), channel_id=1, source_target_pairs={{0,2},{1,3},{2,0},{3,1},{4,6},{5,7},{6,4},{7,5},{8,10},{9,11},{10,... | collective-permute-start | bytes 442376 | tf_op jit(solution)/shard_map/ppermute | solution.py:436
  49.2 0.8 %shard_map.100.refs_0_ = bf16[4,288,768]{2,1,0:T(8,128)(2,1)} custom-call(bf16[96,768]{1,0:T(8,128)(2,1)S(1)} %get-tuple-element.72.refs_0_, bf16[96,768]{1,0:T(8,128)(2,1)S(1)} %get-tuple-element.76.refs_1_, bf16[96,768]{1,0:T(8,128)(2,1)S(1)} %get-tuple-element.79.refs_2_), custom_call_target="tpu_custom_call" | custom-call | flops 10000000000 | bytes 1 | tf_op jit(solution)/shard_map/pallas_call | solution.py:378
  50.1 0.8 %collective-permute-done.7.refs_2_ = bf16[2,96,768]{2,1,0:T(8,128)(2,1)S(1)} collective-permute-done((bf16[2,96,768]{2,1,0:T(8,128)(2,1)S(1)}, bf16[2,96,768]{2,1,0:T(8,128)(2,1)S(1)}, u32[]{:S(2)}, u32[]{:S(2)}) %collective-permute-start.7) | collective-permute-done | bytes 294944 | tf_op jit(solution)/shard_map/ppermute | solution.py:434
  50.9 1.3 %collective-permute-start.9 = (bf16[96,768]{1,0:T(8,128)(2,1)S(1)}, bf16[96,768]{1,0:T(8,128)(2,1)S(1)}, u32[]{:S(2)}, u32[]{:S(2)}) collective-permute-start(bf16[96,768]{1,0:T(8,128)(2,1)S(1)} %slice_bitcast_fusion.1), channel_id=1, source_target_pairs={{0,1},{1,0},{2,3},{3,2},{4,5},{5,4},{6,7},{7,6},{8,9},{9,8},{10,11... | collective-permute-start | bytes 442376 | tf_op jit(solution)/shard_map/ppermute | solution.py:443
  52.1 0.1 collective-permute-start.10
  52.2 0.4 collective-permute-start.13
  52.6 1.8 %collective-permute-done.11.refs_6_ = bf16[96,768]{1,0:T(8,128)(2,1)S(1)} collective-permute-done((bf16[96,768]{1,0:T(8,128)(2,1)S(1)}, bf16[96,768]{1,0:T(8,128)(2,1)S(1)}, u32[]{:S(2)}, u32[]{:S(2)}) %collective-permute-start.11) | collective-permute-done | bytes 147488 | tf_op jit(solution)/shard_map/ppermute | solution.py:437
  54.5 2.7 %collective-permute-done.8.refs_3_ = bf16[96,768]{1,0:T(8,128)(2,1)S(1)} collective-permute-done((bf16[96,768]{1,0:T(8,128)(2,1)S(1)}, bf16[96,768]{1,0:T(8,128)(2,1)S(1)}, u32[]{:S(2)}, u32[]{:S(2)}) %collective-permute-start.8) | collective-permute-done | bytes 147488 | tf_op jit(solution)/shard_map/ppermute | solution.py:436
  57.2 1.1 %shard_map.101 = bf16[4,288,768]{2,1,0:T(8,128)(2,1)} custom-call(bf16[4,288,768]{2,1,0:T(8,128)(2,1)} %shard_map.100.refs_0_, bf16[2,96,768]{2,1,0:T(8,128)(2,1)S(1)} %collective-permute-done.6.refs_1_, bf16[2,96,768]{2,1,0:T(8,128)(2,1)S(1)} %collective-permute-done.7.refs_2_, ...), custom_call_target="tpu_custom_call", output_to_operand_aliasing={{}: (0, {})} | custom-call | flops 1 | bytes 1 | tf_op jit(solution)/shard_map/pallas_call | solution.py:378
  (19 shorter events, 0.1 us)
Async XLA Ops:
  0.0 7.1 %collective-permute-start = (bf16[4,288,768]{2,1,0:T(8,128)(2,1)}, bf16[4,288,768]{2,1,0:T(8,128)(2,1)S(1)}, u32[]{:S(2)}, u32[]{:S(2)}) collective-permute-start(bf16[4,288,768]{2,1,0:T(8,128)(2,1)} %bitcast.10), channel_id=1, source_target_pairs={{0,1},{1,0},{2,3},{3,2},{4,5},{5,4},{6,7},{7,6},{8,9},{9,8},{10,11... | collective-permute-start | bytes 5308424 | tf_op jit(solution)/shard_map/ppermute | solution.py:409
  7.1 12.3 %copy-start.3 = (s32[48]{0:T(128)S(1)}, s32[48]{0:T(128)}, u32[]{:S(2)}) copy-start(s32[48]{0:T(128)} %refs_13_.1) | copy-start | bytes 580
  10.3 13.8 %collective-permute-start.2 = (bf16[2,96,768]{2,1,0:T(8,128)(2,1)S(1)}, bf16[2,96,768]{2,1,0:T(8,128)(2,1)S(1)}, u32[]{:S(2)}, u32[]{:S(2)}) collective-permute-start(bf16[2,96,768]{2,1,0:T(8,128)(2,1)S(1)} %get-tuple-element.68), channel_id=1, source_target_pairs={{0,2},{1,3},{2,0},{3,1},{4,6},{5,7},{6,4},{7,5},{8,10},{9,11},{10,... | collective-permute-start | bytes 884744 | tf_op jit(solution)/shard_map/ppermute | solution.py:423
  11.5 11.4 %collective-permute-start.1 = (bf16[4,12,768]{2,1,0:T(8,128)(2,1)S(1)}, bf16[4,12,768]{2,1,0:T(8,128)(2,1)S(1)}, u32[]{:S(2)}, u32[]{:S(2)}) collective-permute-start(bf16[4,12,768]{2,1,0:T(8,128)(2,1)S(1)} %get-tuple-element.66), channel_id=1, source_target_pairs={{0,4},{4,8},{8,12},{12,16},{16,20},{20,24},{24,28},{28,32},{32,36}... | collective-permute-start | bytes 221192 | tf_op jit(solution)/shard_map/ppermute | solution.py:420
  12.7 11.4 %collective-permute-start.3 = (bf16[4,12,768]{2,1,0:T(8,128)(2,1)S(1)}, bf16[4,12,768]{2,1,0:T(8,128)(2,1)S(1)}, u32[]{:S(2)}, u32[]{:S(2)}) collective-permute-start(bf16[4,12,768]{2,1,0:T(8,128)(2,1)S(1)} %get-tuple-element.70), channel_id=1, source_target_pairs={{4,0},{8,4},{12,8},{16,12},{20,16},{24,20},{28,24},{32,28},{36,32}... | collective-permute-start | bytes 221192 | tf_op jit(solution)/shard_map/ppermute | solution.py:421
  21.2 15.3 %collective-permute-start.4 = (bf16[2,96,768]{2,1,0:T(8,128)(2,1)S(1)}, bf16[2,96,768]{2,1,0:T(8,128)(2,1)S(1)}, u32[]{:S(2)}, u32[]{:S(2)}) collective-permute-start(bf16[2,96,768]{2,1,0:T(8,128)(2,1)S(1)} %get-tuple-element.65), channel_id=1, source_target_pairs={{0,2},{1,3},{2,0},{3,1},{4,6},{5,7},{6,4},{7,5},{8,10},{9,11},{10,... | collective-permute-start | bytes 884744 | tf_op jit(solution)/shard_map/ppermute | solution.py:423
  24.1 3.0 %copy-start.1 = (bf16[768,768]{1,0:T(8,128)(2,1)S(1)}, bf16[768,768]{1,0:T(8,128)(2,1)}, u32[]{:S(2)}) copy-start(bf16[768,768]{1,0:T(8,128)(2,1)} %value_w.5) | copy-start | bytes 3538948
  24.1 3.0 %copy-start.2 = (bf16[768,768]{1,0:T(8,128)(2,1)S(1)}, bf16[768,768]{1,0:T(8,128)(2,1)}, u32[]{:S(2)}) copy-start(bf16[768,768]{1,0:T(8,128)(2,1)} %output_w.5) | copy-start | bytes 3538948
  24.1 2.9 %copy-start = (bf16[2,768,768]{2,1,0:T(8,128)(2,1)S(1)}, bf16[2,768,768]{2,1,0:T(8,128)(2,1)}, u32[]{:S(2)}) copy-start(bf16[2,768,768]{2,1,0:T(8,128)(2,1)} %query_key.5) | copy-start | bytes 7077892
  25.4 16.6 %collective-permute-start.5 = (bf16[2,96,768]{2,1,0:T(8,128)(2,1)S(1)}, bf16[2,96,768]{2,1,0:T(8,128)(2,1)S(1)}, u32[]{:S(2)}, u32[]{:S(2)}) collective-permute-start(bf16[2,96,768]{2,1,0:T(8,128)(2,1)S(1)} %shard_map.95), channel_id=1, source_target_pairs={{0,2},{1,3},{2,0},{3,1},{4,6},{5,7},{6,4},{7,5},{8,10},{9,11},{10,... | collective-permute-start | bytes 884744 | tf_op jit(solution)/shard_map/ppermute | solution.py:425
  31.0 15.0 %collective-permute-start.6 = (bf16[2,96,768]{2,1,0:T(8,128)(2,1)S(1)}, bf16[2,96,768]{2,1,0:T(8,128)(2,1)S(1)}, u32[]{:S(2)}, u32[]{:S(2)}) collective-permute-start(bf16[2,96,768]{2,1,0:T(8,128)(2,1)S(1)} %get-tuple-element.80), channel_id=1, source_target_pairs={{0,2},{1,3},{2,0},{3,1},{4,6},{5,7},{6,4},{7,5},{8,10},{9,11},{10,... | collective-permute-start | bytes 884744 | tf_op jit(solution)/shard_map/ppermute | solution.py:434
  35.0 17.3 %collective-permute-start.12 = (bf16[96,768]{1,0:T(8,128)(2,1)S(1)}, bf16[96,768]{1,0:T(8,128)(2,1)S(1)}, u32[]{:S(2)}, u32[]{:S(2)}) collective-permute-start(bf16[96,768]{1,0:T(8,128)(2,1)S(1)} %get-tuple-element.88), channel_id=1, source_target_pairs={{0,1},{1,0},{2,3},{3,2},{4,5},{5,4},{6,7},{7,6},{8,9},{9,8},{10,11... | collective-permute-start | bytes 442376 | tf_op jit(solution)/shard_map/ppermute | solution.py:444
  40.4 10.4 %collective-permute-start.7 = (bf16[2,96,768]{2,1,0:T(8,128)(2,1)S(1)}, bf16[2,96,768]{2,1,0:T(8,128)(2,1)S(1)}, u32[]{:S(2)}, u32[]{:S(2)}) collective-permute-start(bf16[2,96,768]{2,1,0:T(8,128)(2,1)S(1)} %get-tuple-element.81), channel_id=1, source_target_pairs={{0,2},{1,3},{2,0},{3,1},{4,6},{5,7},{6,4},{7,5},{8,10},{9,11},{10,... | collective-permute-start | bytes 884744 | tf_op jit(solution)/shard_map/ppermute | solution.py:434
  46.0 8.5 %collective-permute-start.11 = (bf16[96,768]{1,0:T(8,128)(2,1)S(1)}, bf16[96,768]{1,0:T(8,128)(2,1)S(1)}, u32[]{:S(2)}, u32[]{:S(2)}) collective-permute-start(bf16[96,768]{1,0:T(8,128)(2,1)S(1)} %get-tuple-element.87), channel_id=1, source_target_pairs={{0,3},{1,2},{2,1},{3,0},{4,7},{5,6},{6,5},{7,4},{8,11},{9,10},{10,... | collective-permute-start | bytes 442376 | tf_op jit(solution)/shard_map/ppermute | solution.py:437
  47.8 9.3 %collective-permute-start.8 = (bf16[96,768]{1,0:T(8,128)(2,1)S(1)}, bf16[96,768]{1,0:T(8,128)(2,1)S(1)}, u32[]{:S(2)}, u32[]{:S(2)}) collective-permute-start(bf16[96,768]{1,0:T(8,128)(2,1)S(1)} %get-tuple-element.83), channel_id=1, source_target_pairs={{0,2},{1,3},{2,0},{3,1},{4,6},{5,7},{6,4},{7,5},{8,10},{9,11},{10,... | collective-permute-start | bytes 442376 | tf_op jit(solution)/shard_map/ppermute | solution.py:436
  50.9 6.3 %collective-permute-start.9 = (bf16[96,768]{1,0:T(8,128)(2,1)S(1)}, bf16[96,768]{1,0:T(8,128)(2,1)S(1)}, u32[]{:S(2)}, u32[]{:S(2)}) collective-permute-start(bf16[96,768]{1,0:T(8,128)(2,1)S(1)} %slice_bitcast_fusion.1), channel_id=1, source_target_pairs={{0,1},{1,0},{2,3},{3,2},{4,5},{5,4},{6,7},{7,6},{8,9},{9,8},{10,11... | collective-permute-start | bytes 442376 | tf_op jit(solution)/shard_map/ppermute | solution.py:443
  52.1 5.0 %collective-permute-start.10 = (bf16[96,768]{1,0:T(8,128)(2,1)S(1)}, bf16[96,768]{1,0:T(8,128)(2,1)S(1)}, u32[]{:S(2)}, u32[]{:S(2)}) collective-permute-start(bf16[96,768]{1,0:T(8,128)(2,1)S(1)} %slice_bitcast_fusion), channel_id=1, source_target_pairs={{0,1},{1,0},{2,3},{3,2},{4,5},{5,4},{6,7},{7,6},{8,9},{9,8},{10,11... | collective-permute-start | bytes 442376 | tf_op jit(solution)/shard_map/ppermute | solution.py:443
  52.2 4.9 %collective-permute-start.13 = (bf16[96,768]{1,0:T(8,128)(2,1)S(1)}, bf16[96,768]{1,0:T(8,128)(2,1)S(1)}, u32[]{:S(2)}, u32[]{:S(2)}) collective-permute-start(bf16[96,768]{1,0:T(8,128)(2,1)S(1)} %get-tuple-element.90), channel_id=1, source_target_pairs={{0,1},{1,0},{2,3},{3,2},{4,5},{5,4},{6,7},{7,6},{8,9},{9,8},{10,11... | collective-permute-start | bytes 442376 | tf_op jit(solution)/shard_map/ppermute | solution.py:445
  54.5 2.7 %collective-permute-start.14 = (bf16[96,768]{1,0:T(8,128)(2,1)S(1)}, bf16[96,768]{1,0:T(8,128)(2,1)S(1)}, u32[]{:S(2)}, u32[]{:S(2)}) collective-permute-start(bf16[96,768]{1,0:T(8,128)(2,1)S(1)} %get-tuple-element.92), channel_id=1, source_target_pairs={{0,1},{1,0},{2,3},{3,2},{4,5},{5,4},{6,7},{7,6},{8,9},{9,8},{10,11... | collective-permute-start | bytes 442376 | tf_op jit(solution)/shard_map/ppermute | solution.py:445

commit v5 on v4

--- a/solution.py
+++ b/solution.py
@@ -416,10 +416,10 @@
     )
     shared = (nodes_a, *rows_a[:4], nodes_b, *rows_b, target_w, node_w, bias)
     then = lambda x: (after(nodes_a, x), *shared[1:])
-    far[1], kept = later(levels, far_piece(1), shared, (level_mask,), "mask")
+    (far[1],) = later(levels, far_piece(1), shared)
     west = lax.ppermute(to_east, "sector", up)
     east = lax.ppermute(to_west, "sector", down)
-    (own[0],) = later(levels, own_piece(0), then((far[1], west)))
+    own[0], kept = later(levels, own_piece(0), then((far[1], west)), (level_mask,), "mask")
     arrived = [lax.ppermute(far[c], "level", opposite) for c in range(2)]
     (far[2],) = later(levels, far_piece(2), then((own[0], arrived[0])), (west, east), "edges")
     arrived += [lax.ppermute(far[2], "level", opposite)]
@@ -444,8 +444,8 @@
     close = {0: lax.ppermute(close[0], "level", sibling)} | {
         c: lax.ppermute(late(close[c]), "level", sibling) for c in (1, 2)
     }
-    targets = ((True, False), (True, True), (False, True))
-    out = finish(levels, targets, shape, (out,), listed(back) + listed(distant) + listed(close))
+    out = finish(levels, ((False, True),), shape, (out,), listed(close))
+    out = finish(levels, ((True, False), (True, True)), shape, (out,), listed(back) + listed(distant))
     return jnp.transpose(out.reshape(lat, levels, lon, width), (0, 2, 1, 3))
 
 

time: 58.6 us -> 58.2 us (level)
  waiting for transfers between devices: 5.29 us -> 3.64 us
  starting transfers between devices: 25.6 us -> 26.3 us
  Pallas kernels: 27.2 us -> 27.8 us
    ppermute x1, waiting for transfers between devices: 1.83 us -> 0.07 us  [per_device(): distant[c] = lax.ppermute(after(toward[1], back[0]), 'level', diagonal)]
    ppermute x2, starting transfers between devices: 0.41 us -> 1.48 us  [per_device(): lax.ppermute(late(close[c]), 'level', sibling)]
    ppermute x2, waiting for transfers between devices: 0.77 us -> 0.01 us  [per_device(): back[c] = lax.ppermute(toward[0], 'level', opposite)]
    pallas_call x2 -> x3, Pallas kernels: 1.96 us -> 2.62 us  [finish(): pl.pallas_call(functools.partial(finish_kernel, levels, targets, len(give...]
  transfers between devices with their start and end apart: 15 -> 15, of which waited for: 3 -> 4; matrix products, arithmetic and copies ran while one was open for 0% -> 0% of each run, Pallas kernels for 39% -> 41%
where the time goes in v5:
time: 58.2 us; the launch traced here: 58.1 us
  Pallas kernels  27.8 us (48%)
  starting transfers between devices  26.3 us (45%)
  waiting for transfers between devices  3.64 us (6%)
    pallas_call x3, Pallas kernels, attention(): pl.pallas_call(attention_kernel, in_specs=[WHOLE] * len(args), out_specs=...  11.6 us
    ppermute x1, starting transfers between devices, per_device(): east = lax.ppermute(to_west, 'sector', down)  6.68 us
    pallas_call x4, Pallas kernels, later(): pl.pallas_call(functools.partial(later_kernel, pieces, levels, has), in_s...  6.56 us
    pallas_call x1, Pallas kernels, first(): pl.pallas_call(functools.partial(first_kernel, levels), in_specs=[OUTSIDE...  3.83 us
    ppermute x1, starting transfers between devices, per_device(): nodes_b = lax.ppermute(nodes, 'level', sibling)  3.24 us
    pallas_call x1, Pallas kernels, second(): pl.pallas_call(functools.partial(second_kernel, pieces, levels), in_specs...  3.18 us
    ppermute x2, starting transfers between devices, per_device(): back[c] = lax.ppermute(toward[0], 'level', opposite)  3.04 us
    ppermute x1, waiting for transfers between devices, per_device(): back[c] = lax.ppermute(after(toward[0], back[0]), 'level', opposite)  3.02 us
  transfers between devices with their start and end apart: 15, of which 4 were waited for; matrix products, arithmetic and copies ran while one was open for 0% of the time, Pallas kernels for 41%

profile of v5, /device:TPU:1, one launch (start us, length us, event | category | flops | bytes accessed | tf_op | source)
XLA Modules:
  0.0 58.1 jit_solution(17346548990471974833)
XLA Ops:
  0.0 3.2 %collective-permute-start = (bf16[4,288,768]{2,1,0:T(8,128)(2,1)}, bf16[4,288,768]{2,1,0:T(8,128)(2,1)S(1)}, u32[]{:S(2)}, u32[]{:S(2)}) collective-permute-start(bf16[4,288,768]{2,1,0:T(8,128)(2,1)} %bitcast.10), channel_id=1, source_target_pairs={{0,1},{1,0},{2,3},{3,2},{4,5},{5,4},{6,7},{7,6},{8,9},{9,8},{10,11... | collective-permute-start | bytes 5308424 | tf_op jit(solution)/shard_map/ppermute | solution.py:409
  3.2 3.8 %shard_map.91 = (bf16[3,288,768]{2,1,0:T(8,128)(2,1)S(1)}, bf16[768,768]{1,0:T(8,128)(2,1)S(1)}, bf16[768,768]{1,0:T(8,128)(2,1)S(1)}, f32[4,768]{1,0:T(4,128)S(...) custom-call(bf16[4,288,768]{2,1,0:T(8,128)(2,1)} %bitcast.11, ...), custom_call_target="tpu_custom_call" | custom-call | flops 1 | bytes 1 | tf_op jit(solution)/shard_map/pallas_call | solution.py:196
  7.1 3.2 %shard_map.92 = (bf16[3,288,768]{2,1,0:T(8,128)(2,1)S(1)}, bf16[3,288,768]{2,1,0:T(8,128)(2,1)S(1)}, bf16[2,288,768]{2,1,0:T(8,128)(2,1)S(1)}, bf16[2,288,768]{2...) custom-call(bf16[3,288,768]{2,1,0:T(8,128)(2,1)S(1)} %get-tuple-elem, ...), custom_call_target="tpu_custom_call" | custom-call | flops 1 | bytes 1 | tf_op jit(solution)/shard_map/pallas_call | solution.py:232
  10.3 1.2 %collective-permute-start.2 = (bf16[2,96,768]{2,1,0:T(8,128)(2,1)S(1)}, bf16[2,96,768]{2,1,0:T(8,128)(2,1)S(1)}, u32[]{:S(2)}, u32[]{:S(2)}) collective-permute-start(bf16[2,96,768]{2,1,0:T(8,128)(2,1)S(1)} %get-tuple-element.68), channel_id=1, source_target_pairs={{0,2},{1,3},{2,0},{3,1},{4,6},{5,7},{6,4},{7,5},{8,10},{9,11},{10,... | collective-permute-start | bytes 884744 | tf_op jit(solution)/shard_map/ppermute | solution.py:423
  11.5 1.2 %collective-permute-start.1 = (bf16[4,12,768]{2,1,0:T(8,128)(2,1)S(1)}, bf16[4,12,768]{2,1,0:T(8,128)(2,1)S(1)}, u32[]{:S(2)}, u32[]{:S(2)}) collective-permute-start(bf16[4,12,768]{2,1,0:T(8,128)(2,1)S(1)} %get-tuple-element.64), channel_id=1, source_target_pairs={{0,4},{4,8},{8,12},{12,16},{16,20},{20,24},{24,28},{28,32},{32,36}... | collective-permute-start | bytes 221192 | tf_op jit(solution)/shard_map/ppermute | solution.py:420
  12.7 6.7 %collective-permute-start.3 = (bf16[4,12,768]{2,1,0:T(8,128)(2,1)S(1)}, bf16[4,12,768]{2,1,0:T(8,128)(2,1)S(1)}, u32[]{:S(2)}, u32[]{:S(2)}) collective-permute-start(bf16[4,12,768]{2,1,0:T(8,128)(2,1)S(1)} %get-tuple-element.70), channel_id=1, source_target_pairs={{4,0},{8,4},{12,8},{16,12},{20,16},{24,20},{28,24},{32,28},{36,32}... | collective-permute-start | bytes 221192 | tf_op jit(solution)/shard_map/ppermute | solution.py:421
  19.4 1.2 %shard_map.93 = bf16[2,96,768]{2,1,0:T(8,128)(2,1)S(1)} custom-call(bf16[3,288,768]{2,1,0:T(8,128)(2,1)S(1)} %get-tuple-element.73.nodes_a.refs_0_, bf16[3,288,768]{2,1,0:T(8,128)(2,1)S(1)} %get-tuple-element.50.normed_a.refs_1_, bf16[3,288,768]{2,1,0:T(8,128)(2,1)S(1)} %get-tuple-element.51.source_a.refs_2_, ...), custom_call_target="tpu_custom_call" | custom-call | flops 1 | bytes 1 | tf_op jit(solution)/shard_map/pallas_call | solution.py:280
  20.6 1.7 %collective-permute-start.4 = (bf16[2,96,768]{2,1,0:T(8,128)(2,1)S(1)}, bf16[2,96,768]{2,1,0:T(8,128)(2,1)S(1)}, u32[]{:S(2)}, u32[]{:S(2)}) collective-permute-start(bf16[2,96,768]{2,1,0:T(8,128)(2,1)S(1)} %shard_map.93), channel_id=1, source_target_pairs={{0,2},{1,3},{2,0},{3,1},{4,6},{5,7},{6,4},{7,5},{8,10},{9,11},{10,... | collective-permute-start | bytes 884744 | tf_op jit(solution)/shard_map/ppermute | solution.py:423
  22.3 0.0 collective-permute-done.1.refs_13_
  22.3 1.8 %shard_map.94 = (bf16[2,96,768]{2,1,0:T(8,128)(2,1)S(1)}, f32[48,128]{1,0:T(8,128)S(1)}) custom-call(bf16[3,288,768]{2,1,0:T(8,128)(2,1)S(1)} %get-tuple-element.73.nodes_a.refs_0_, bf16[3,288,768]{2,1,0:T(8,128)(2,1)S(1)} %get-tuple-element.50.normed_a.refs_1_, bf16[3,288,768]{2,1,0:T(8,128)(2,1)S(1)} %get-tuple-element.51.source_a.refs_2_, ...), custom_call_target="tpu_custom_call" | custom-call | flops 1 | bytes 1 | tf_op jit(solution)/shard_map/pallas_call | solution.py:280
  24.2 1.3 %shard_map.95 = bf16[2,96,768]{2,1,0:T(8,128)(2,1)S(1)} custom-call(bf16[3,288,768]{2,1,0:T(8,128)(2,1)S(1)} %get-tuple-element.73.nodes_a.refs_0_, bf16[3,288,768]{2,1,0:T(8,128)(2,1)S(1)} %get-tuple-element.50.normed_a.refs_1_, bf16[3,288,768]{2,1,0:T(8,128)(2,1)S(1)} %get-tuple-element.51.source_a.refs_2_, ...), custom_call_target="tpu_custom_call" | custom-call | flops 1 | bytes 1 | tf_op jit(solution)/shard_map/pallas_call | solution.py:280
  25.5 1.9 %collective-permute-start.5 = (bf16[2,96,768]{2,1,0:T(8,128)(2,1)S(1)}, bf16[2,96,768]{2,1,0:T(8,128)(2,1)S(1)}, u32[]{:S(2)}, u32[]{:S(2)}) collective-permute-start(bf16[2,96,768]{2,1,0:T(8,128)(2,1)S(1)} %shard_map.95), channel_id=1, source_target_pairs={{0,2},{1,3},{2,0},{3,1},{4,6},{5,7},{6,4},{7,5},{8,10},{9,11},{10,... | collective-permute-start | bytes 884744 | tf_op jit(solution)/shard_map/ppermute | solution.py:425
  27.3 3.9 %shard_map.96 = (bf16[96,768]{1,0:T(8,128)(2,1)S(1)}, bf16[96,768]{1,0:T(8,128)(2,1)S(1)}, bf16[2,96,768]{2,1,0:T(8,128)(2,1)S(1)}) custom-call(f32[48,128]{1,0:T(8,128)S(1)} %get-tuple-element.66.kept_ref, bf16[2,96,768]{2,1,0:T(8,128)(2,1)S(1)} %get-tuple-element.71.own_ref, bf16[2,96,768]{2,1,0:T(8,128)(2,1)S(1)} %collective-permute-done.2.opposite_ref, ...), custom_call_target="tpu_custom_call" | custom-call | flops 1 | bytes 1 | tf_op jit(solution)/shard_map/pallas_call | solution.py:346
  31.2 1.5 %collective-permute-start.7 = (bf16[2,96,768]{2,1,0:T(8,128)(2,1)S(1)}, bf16[2,96,768]{2,1,0:T(8,128)(2,1)S(1)}, u32[]{:S(2)}, u32[]{:S(2)}) collective-permute-start(bf16[2,96,768]{2,1,0:T(8,128)(2,1)S(1)} %get-tuple-element.82), channel_id=1, source_target_pairs={{0,2},{1,3},{2,0},{3,1},{4,6},{5,7},{6,4},{7,5},{8,10},{9,11},{10,... | collective-permute-start | bytes 884744 | tf_op jit(solution)/shard_map/ppermute | solution.py:434
  32.7 2.3 %shard_map.97 = (bf16[2,96,768]{2,1,0:T(8,128)(2,1)S(1)}, bf16[2,96,768]{2,1,0:T(8,128)(2,1)S(1)}) custom-call(bf16[3,288,768]{2,1,0:T(8,128)(2,1)S(1)} %get-tuple-element.73.nodes_a.refs_0_, bf16[3,288,768]{2,1,0:T(8,128)(2,1)S(1)} %get-tuple-element.50.normed_a.refs_1_, bf16[3,288,768]{2,1,0:T(8,128)(2,1)S(1)} %get-tuple-element.51.source_a.refs_2_, ...), custom_call_target="tpu_custom_call" | custom-call | flops 1 | bytes 1 | tf_op jit(solution)/shard_map/pallas_call | solution.py:280
  35.0 3.9 %shard_map.98 = (bf16[96,768]{1,0:T(8,128)(2,1)S(1)}, bf16[96,768]{1,0:T(8,128)(2,1)S(1)}, bf16[2,96,768]{2,1,0:T(8,128)(2,1)S(1)}) custom-call(f32[48,128]{1,0:T(8,128)S(1)} %get-tuple-element.66.kept_ref, bf16[2,96,768]{2,1,0:T(8,128)(2,1)S(1)} %get-tuple-element.75.own_ref, bf16[2,96,768]{2,1,0:T(8,128)(2,1)S(1)} %collective-permute-done.4.opposite_ref, ...), custom_call_target="tpu_custom_call" | custom-call | flops 1 | bytes 1 | tf_op jit(solution)/shard_map/pallas_call | solution.py:346
  38.9 1.5 %collective-permute-start.6 = (bf16[96,768]{1,0:T(8,128)(2,1)S(1)}, bf16[96,768]{1,0:T(8,128)(2,1)S(1)}, u32[]{:S(2)}, u32[]{:S(2)}) collective-permute-start(bf16[96,768]{1,0:T(8,128)(2,1)S(1)} %get-tuple-element.80), channel_id=1, source_target_pairs={{0,1},{1,0},{2,3},{3,2},{4,5},{5,4},{6,7},{7,6},{8,9},{9,8},{10,11... | collective-permute-start | bytes 442376 | tf_op jit(solution)/shard_map/ppermute | solution.py:444
  40.3 1.6 %collective-permute-start.10 = (bf16[2,96,768]{2,1,0:T(8,128)(2,1)S(1)}, bf16[2,96,768]{2,1,0:T(8,128)(2,1)S(1)}, u32[]{:S(2)}, u32[]{:S(2)}) collective-permute-start(bf16[2,96,768]{2,1,0:T(8,128)(2,1)S(1)} %get-tuple-element.86), channel_id=1, source_target_pairs={{0,2},{1,3},{2,0},{3,1},{4,6},{5,7},{6,4},{7,5},{8,10},{9,11},{10,... | collective-permute-start | bytes 884744 | tf_op jit(solution)/shard_map/ppermute | solution.py:434
  41.9 3.9 %shard_map.99 = (bf16[96,768]{1,0:T(8,128)(2,1)S(1)}, bf16[96,768]{1,0:T(8,128)(2,1)S(1)}, bf16[96,768]{1,0:T(8,128)(2,1)S(1)}, bf16[96,768]{1,0:T(8,128)(2,1)S(1)}) custom-call(f32[48,128]{1,0:T(8,128)S(1)} %get-tuple-element.66.kept_ref, bf16[2,96,768]{2,1,0:T(8,128)(2,1)S(1)} %get-tuple-element.78.own_ref, ...), custom_call_target="tpu_custom_call" | custom-call | flops 1 | bytes 1 | tf_op jit(solution)/shard_map/pallas_call | solution.py:346
  45.8 2.0 %collective-permute-start.14 = (bf16[96,768]{1,0:T(8,128)(2,1)S(1)}, bf16[96,768]{1,0:T(8,128)(2,1)S(1)}, u32[]{:S(2)}, u32[]{:S(2)}) collective-permute-start(bf16[96,768]{1,0:T(8,128)(2,1)S(1)} %get-tuple-element.92), channel_id=1, source_target_pairs={{0,3},{1,2},{2,1},{3,0},{4,7},{5,6},{6,5},{7,4},{8,11},{9,10},{10,... | collective-permute-start | bytes 442376 | tf_op jit(solution)/shard_map/ppermute | solution.py:437
  47.8 1.6 %collective-permute-start.11 = (bf16[96,768]{1,0:T(8,128)(2,1)S(1)}, bf16[96,768]{1,0:T(8,128)(2,1)S(1)}, u32[]{:S(2)}, u32[]{:S(2)}) collective-permute-start(bf16[96,768]{1,0:T(8,128)(2,1)S(1)} %get-tuple-element.88), channel_id=1, source_target_pairs={{0,2},{1,3},{2,0},{3,1},{4,6},{5,7},{6,4},{7,5},{8,10},{9,11},{10,... | collective-permute-start | bytes 442376 | tf_op jit(solution)/shard_map/ppermute | solution.py:436
  49.3 0.8 %shard_map.100.refs_0_ = bf16[4,288,768]{2,1,0:T(8,128)(2,1)} custom-call(bf16[96,768]{1,0:T(8,128)(2,1)S(1)} %get-tuple-element.72.refs_0_, bf16[96,768]{1,0:T(8,128)(2,1)S(1)} %get-tuple-element.76.refs_1_, bf16[96,768]{1,0:T(8,128)(2,1)S(1)} %get-tuple-element.79.refs_2_), custom_call_target="tpu_custom_call" | custom-call | flops 10000000000 | bytes 1 | tf_op jit(solution)/shard_map/pallas_call | solution.py:378
  50.2 1.4 %collective-permute-start.8 = (bf16[96,768]{1,0:T(8,128)(2,1)S(1)}, bf16[96,768]{1,0:T(8,128)(2,1)S(1)}, u32[]{:S(2)}, u32[]{:S(2)}) collective-permute-start(bf16[96,768]{1,0:T(8,128)(2,1)S(1)} %get-tuple-element.83), channel_id=1, source_target_pairs={{0,1},{1,0},{2,3},{3,2},{4,5},{5,4},{6,7},{7,6},{8,9},{9,8},{10,11... | collective-permute-start | bytes 442376 | tf_op jit(solution)/shard_map/ppermute | solution.py:445
  51.6 0.1 collective-permute-start.9
  51.7 0.5 collective-permute-start.12
  52.2 0.4 collective-permute-done.8.refs_2_
  52.6 0.4 collective-permute-start.13
  53.0 0.1 collective-permute-done.9.refs_3_
  53.1 0.8 %shard_map.101.refs_0_ = bf16[4,288,768]{2,1,0:T(8,128)(2,1)} custom-call(bf16[4,288,768]{2,1,0:T(8,128)(2,1)} %shard_map.100.refs_0_, bf16[96,768]{1,0:T(8,128)(2,1)S(1)} %collective-permute-done.6.refs_1_, bf16[96,768]{1,0:T(8,128)(2,1)S(1)} %collective-permute-done.8.refs_2_, ...), custom_call_target="tpu_custom_call", output_to_operand_aliasing={{}: (0, {})} | custom-call | flops 1 | bytes 1 | tf_op jit(solution)/shard_map/pallas_call | solution.py:378
  53.9 0.1 collective-permute-done.14.refs_6_
  54.0 3.0 %collective-permute-done.11.refs_3_ = bf16[96,768]{1,0:T(8,128)(2,1)S(1)} collective-permute-done((bf16[96,768]{1,0:T(8,128)(2,1)S(1)}, bf16[96,768]{1,0:T(8,128)(2,1)S(1)}, u32[]{:S(2)}, u32[]{:S(2)}) %collective-permute-start.11) | collective-permute-done | bytes 147488 | tf_op jit(solution)/shard_map/ppermute | solution.py:436
  57.0 1.0 %shard_map.102 = bf16[4,288,768]{2,1,0:T(8,128)(2,1)} custom-call(bf16[4,288,768]{2,1,0:T(8,128)(2,1)} %shard_map.101.refs_0_, bf16[2,96,768]{2,1,0:T(8,128)(2,1)S(1)} %collective-permute-done.7.refs_1_, bf16[2,96,768]{2,1,0:T(8,128)(2,1)S(1)} %collective-permute-done.10.refs_2_, ...), custom_call_target="tpu_custom_call", output_to_operand_aliasing={{}: (0, {})} | custom-call | flops 1 | bytes 1 | tf_op jit(solution)/shard_map/pallas_call | solution.py:378
  (20 shorter events, 0.1 us)
Async XLA Ops:
  0.0 7.1 %collective-permute-start = (bf16[4,288,768]{2,1,0:T(8,128)(2,1)}, bf16[4,288,768]{2,1,0:T(8,128)(2,1)S(1)}, u32[]{:S(2)}, u32[]{:S(2)}) collective-permute-start(bf16[4,288,768]{2,1,0:T(8,128)(2,1)} %bitcast.10), channel_id=1, source_target_pairs={{0,1},{1,0},{2,3},{3,2},{4,5},{5,4},{6,7},{7,6},{8,9},{9,8},{10,11... | collective-permute-start | bytes 5308424 | tf_op jit(solution)/shard_map/ppermute | solution.py:409
  10.3 13.8 %collective-permute-start.2 = (bf16[2,96,768]{2,1,0:T(8,128)(2,1)S(1)}, bf16[2,96,768]{2,1,0:T(8,128)(2,1)S(1)}, u32[]{:S(2)}, u32[]{:S(2)}) collective-permute-start(bf16[2,96,768]{2,1,0:T(8,128)(2,1)S(1)} %get-tuple-element.68), channel_id=1, source_target_pairs={{0,2},{1,3},{2,0},{3,1},{4,6},{5,7},{6,4},{7,5},{8,10},{9,11},{10,... | collective-permute-start | bytes 884744 | tf_op jit(solution)/shard_map/ppermute | solution.py:423
  11.5 10.8 %collective-permute-start.1 = (bf16[4,12,768]{2,1,0:T(8,128)(2,1)S(1)}, bf16[4,12,768]{2,1,0:T(8,128)(2,1)S(1)}, u32[]{:S(2)}, u32[]{:S(2)}) collective-permute-start(bf16[4,12,768]{2,1,0:T(8,128)(2,1)S(1)} %get-tuple-element.64), channel_id=1, source_target_pairs={{0,4},{4,8},{8,12},{12,16},{16,20},{20,24},{24,28},{28,32},{32,36}... | collective-permute-start | bytes 221192 | tf_op jit(solution)/shard_map/ppermute | solution.py:420
  12.7 11.4 %collective-permute-start.3 = (bf16[4,12,768]{2,1,0:T(8,128)(2,1)S(1)}, bf16[4,12,768]{2,1,0:T(8,128)(2,1)S(1)}, u32[]{:S(2)}, u32[]{:S(2)}) collective-permute-start(bf16[4,12,768]{2,1,0:T(8,128)(2,1)S(1)} %get-tuple-element.70), channel_id=1, source_target_pairs={{4,0},{8,4},{12,8},{16,12},{20,16},{24,20},{28,24},{32,28},{36,32}... | collective-permute-start | bytes 221192 | tf_op jit(solution)/shard_map/ppermute | solution.py:421
  19.4 2.9 %copy-start.3 = (s32[48]{0:T(128)S(1)}, s32[48]{0:T(128)}, u32[]{:S(2)}) copy-start(s32[48]{0:T(128)} %refs_13_.1) | copy-start | bytes 580
  20.6 14.4 %collective-permute-start.4 = (bf16[2,96,768]{2,1,0:T(8,128)(2,1)S(1)}, bf16[2,96,768]{2,1,0:T(8,128)(2,1)S(1)}, u32[]{:S(2)}, u32[]{:S(2)}) collective-permute-start(bf16[2,96,768]{2,1,0:T(8,128)(2,1)S(1)} %shard_map.93), channel_id=1, source_target_pairs={{0,2},{1,3},{2,0},{3,1},{4,6},{5,7},{6,4},{7,5},{8,10},{9,11},{10,... | collective-permute-start | bytes 884744 | tf_op jit(solution)/shard_map/ppermute | solution.py:423
  24.1 3.2 %copy-start.1 = (bf16[768,768]{1,0:T(8,128)(2,1)S(1)}, bf16[768,768]{1,0:T(8,128)(2,1)}, u32[]{:S(2)}) copy-start(bf16[768,768]{1,0:T(8,128)(2,1)} %value_w.5) | copy-start | bytes 3538948
  24.1 3.2 %copy-start.2 = (bf16[768,768]{1,0:T(8,128)(2,1)S(1)}, bf16[768,768]{1,0:T(8,128)(2,1)}, u32[]{:S(2)}) copy-start(bf16[768,768]{1,0:T(8,128)(2,1)} %output_w.5) | copy-start | bytes 3538948
  24.2 3.2 %copy-start = (bf16[2,768,768]{2,1,0:T(8,128)(2,1)S(1)}, bf16[2,768,768]{2,1,0:T(8,128)(2,1)}, u32[]{:S(2)}) copy-start(bf16[2,768,768]{2,1,0:T(8,128)(2,1)} %query_key.5) | copy-start | bytes 7077892
  25.5 16.5 %collective-permute-start.5 = (bf16[2,96,768]{2,1,0:T(8,128)(2,1)S(1)}, bf16[2,96,768]{2,1,0:T(8,128)(2,1)S(1)}, u32[]{:S(2)}, u32[]{:S(2)}) collective-permute-start(bf16[2,96,768]{2,1,0:T(8,128)(2,1)S(1)} %shard_map.95), channel_id=1, source_target_pairs={{0,2},{1,3},{2,0},{3,1},{4,6},{5,7},{6,4},{7,5},{8,10},{9,11},{10,... | collective-permute-start | bytes 884744 | tf_op jit(solution)/shard_map/ppermute | solution.py:425
  31.2 14.6 %collective-permute-start.7 = (bf16[2,96,768]{2,1,0:T(8,128)(2,1)S(1)}, bf16[2,96,768]{2,1,0:T(8,128)(2,1)S(1)}, u32[]{:S(2)}, u32[]{:S(2)}) collective-permute-start(bf16[2,96,768]{2,1,0:T(8,128)(2,1)S(1)} %get-tuple-element.82), channel_id=1, source_target_pairs={{0,2},{1,3},{2,0},{3,1},{4,6},{5,7},{6,4},{7,5},{8,10},{9,11},{10,... | collective-permute-start | bytes 884744 | tf_op jit(solution)/shard_map/ppermute | solution.py:434
  38.9 12.8 %collective-permute-start.6 = (bf16[96,768]{1,0:T(8,128)(2,1)S(1)}, bf16[96,768]{1,0:T(8,128)(2,1)S(1)}, u32[]{:S(2)}, u32[]{:S(2)}) collective-permute-start(bf16[96,768]{1,0:T(8,128)(2,1)S(1)} %get-tuple-element.80), channel_id=1, source_target_pairs={{0,1},{1,0},{2,3},{3,2},{4,5},{5,4},{6,7},{7,6},{8,9},{9,8},{10,11... | collective-permute-start | bytes 442376 | tf_op jit(solution)/shard_map/ppermute | solution.py:444
  40.3 9.8 %collective-permute-start.10 = (bf16[2,96,768]{2,1,0:T(8,128)(2,1)S(1)}, bf16[2,96,768]{2,1,0:T(8,128)(2,1)S(1)}, u32[]{:S(2)}, u32[]{:S(2)}) collective-permute-start(bf16[2,96,768]{2,1,0:T(8,128)(2,1)S(1)} %get-tuple-element.86), channel_id=1, source_target_pairs={{0,2},{1,3},{2,0},{3,1},{4,6},{5,7},{6,4},{7,5},{8,10},{9,11},{10,... | collective-permute-start | bytes 884744 | tf_op jit(solution)/shard_map/ppermute | solution.py:434
  45.8 8.2 %collective-permute-start.14 = (bf16[96,768]{1,0:T(8,128)(2,1)S(1)}, bf16[96,768]{1,0:T(8,128)(2,1)S(1)}, u32[]{:S(2)}, u32[]{:S(2)}) collective-permute-start(bf16[96,768]{1,0:T(8,128)(2,1)S(1)} %get-tuple-element.92), channel_id=1, source_target_pairs={{0,3},{1,2},{2,1},{3,0},{4,7},{5,6},{6,5},{7,4},{8,11},{9,10},{10,... | collective-permute-start | bytes 442376 | tf_op jit(solution)/shard_map/ppermute | solution.py:437
  47.8 9.2 %collective-permute-start.11 = (bf16[96,768]{1,0:T(8,128)(2,1)S(1)}, bf16[96,768]{1,0:T(8,128)(2,1)S(1)}, u32[]{:S(2)}, u32[]{:S(2)}) collective-permute-start(bf16[96,768]{1,0:T(8,128)(2,1)S(1)} %get-tuple-element.88), channel_id=1, source_target_pairs={{0,2},{1,3},{2,0},{3,1},{4,6},{5,7},{6,4},{7,5},{8,10},{9,11},{10,... | collective-permute-start | bytes 442376 | tf_op jit(solution)/shard_map/ppermute | solution.py:436
  50.2 2.4 %collective-permute-start.8 = (bf16[96,768]{1,0:T(8,128)(2,1)S(1)}, bf16[96,768]{1,0:T(8,128)(2,1)S(1)}, u32[]{:S(2)}, u32[]{:S(2)}) collective-permute-start(bf16[96,768]{1,0:T(8,128)(2,1)S(1)} %get-tuple-element.83), channel_id=1, source_target_pairs={{0,1},{1,0},{2,3},{3,2},{4,5},{5,4},{6,7},{7,6},{8,9},{9,8},{10,11... | collective-permute-start | bytes 442376 | tf_op jit(solution)/shard_map/ppermute | solution.py:445
  51.6 1.5 %collective-permute-start.9 = (bf16[96,768]{1,0:T(8,128)(2,1)S(1)}, bf16[96,768]{1,0:T(8,128)(2,1)S(1)}, u32[]{:S(2)}, u32[]{:S(2)}) collective-permute-start(bf16[96,768]{1,0:T(8,128)(2,1)S(1)} %get-tuple-element.85), channel_id=1, source_target_pairs={{0,1},{1,0},{2,3},{3,2},{4,5},{5,4},{6,7},{7,6},{8,9},{9,8},{10,11... | collective-permute-start | bytes 442376 | tf_op jit(solution)/shard_map/ppermute | solution.py:445
  51.7 5.3 %collective-permute-start.12 = (bf16[96,768]{1,0:T(8,128)(2,1)S(1)}, bf16[96,768]{1,0:T(8,128)(2,1)S(1)}, u32[]{:S(2)}, u32[]{:S(2)}) collective-permute-start(bf16[96,768]{1,0:T(8,128)(2,1)S(1)} %slice_bitcast_fusion.1), channel_id=1, source_target_pairs={{0,1},{1,0},{2,3},{3,2},{4,5},{5,4},{6,7},{7,6},{8,9},{9,8},{10,11... | collective-permute-start | bytes 442376 | tf_op jit(solution)/shard_map/ppermute | solution.py:443
  52.6 4.4 %collective-permute-start.13 = (bf16[96,768]{1,0:T(8,128)(2,1)S(1)}, bf16[96,768]{1,0:T(8,128)(2,1)S(1)}, u32[]{:S(2)}, u32[]{:S(2)}) collective-permute-start(bf16[96,768]{1,0:T(8,128)(2,1)S(1)} %slice_bitcast_fusion), channel_id=1, source_target_pairs={{0,1},{1,0},{2,3},{3,2},{4,5},{5,4},{6,7},{7,6},{8,9},{9,8},{10,11... | collective-permute-start | bytes 442376 | tf_op jit(solution)/shard_map/ppermute | solution.py:443
